TPU v7x, 128 devices: a whole 4x4x4 slice. The times are simulated.
128 devices in a mesh: seg: 4 (over z), blk: 32 (over x, y, core).
Axes of the slice: x: 4, y: 4, z: 4, core: 2. Of those that a mesh axis runs over, the one named last changes fastest.
Arguments:
- records: float32 [12, 32768, 512], P('seg', 'blk'), may hold values from -600 to 600, as said below
- pairs: int32 [256, 8], P(('blk', 'seg')), may hold values from 0 to 1, as said below
Outputs:
- forward: float32 [256, 8, 65, 128], P(('blk', 'seg'))
- backward: float32 [256, 8, 65, 128], P(('blk', 'seg'))
Inputs may be any that keep to these rules, and one draw needn't show every extreme that they name: records are finite. pairs is 0 where g + d >= 256; among the 16 entries of rows 2 * o to 2 * o + 1 at most 8 are 1, and exactly 8 for some o.
All inputs are finite; a program needn't handle non-finite values.
Results may differ from a plain program's by a relative error of at most 0.0041.
Values may be sent and summed in bfloat16 or wider, within the bound.
No kernel may reach another device: no remote copies, remote signals or barrier semaphores. Data moves between devices by JAX's collectives and lax.ppermute only.
A program may use at most 192 MiB of HBM per device.

v0:
```python
import jax
import jax.numpy as jnp
from jax import lax
from jax.sharding import PartitionSpec as P

MAXLAG = 32
SMOOTH = 32
BAND = 64


def from_behind(block, axis, distance):
    devices = range(lax.axis_size(axis))
    route = [(i - distance, i) for i in devices if i - distance in devices]
    return lax.ppermute(block, axis, route)


def smooth_table(length, half):
    rows = jnp.arange(length)[:, None]
    cols = jnp.arange(length)[None, :]
    inside = (jnp.abs(rows - cols) <= half).astype(jnp.float32)
    counted = jnp.sum(inside, axis=0, keepdims=True)
    return inside / counted


def fourier_table(length, bins):
    times = jnp.arange(length)[:, None]
    freqs = jnp.arange(bins)[None, :]
    phase = (times * freqs % length).astype(jnp.float32) * (2.0 * jnp.pi / length)
    return jnp.concatenate([jnp.cos(phase), -jnp.sin(phase)], axis=1)


def lag_table(length, bins, most_lag):
    freqs = jnp.arange(bins)[:, None]
    shifts = jnp.arange(-most_lag, most_lag + 1)[None, :]
    phase = (freqs * shifts % length).astype(jnp.float32) * (2.0 * jnp.pi / length)
    return jnp.concatenate([jnp.cos(phase), -jnp.sin(phase)], axis=0)


def whiten(samples):
    length = samples.shape[-1]
    bins = length // 2
    flat = samples.reshape(-1, length)
    level = jnp.dot(jnp.abs(flat), smooth_table(length, SMOOTH), precision=lax.Precision.HIGHEST)
    normed = flat / (level + 1e-06)
    spectrum = jnp.dot(normed, fourier_table(length, bins), precision=lax.Precision.HIGHEST)
    square = spectrum * spectrum
    bands = bins // BAND
    power = square[:, :bins].reshape(-1, bands, BAND).sum(-1) + square[:, bins:].reshape(
        -1, bands, BAND
    ).sum(-1)
    factor = 1.0 / jnp.sqrt(power / (2 * BAND) + 1e-05)
    factor = jnp.concatenate([factor, factor], axis=1)
    white = spectrum.reshape(-1, 2 * bands, BAND) * factor[:, :, None]
    return white.reshape(samples.shape).astype(jnp.bfloat16)


def correlate(own, other):
    bins = own.shape[-1] // 2
    segs = own.shape[0]
    form = "sjcf,sjdcf->jdcf"
    own_re = own[..., :bins]
    own_im = own[..., bins:]
    far_re = other[..., :bins]
    far_im = other[..., bins:]
    real = jnp.einsum(form, own_re, far_re, preferred_element_type=jnp.float32) + jnp.einsum(
        form, own_im, far_im, preferred_element_type=jnp.float32
    )
    imag = jnp.einsum(form, own_re, far_im, preferred_element_type=jnp.float32) - jnp.einsum(
        form, own_im, far_re, preferred_element_type=jnp.float32
    )
    joined = jnp.concatenate([real, imag], axis=-1)
    scale = 1.0 / jnp.sqrt(jnp.float32(segs * bins))
    return (
        jnp.einsum(
            "jdcf,fl->jdlc",
            joined,
            lag_table(2 * bins, bins, MAXLAG),
            precision=lax.Precision.HIGHEST,
        )
        * scale
    )


def shards(records, pairs):
    place = lax.axis_index("seg")
    recordings = lax.all_to_all(records, "seg", split_axis=1, concat_axis=0, tiled=True)
    white = whiten(recordings)
    segs, rows, length = white.shape
    blocks, reach = pairs.shape
    chans = rows // blocks
    white = white.reshape(segs, blocks, chans, length)
    group = lax.all_gather(white, "seg", axis=1, tiled=True)
    ahead = from_behind(group, "blk", -1)
    window = jnp.concatenate([group, ahead], axis=1)
    first = place * blocks
    live = pairs.astype(jnp.float32)
    partners = jnp.stack(
        [
            lax.dynamic_slice_in_dim(window, first + offset, blocks, 1)
            for offset in range(1, reach + 1)
        ],
        axis=2,
    )
    forward = correlate(white, partners) * live[:, :, None, None]
    behind = from_behind(forward, "blk", 1)
    earlier, current = (
        lax.all_gather(behind, "seg", axis=0, tiled=True),
        lax.all_gather(forward, "seg", axis=0, tiled=True),
    )
    trail = jnp.concatenate([earlier, current], axis=0)
    span = current.shape[0]
    backward = jnp.stack(
        [
            lax.dynamic_slice_in_dim(trail, span + first - offset, blocks, 0)[:, offset - 1, ::-1]
            for offset in range(1, reach + 1)
        ],
        axis=1,
    )
    return (forward, backward)


def solution(mesh):
    return jax.shard_map(
        shards,
        mesh=mesh,
        in_specs=(P("seg", "blk", None), P(("blk", "seg"), None)),
        out_specs=(P(("blk", "seg"), None, None, None), P(("blk", "seg"), None, None, None)),
        check_vma=False,
    )
```

profile of v0, /device:TPU:6, one launch (start us, length us, event | category | flops | bytes accessed | tf_op | source)
XLA Modules:
  0.0 598.8 jit_solution(8635002225935700792)
XLA Ops:
  7.2 10.3 %copy.28 = f32[3,1024,512]{2,0,1:T(4,128)} copy(f32[3,1024,512]{2,1,0:T(8,128)} %param.2) | data formatting | bytes 12582912 | tf_op args[0]
  17.5 5.6 all-to-all-start
  23.1 0.0 all-gather.4.cloned.1.call-start
  23.2 0.1 convert_reduce_fusion
  23.3 2.1 sine_negate_fusion
  25.3 92.7 %all-to-all-done = f32[3,1024,512]{2,0,1:T(4,128)} async-done(((f32[3,1024,512]{2,0,1:T(4,128)}), f32[3,1024,512]{2,0,1:T(4,128)}, u32[]{:S(2)}, u32[]{:S(2)}) %all-to-all-start) | async-done | bytes 6291488 | tf_op jit(solution)/shard_map/all_to_all | solution.py:86
  118.0 5.4 copy.29
  123.4 3.4 copy.30
  126.8 6.5 %copy.31 = f32[3072,512]{0,1:T(8,128)} copy(f32[3072,512]{1,0:T(8,128)} %bitcast.68) | data formatting | bytes 12582912 | tf_op jit(solution)/shard_map/reshape | solution.py:42
  133.3 0.0 copy-start.1
  133.3 22.3 %fusion.6 = f32[512,3072]{1,0:T(8,128)S(1)} fusion(f32[3072,512]{1,0:T(8,128)} %bitcast.69, f32[512]{0:T(512)S(1)} %convert_reduce_fusion), kind=kOutput, calls=%fused_computation.14 | convolution fusion | flops 9666560000 | bytes 12584960 | tf_op jit(solution)/shard_map/dot_general | solution.py:43
  155.6 0.0 copy-done.1
  155.7 12.9 %fusion.48 = (f32[3072,512]{0,1:T(8,128)S(1)}, f32[3072,512]{0,1:T(8,128)}) fusion(f32[512,256]{1,0:T(8,128)S(1)} %get-tuple-element.36, f32[512,256]{1,0:T(8,128)S(1)} %get-tuple-element.37, f32[3072,512]{0,1:T(8,128)S(1)} %copy-done.1, f32[512,3072]{1,0:T(8,128)S(1)} %fusion.6), kind=kOutput, calls=%fused_computation.94 | convolution fusion | flops 9668657152 | bytes 26214400 | tf_op jit(solution)/shard_map/dot_general | solution.py:45
  168.6 0.6 bitcast_reduce_fusion
  169.3 3.3 mul.100
  172.6 9.2 %mul.101 = f32[12,2,128,512]{2,1,0,3:T(2,128)} reshape(f32[3072,8,64]{0,2,1:T(8,128)} %mul.100) | data formatting | bytes 12582912 | tf_op jit(solution)/shard_map/mul | solution.py:53
  181.8 9.5 %reshape.31 = f32[12,2,128,512]{2,1,0,3:T(2,128)} reshape(f32[3072,512]{0,1:T(8,128)} %get-tuple-element.35) | data formatting | bytes 12582912 | tf_op jit(solution)/shard_map/reshape | solution.py:53
  191.3 7.8 %multiply_convert_fusion = bf16[12,2,128,512]{2,1,0,3:T(2,128)(2,1)S(1)} fusion(f32[12,2,128,512]{2,1,0,3:T(2,128)} %reshape.31, f32[12,2,128,512]{2,1,0,3:T(2,128)} %mul.101), kind=kLoop, calls=%fused_computation.12 | loop fusion | flops 3145728 | bytes 15728640 | tf_op jit(solution)/shard_map/convert_element_type | solution.py:54
  199.2 0.0 copy-start.4
  199.2 6.7 %copy.32 = bf16[12,2,128,512]{3,2,0,1:T(8,128)(2,1)} copy(bf16[12,2,128,512]{2,1,0,3:T(2,128)(2,1)S(1)} %multiply_convert_fusion) | data formatting | bytes 6291456 | tf_op jit(solution)/shard_map/convert_element_type | solution.py:54
  205.9 0.0 all-gather.4.cloned.1.call-update
  205.9 0.0 all-gather.6.cloned.1.call-start
  206.0 117.9 %all-gather.4.cloned.1.call-done = bf16[12,8,128,512]{3,2,0,1:T(8,128)(2,1)} async-done(((bf16[12,2,128,512]{3,2,0,1:T(8,128)(2,1)}), bf16[12,8,128,512]{3,2,0,1:T(8,128)(2,1)}) %all-gather.4.cloned.1.call-update) | async-done | bytes 12582928 | tf_op jit(solution)/shard_map/all_gather | solution.py:92
  323.9 4.4 collective-permute-start
  328.3 0.0 copy-done.4
  328.3 0.4 fusion.43
  328.7 4.8 fusion.15
  333.5 4.3 copy.69
  337.8 5.9 copy.70
  343.8 6.4 %constant_dynamic-update-slice_fusion.1 = bf16[12,16,128,512]{3,2,0,1:T(8,128)(2,1)S(1)} fusion(bf16[12,8,128,512]{3,2,0,1:T(8,128)(2,1)} %all-gather.4.cloned.1.call-done), kind=kLoop, calls=%fused_computation.77 | loop fusion | bytes 25165824
  350.1 114.4 %collective-permute-done = bf16[12,8,128,512]{3,2,0,1:T(8,128)(2,1)} collective-permute-done((bf16[12,8,128,512]{3,2,0,1:T(8,128)(2,1)}, bf16[12,8,128,512]{3,2,0,1:T(8,128)(2,1)}, u32[]{:S(2)}, u32[]{:S(2)}) %collective-permute-start) | collective-permute-done | bytes 12582944 | tf_op jit(solution)/shard_map/ppermute | solution.py:14
  464.5 6.7 %constant_dynamic-update-slice_fusion = bf16[12,16,128,512]{3,2,0,1:T(8,128)(2,1)S(1)} fusion(bf16[12,16,128,512]{3,2,0,1:T(8,128)(2,1)S(1)} %constant_dynamic-update-slice_fusion.1, bf16[12,8,128,512]{3,2,0,1:T(8,128)(2,1)} %collective-permute-done), kind=kLoop, calls=%fused_computation.76 | loop fusion | bytes 25165824 | tf_op jit(solution)/shard_map/concatenate | solution.py:94
  471.2 2.0 bitcast_dynamic-update-slice_fusion.7
  473.1 2.0 bitcast_dynamic-update-slice_fusion.6
  475.1 2.0 bitcast_dynamic-update-slice_fusion.5
  477.1 1.9 bitcast_dynamic-update-slice_fusion.4
  479.0 1.9 bitcast_dynamic-update-slice_fusion.3
  481.0 1.9 bitcast_dynamic-update-slice_fusion.2
  482.9 0.0 copy-start
  482.9 2.0 bitcast_dynamic-update-slice_fusion.1
  484.9 2.0 bitcast_dynamic-update-slice_fusion
  486.8 0.0 copy-done
  486.8 14.4 %fusion = (f32[2,128,256,8]{2,1,0,3:T(8,128)S(1)}, f32[2,128,256,8]{2,1,0,3:T(8,128)S(1)}, f32[2,128,256,8]{2,1,0,3:T(8,128)S(1)}, f32[2,128,256,8]{2,1,0,3:T(8,128)S(1)}) fusion(f32[2,128,256,12]{2,1,3,0:T(8,128)S(1)} %copy.69, bf16[12,2,8,128,512]{4,3,0,1,2:T(8,128)(2,1)} %bitcast_dynamic-update-slice_fusion, f32[2,128,256,12]{2,1,3,0:T(8,128)S(1)} %copy-done), kind=kLoop, calls=%fused_computation.4 | loop fusion | flops 60817408 | bytes 39845888
  501.3 0.3 fusion.14
  501.5 0.3 fusion.13
  501.9 4.1 fusion.20
  506.0 0.1 copy.35
  506.1 0.0 copy-start.2
  506.2 1.9 collective-permute-start.1
  508.1 10.9 %collective-permute-done.1 = f32[2,8,65,128]{3,1,2,0:T(8,128)S(1)} collective-permute-done((f32[2,8,65,128]{3,1,2,0:T(8,128)S(1)}, f32[2,8,65,128]{3,1,2,0:T(8,128)S(1)}, u32[]{:S(2)}, u32[]{:S(2)}) %collective-permute-start.1) | collective-permute-done | bytes 532512 | tf_op jit(solution)/shard_map/ppermute | solution.py:14
  519.0 0.0 copy-start.3
  519.0 0.8 copy-done.3
  519.8 0.0 all-gather.6.cloned.1.call-update
  519.8 0.0 all-gather.8.cloned.1.call-start
  519.9 0.0 copy-done.2
  519.9 0.7 all-gather.8.cloned.1.call-update
  520.6 29.0 %all-gather.6.cloned.1.call-done = f32[8,8,65,128]{3,1,2,0:T(8,128)} async-done(((f32[2,8,65,128]{3,1,2,0:T(8,128)}), f32[8,8,65,128]{3,1,2,0:T(8,128)}) %all-gather.6.cloned.1.call-update) | async-done | bytes 2129936 | tf_op jit(solution)/shard_map/all_gather | solution.py:107
  549.6 3.1 constant_dynamic-update-slice_fusion.3
  552.7 30.4 %all-gather.8.cloned.1.call-done = f32[8,8,65,128]{3,1,2,0:T(8,128)} async-done(((f32[2,8,65,128]{3,1,2,0:T(8,128)}), f32[8,8,65,128]{3,1,2,0:T(8,128)}) %all-gather.8.cloned.1.call-update) | async-done | bytes 2129936 | tf_op jit(solution)/shard_map/all_gather | solution.py:108
  583.1 3.0 constant_dynamic-update-slice_fusion.2
  586.1 2.5 constant_dynamic-slice_fusion
  589.1 3.0 stack.39
  (12 shorter events, 0.4 us)
Async XLA Ops:
  17.5 100.5 %all-to-all-start = ((f32[3,1024,512]{2,0,1:T(4,128)}), f32[3,1024,512]{2,0,1:T(4,128)}, u32[]{:S(2)}, u32[]{:S(2)}) async-start(f32[3,1024,512]{2,0,1:T(4,128)} %copy.28), calls=%async_computation | async-start | bytes 16777216 | tf_op jit(solution)/shard_map/all_to_all | solution.py:86
  23.1 300.8 %all-gather.4.cloned.1.call-start = ((), (), s32[]{:S(2)}) async-start(), calls=%async_computation.1 | async-start | bytes 15728640 | tf_op jit(solution)/shard_map/all_gather | solution.py:92
  133.3 22.3 %copy-start.1 = (f32[3072,512]{0,1:T(8,128)S(1)}, f32[3072,512]{0,1:T(8,128)}, u32[]{:S(2)}) copy-start(f32[3072,512]{0,1:T(8,128)} %copy.31) | copy-start | bytes 18874372
  199.2 129.1 %copy-start.4 = (s32[2,8]{1,0:T(2,128)S(1)}, s32[2,8]{1,0:T(2,128)}, u32[]{:S(2)}) copy-start(s32[2,8]{1,0:T(2,128)} %param.3) | copy-start | bytes 196
  205.9 343.6 %all-gather.6.cloned.1.call-start = ((), (), s32[]{:S(2)}) async-start(), calls=%async_computation.2 | async-start | bytes 2662400 | tf_op jit(solution)/shard_map/all_gather | solution.py:107
  323.9 140.6 %collective-permute-start = (bf16[12,8,128,512]{3,2,0,1:T(8,128)(2,1)}, bf16[12,8,128,512]{3,2,0,1:T(8,128)(2,1)}, u32[]{:S(2)}, u32[]{:S(2)}) collective-permute-start(bf16[12,8,128,512]{3,2,0,1:T(8,128)(2,1)} %all-gather.4.cloned.1.call-done), channel_id=1, source_target_pairs={{1,0},{2,1},{3,2},{4,3},{5,4},{6,5},{7,6},{8,7},{9,8},{10,9},{11,1... | collective-permute-start | bytes 37748744 | tf_op jit(solution)/shard_map/ppermute | solution.py:14
  482.9 3.9 copy-start
  506.1 13.8 %copy-start.2 = (f32[2,8,65,128]{3,1,2,0:T(8,128)}, f32[2,8,65,128]{3,1,2,0:T(8,128)S(1)}, u32[]{:S(2)}) copy-start(f32[2,8,65,128]{3,1,2,0:T(8,128)S(1)} %copy.35) | copy-start | bytes 1597444
  506.2 12.9 %collective-permute-start.1 = (f32[2,8,65,128]{3,1,2,0:T(8,128)S(1)}, f32[2,8,65,128]{3,1,2,0:T(8,128)S(1)}, u32[]{:S(2)}, u32[]{:S(2)}) collective-permute-start(f32[2,8,65,128]{3,1,2,0:T(8,128)S(1)} %copy.35), channel_id=1, source_target_pairs={{0,1},{1,2},{2,3},{3,4},{4,5},{5,6},{6,7},{7,8},{8,9},{9,10},{10,1... | collective-permute-start | bytes 1597448 | tf_op jit(solution)/shard_map/ppermute | solution.py:14
  519.0 0.8 copy-start.3
  519.8 63.2 %all-gather.8.cloned.1.call-start = ((), (), s32[]{:S(2)}) async-start(), calls=%async_computation.3 | async-start | bytes 2662400 | tf_op jit(solution)/shard_map/all_gather | solution.py:108
Sparse Core Ops, SparseCore 0:
  206.1 117.8 all-gather.3
  520.0 29.5 all-gather.5
  551.8 31.1 all-gather.7
where the time goes:
time: 608 us; the launch traced here: 599 us
  waiting for transfers between devices  396 us (65%)
  local copies, waits for them, and re-layouts  106 us (17%)
  matrix products  39.4 us (6%)
  other arithmetic  30.9 us (5%)
  between operations  14.2 us (2%)
  starting transfers between devices  12 us (2%)
    ppermute x2, waiting for transfers between devices, from_behind(): return lax.ppermute(block, axis, route)  125 us
    all_gather x1, waiting for transfers between devices, shards(): group = lax.all_gather(white, 'seg', axis=1, tiled=True)  118 us
    all_to_all x1, waiting for transfers between devices, shards(): lax.all_to_all(records, 'seg', split_axis=1, concat_axis=0, tiled=True)  92.7 us
    unnamed x23, local copies, waits for them, and re-layouts  44.6 us
    all_gather x1, waiting for transfers between devices, shards(): lax.all_gather(forward, 'seg', axis=0, tiled=True)  30.4 us
    all_gather x1, waiting for transfers between devices, shards(): lax.all_gather(behind, 'seg', axis=0, tiled=True)  29 us
    dot_general x1, matrix products, whiten(): jnp.dot(jnp.abs(flat), smooth_table(length, SMOOTH), precision=lax.Precis...  22.3 us
    unnamed x2, other arithmetic  19.2 us
  transfers between devices with their start and end apart: 6, of which 6 were waited for; matrix products, arithmetic and copies ran while one was open for 5% of the time, Pallas kernels for 0%

commit v1 on v0

v1 whole, which is shorter than its diff:
```python
import functools

import jax
import jax.numpy as jnp
import ml_dtypes
import numpy as np
from jax import lax
from jax.experimental import pallas as pl
from jax.experimental.pallas import tpu as pltpu
from jax.sharding import PartitionSpec as P

BINS = 256
LENGTH = 512
CHANS = 128
MAXLAG = 32
LAGS = 2 * MAXLAG + 1
REACH = 8
SMOOTH = 32
BAND = 64
GROUP = 8
HALF = GROUP // 2
ROWS = 256
SUB = 128
SLOTS = 13
BODY = 64
CHUNK = SLOTS * BODY + 16
SEND2 = 8 * BODY + 16
SEND3 = 4 * BODY + 16
VMEM_LIMIT = 56 * 1024 * 1024
BF = jnp.bfloat16
F32 = jnp.float32


def split(array):
    high = array.astype(ml_dtypes.bfloat16)
    low = (array - high.astype(np.float32)).astype(ml_dtypes.bfloat16)
    return high, low


def tables():
    times = np.arange(LENGTH)
    inside = (np.abs(times[:, None] - times[None, :]) <= SMOOTH).astype(np.float32)
    share = (1.0 / inside.sum(0, keepdims=True)).astype(np.float32)
    band = inside.astype(ml_dtypes.bfloat16)
    phase = (times[:, None] * np.arange(BINS)[None, :] % LENGTH) * (2.0 * np.pi / LENGTH)
    fourier = np.concatenate([np.cos(phase), -np.sin(phase)], axis=1).astype(np.float32)
    fhi, flo = split(fourier)
    which = np.arange(BINS) // BAND
    same = ((which[:, None] == which[None, :]) / (2.0 * BAND)).astype(ml_dtypes.bfloat16)
    return band, share, fhi, flo, same


def lag_rows(segments):
    shifts = np.arange(-MAXLAG, MAXLAG + 1)
    phase = (shifts[:, None] * np.arange(BINS)[None, :] % LENGTH) * (2.0 * np.pi / LENGTH)
    table = np.concatenate([np.cos(phase), -np.sin(phase)], axis=1) / np.sqrt(segments * BINS)
    table = np.concatenate([table, np.zeros((80 - LAGS, LENGTH))], axis=0).astype(np.float32)
    return np.concatenate(split(table), axis=0)


def dot(a, b):
    return jnp.dot(a, b, preferred_element_type=F32)


def dot_nt(a, b):
    return lax.dot_general(a, b, (((1,), (1,)), ((), ())), preferred_element_type=F32)


def halves(x):
    high = x.astype(BF)
    return high, (x - high.astype(F32)).astype(BF)


def whiten_body(half, records, band, share, fhi, flo, same, white):
    del half
    for part in range(ROWS // SUB):
        x = records[0, pl.ds(part * SUB, SUB), :]
        ahi, alo = halves(jnp.abs(x))
        level = (dot(ahi, band[...]) + dot(alo, band[...])) * share[...]
        nhi, nlo = halves(x / (level + 1e-06))
        spectrum = dot(nhi, fhi[...]) + dot(nlo, fhi[...]) + dot(nhi, flo[...])
        re = spectrum[:, :BINS]
        im = spectrum[:, BINS:]
        power = dot((re * re + im * im).astype(BF), same[...])
        factor = lax.rsqrt(power + 1e-05)
        white[part, 0, :, :BINS] = (re * factor).astype(BF)
        white[part, 0, :, BINS:] = (im * factor).astype(BF)


def whiten(half, records, consts):
    segs = records.shape[0]
    steps = HALF * CHANS // ROWS
    per = ROWS // CHANS

    def whole(array):
        return pl.BlockSpec(array.shape, lambda s, i, h: (0, 0))

    return pl.pallas_call(
        whiten_body,
        grid_spec=pltpu.PrefetchScalarGridSpec(
            num_scalar_prefetch=1,
            grid=(segs, steps),
            in_specs=[pl.BlockSpec((1, ROWS, LENGTH), lambda s, i, h: (s, h[0] * steps + i, 0))]
            + [whole(c) for c in consts],
            out_specs=pl.BlockSpec((per, 1, CHANS, LENGTH), lambda s, i, h: (i, s, 0, 0)),
        ),
        out_shape=jax.ShapeDtypeStruct((HALF, segs, CHANS, LENGTH), BF),
        compiler_params=pltpu.CompilerParams(vmem_limit_bytes=VMEM_LIMIT),
        cost_estimate=pl.CostEstimate(
            flops=segs * HALF * CHANS * LENGTH * LENGTH * 11,
            bytes_accessed=segs * HALF * CHANS * LENGTH * 6,
            transcendentals=0,
        ),
        name="whiten",
    )(half, records, *consts)


def row_of(b, p, total):
    return lax.rem(b * GROUP - HALF + p + total, total)


def correlate_body(
    meta, tab, own_ext, own_int, got_ext, got_int, lag, keep, out1, out2, out3, slots, win, stk, pq, cnt, sems
):
    b = meta[0]
    s = meta[1]
    core = meta[2]
    segs = win.shape[1]
    total = tab.shape[0] // REACH

    def load(k, source, quad):
        return pltpu.make_async_copy(source, win.at[pl.ds(quad * HALF, HALF)], sems.at[k])

    copies = [
        load(0, own_ext, 1 + core),
        load(1, own_int, 2 - core),
        load(2, got_ext, 3 * core),
        load(3, got_int, 3 - 3 * core),
    ]
    for copy in copies:
        copy.start()
    for k in range(4):
        cnt[k] = 0
    for copy in copies:
        copy.wait()

    def put(owner, entry, stack):
        n = cnt[owner]
        cnt[owner] = n + 1
        slots[entry] = n
        r = jnp.bitwise_and(owner - s, 3)
        stk[r, pl.ds(pl.multiple_of(n * BODY, BODY), BODY), :] = stack[:BODY]
        stk[r, pl.ds(SLOTS * BODY + n, 1), :] = stack[BODY:LAGS]

    def pair(p, d):
        q = p + d
        for chunk in range(CHANS // 16):
            rows = pl.ds(chunk * 16, 16)
            real = jnp.zeros((16, BINS), F32)
            imag = jnp.zeros((16, BINS), F32)
            for k in range(segs):
                are = win[p, k, rows, :BINS].astype(F32)
                aim = win[p, k, rows, BINS:].astype(F32)
                bre = win[q, k, rows, :BINS].astype(F32)
                bim = win[q, k, rows, BINS:].astype(F32)
                real += are * bre + aim * bim
                imag += are * bim - aim * bre
            rhi, rlo = halves(real)
            ihi, ilo = halves(imag)
            pq[0, rows, :BINS] = rhi
            pq[0, rows, BINS:] = ihi
            pq[1, rows, :BINS] = rlo
            pq[1, rows, BINS:] = ilo
        both = dot_nt(lag[...], pq[0])
        stack = both[:80] + both[80:] + dot_nt(lag[:80], pq[1])
        owner = jnp.where(p < HALF, 2 + p // 2, (p - HALF) // 2)
        put(owner, p * REACH + d - 1, stack)
        far = p - 6
        near = q - 12

        @pl.when((far >= 0) & (far < 2) & (near >= 0) & (near < 2))
        def _():
            put(0, 96 + far * 2 + near, stack)

    def visit(n, carry):
        p = n // REACH
        d = n % REACH + 1
        live = tab[row_of(b, p, total) * REACH + d - 1] != 0
        here = jnp.where(p < HALF, p + d >= HALF, (p + d < 12) | (p < 8))

        @pl.when(live & here)
        def _():
            pair(p, d)

        return carry

    lax.fori_loop(0, 12 * REACH, visit, 0)
    keep[...] = stk[0]
    out1[...] = stk[1].astype(BF)
    out2[...] = stk[2].astype(BF)
    out3[...] = stk[3].astype(BF)


def correlate(meta, tab, own_ext, own_int, got_ext, got_int, lag):
    segs = own_ext.shape[1]
    smem = pl.BlockSpec(memory_space=pltpu.SMEM)
    vmem = pl.BlockSpec(memory_space=pltpu.VMEM)
    hbm = pl.BlockSpec(memory_space=pl.ANY)
    chunk = jax.ShapeDtypeStruct((CHUNK, CHANS), BF)
    return pl.pallas_call(
        correlate_body,
        in_specs=[smem, smem, hbm, hbm, hbm, hbm, vmem],
        out_specs=[vmem, vmem, vmem, vmem, smem],
        out_shape=[
            jax.ShapeDtypeStruct((CHUNK, CHANS), F32),
            chunk,
            chunk,
            chunk,
            jax.ShapeDtypeStruct((128,), jnp.int32),
        ],
        scratch_shapes=[
            pltpu.VMEM((4 * HALF, segs, CHANS, LENGTH), BF),
            pltpu.VMEM((4, CHUNK, CHANS), F32),
            pltpu.VMEM((2, CHANS, LENGTH), BF),
            pltpu.SMEM((4,), jnp.int32),
            pltpu.SemaphoreType.DMA((4,)),
        ],
        compiler_params=pltpu.CompilerParams(vmem_limit_bytes=VMEM_LIMIT),
        name="correlate",
    )(meta, tab, own_ext, own_int, got_ext, got_int, lag)


def combine_body(meta, tab, slots, keep, got1, got2, got3, full, send2, out1, out2, out3, stage2, stage3):
    b = meta[0]
    s = meta[1]
    total = tab.shape[0] // REACH
    full[...] = (keep[...] + got1[...].astype(F32)) + (got2[...].astype(F32) + got3[...].astype(F32))

    def move(entry, p, d, dest, size, k):
        @pl.when(tab[row_of(b, p, total) * REACH + d - 1] != 0)
        def _():
            n = slots[entry]
            dest[pl.ds(k * BODY, BODY), :] = full[pl.ds(pl.multiple_of(n * BODY, BODY), BODY), :]
            dest[pl.ds(size * BODY + k, 1), :] = full[pl.ds(SLOTS * BODY + n, 1), :]

    @pl.when(s >= 2)
    def _():
        stage2[: 8 * BODY, :] = full[: 8 * BODY, :]
        stage2[8 * BODY :, :] = full[SLOTS * BODY :, :]

    for owner in (0, 1):

        @pl.when(s == owner)
        def _(owner=owner):
            for k, (i, j) in enumerate(UPWARD[owner]):
                p, d = HALF + i, GROUP + j - i
                entry = p * REACH + d - 1 if i // 2 == owner else 96 + (i - 2) * 2 + j
                move(entry, p, d, stage2, 8, k)

    send2[...] = stage2[...].astype(send2.dtype)
    for r, out in ((1, out1), (2, out2), (3, out3)):
        to = jnp.bitwise_and(s + r, 3)

        @pl.when((s < to) | (s >= 2))
        def _(r=r, to=to):
            for i in range(2):
                for j in range(2):
                    ahead = s < to
                    row = 2 * s + i
                    p = jnp.where(ahead, HALF + row, row - HALF)
                    d = 2 * to + j - row + jnp.where(ahead, 0, GROUP)
                    move(p * REACH + d - 1, p, d, stage3.at[r - 1], 4, 2 * i + j)

        out[...] = stage3[r - 1].astype(out.dtype)


UPWARD = (
    ((0, 0), (1, 0), (1, 1), (2, 0), (2, 1), (3, 0), (3, 1)),
    ((2, 2), (3, 2), (3, 3)),
)


def combine(meta, tab, slots, keep, got1, got2, got3):
    smem = pl.BlockSpec(memory_space=pltpu.SMEM)
    vmem = pl.BlockSpec(memory_space=pltpu.VMEM)
    third = jax.ShapeDtypeStruct((SEND3, CHANS), BF)
    return pl.pallas_call(
        combine_body,
        in_specs=[smem, smem, smem, vmem, vmem, vmem, vmem],
        out_specs=[vmem] * 5,
        out_shape=[
            jax.ShapeDtypeStruct((CHUNK, CHANS), F32),
            jax.ShapeDtypeStruct((SEND2, CHANS), BF),
            third,
            third,
            third,
        ],
        scratch_shapes=[
            pltpu.VMEM((SEND2, CHANS), F32),
            pltpu.VMEM((3, SEND3, CHANS), F32),
        ],
        compiler_params=pltpu.CompilerParams(vmem_limit_bytes=VMEM_LIMIT),
        name="combine",
    )(meta, tab, slots, keep, got1, got2, got3)


def finish_body(meta, tab, slots, full, got2, got31, got32, got33, fwd, bwd, two, three):
    b = meta[0]
    s = meta[1]
    total = tab.shape[0] // REACH
    two[...] = got2[...].astype(F32)
    three[0] = got31[...].astype(F32)
    three[1] = got32[...].astype(F32)
    three[2] = got33[...].astype(F32)
    fwd[...] = jnp.zeros(fwd.shape, F32)
    bwd[...] = jnp.zeros(bwd.shape, F32)

    def live(p, d):
        return tab[row_of(b, p, total) * REACH + d - 1] != 0

    def ahead(source, size, n, i, d):
        fwd[i, d - 1, pl.ds(0, BODY), :] = source[pl.ds(pl.multiple_of(n * BODY, BODY), BODY), :]
        fwd[i, d - 1, pl.ds(BODY, 1), :] = source[pl.ds(size * BODY + n, 1), :]

    def behind(source, size, n, j, d):
        bwd[j, d - 1, pl.ds(0, 1), :] = source[pl.ds(size * BODY + n, 1), :]
        for m in range(1, LAGS):
            bwd[j, d - 1, pl.ds(m, 1), :] = source[pl.ds(n * BODY + BODY - m, 1), :]

    from_above = jnp.int32(0)
    for i in range(2):
        for d in range(1, REACH + 1):
            row = 2 * s + i
            p = HALF + row
            on = live(p, d)
            crossed = (s >= 2) & (row + d >= GROUP)

            @pl.when(on & jnp.logical_not(crossed))
            def _(i=i, d=d, p=p):
                ahead(full, SLOTS, slots[p * REACH + d - 1], i, d)

            @pl.when(on & crossed)
            def _(i=i, d=d, n=from_above):
                ahead(two, 8, n, i, d)

            from_above = from_above + jnp.where(on & crossed, 1, 0)

    for j in range(2):
        for d in range(1, REACH + 1):
            col = 2 * s + j
            low = col - d
            p = HALF + low
            on = live(p, d)
            before = low < 0
            row = jnp.where(before, low + GROUP, low)
            owner = row // 2
            up = before & (owner < 2)
            mine = (owner == s) & jnp.logical_not(up)

            @pl.when(on & mine)
            def _(j=j, d=d, p=p):
                behind(full, SLOTS, slots[p * REACH + d - 1], j, d)

            @pl.when(on & up)
            def _(j=j, d=d, row=row):
                k0 = jnp.where(row == 0, 0, 2 * row - 1) + j
                k1 = jnp.where(row == 2, 0, 1) + j
                behind(two, 8, jnp.where(s == 0, k0, k1), j, d)

            @pl.when(on & jnp.logical_not(mine) & jnp.logical_not(up))
            def _(j=j, d=d, row=row, owner=owner):
                r = jnp.bitwise_and(s - owner, 3)
                behind(three.at[r - 1], 4, (row - 2 * owner) * 2 + j, j, d)


def finish(meta, tab, slots, full, got2, got31, got32, got33, blocks):
    smem = pl.BlockSpec(memory_space=pltpu.SMEM)
    vmem = pl.BlockSpec(memory_space=pltpu.VMEM)
    out = jax.ShapeDtypeStruct((blocks, REACH, LAGS, CHANS), F32)
    return pl.pallas_call(
        finish_body,
        in_specs=[smem, smem, smem] + [vmem] * 5,
        out_specs=[vmem, vmem],
        out_shape=[out, out],
        scratch_shapes=[
            pltpu.VMEM((SEND2, CHANS), F32),
            pltpu.VMEM((3, SEND3, CHANS), F32),
        ],
        compiler_params=pltpu.CompilerParams(vmem_limit_bytes=VMEM_LIMIT),
        name="finish",
    )(meta, tab, slots, full, got2, got31, got32, got33)


def shards(groups, planes, consts, lag, records, pairs):
    b = lax.axis_index("blk").astype(jnp.int32)
    s = lax.axis_index("seg").astype(jnp.int32)
    core = jnp.bitwise_and(b, 1)
    meta = jnp.stack([b, s, core])
    tab = lax.all_gather(pairs.reshape(-1), ("blk", "seg"), tiled=True)

    outer = [(g, (g + 1) % groups if g % 2 else (g - 1) % groups) for g in range(groups)]
    inner = [(g, g ^ 1) for g in range(groups)]
    own_ext = whiten(core[None], records, consts)
    got_ext = lax.ppermute(own_ext, "blk", outer)
    own_int = whiten((1 - core)[None], records, consts)
    got_int = lax.ppermute(own_int, "blk", inner)
    keep, out1, out2, out3, slots = correlate(meta, tab, own_ext, own_int, got_ext, got_int, lag)

    def ring(x, r):
        return lax.ppermute(x, "seg", [(z, (z + r) % planes) for z in range(planes)])

    full, send2, s31, s32, s33 = combine(
        meta, tab, slots, keep, ring(out1, 1), ring(out2, 2), ring(out3, 3)
    )
    shift = [
        (z * groups + g, z * groups + (g + (1 if z < 2 else -1)) % groups)
        for z in range(planes)
        for g in range(groups)
    ]
    got2 = lax.ppermute(send2, ("seg", "blk"), shift)
    return tuple(
        finish(
            meta, tab, slots, full, got2, ring(s31, 1), ring(s32, 2), ring(s33, 3), pairs.shape[0]
        )
    )


def solution(mesh):
    groups = mesh.shape["blk"]
    planes = mesh.shape["seg"]
    consts = tables()

    def run(records, pairs):
        body = functools.partial(
            shards,
            groups,
            planes,
            tuple(jnp.asarray(c) for c in consts),
            jnp.asarray(lag_rows(records.shape[0])),
        )
        return jax.shard_map(
            body,
            mesh=mesh,
            in_specs=(P("seg", "blk", None), P(("blk", "seg"), None)),
            out_specs=(P(("blk", "seg"), None, None, None), P(("blk", "seg"), None, None, None)),
            check_vma=False,
        )(records, pairs)

    return run
```

time: 608 us -> 143 us (0.24)
  the two profiles are of different devices: /device:TPU:6 before, /device:TPU:0 now
where the time goes in v1:
time: 143 us
  blocking collectives  66.7 us (47%)
  Pallas kernels  35.2 us (25%)
  starting transfers between devices  16.7 us (12%)
  waiting for transfers between devices  14.3 us (10%)
  local copies, waits for them, and re-layouts  8.65 us (6%)
    unnamed x1, blocking collectives  66.7 us
    pallas_call x2, Pallas kernels, whiten(): pl.pallas_call(whiten_body, grid_spec=pltpu.PrefetchScalarGridSpec(num_sc...  21 us
    ppermute x6, waiting for transfers between devices, ring(): lax.ppermute(x, 'seg', [(z, (z + r) % planes) for z in range(planes)])  14.2 us
    ppermute x6, starting transfers between devices, ring(): lax.ppermute(x, 'seg', [(z, (z + r) % planes) for z in range(planes)])  12 us
    pallas_call x1, Pallas kernels, correlate(): pl.pallas_call(correlate_body, in_specs=[smem, smem, hbm, hbm, hbm, hbm,...  8.61 us
    ppermute x1, starting transfers between devices, shards(): got_ext = lax.ppermute(own_ext, 'blk', outer)  4.73 us
    unnamed x25, local copies, waits for them, and re-layouts  4.64 us
    pallas_call x2, local copies, waits for them, and re-layouts, finish(): pl.pallas_call(finish_body, in_specs=[smem, smem, smem] + [vmem] * 5, out...  3.93 us
  transfers between devices with their start and end apart: 9, of which 5 were waited for; matrix products, arithmetic and copies ran while one was open for 1% of the time, Pallas kernels for 7%

profile of v1, /device:TPU:0, one launch (start us, length us, event | category | flops | bytes accessed | tf_op | source)
XLA Modules:
  0.0 143.4 jit_solution(9183795438593675663)
XLA Ops:
  0.6 10.5 %whiten.2.own_ext = bf16[4,3,128,512]{3,2,1,0:T(8,128)(2,1)} custom-call(s32[1]{0:T(128)} %bitcast.2.half, f32[3,1024,512]{2,1,0:T(8,128)} %records.3, bf16[512,512]{1,0:T(8,128)(2,1)} %constant.23.clone.band, f32[1,512]{1,0:T(1,128)} %constant.24.clone.share, bf16[512,512]{1,0:T(8,128)(2,1)} %constant.25.clone.fhi, bf16[512,512]{1,0:T(8,128)(2,1)} %constant.26.clone.flo, ...), custom_call_target="tpu_custom_call" | custom-call | flops 4429185024 | bytes 4718592 | tf_op jit(solution)/shard_map/whiten/pallas_call | solution.py:98
  11.1 4.7 %collective-permute-start = (bf16[4,3,128,512]{3,2,1,0:T(8,128)(2,1)}, bf16[4,3,128,512]{3,2,1,0:T(8,128)(2,1)S(1)}, u32[]{:S(2)}, u32[]{:S(2)}) collective-permute-start(bf16[4,3,128,512]{3,2,1,0:T(8,128)(2,1)} %whiten.2.own_ext), channel_id=1, source_target_pairs={{0,31},{1,2},{2,1},{3,4},{4,3},{5,6},{6,5},{7,8},{8,7},{9,10},{10,... | collective-permute-start | bytes 4718600 | tf_op jit(solution)/shard_map/ppermute | solution.py:404
  15.9 0.0 copy-start.9
  15.9 0.0 copy-start.10
  15.9 10.5 %whiten.3.own_int = bf16[4,3,128,512]{3,2,1,0:T(8,128)(2,1)} custom-call(s32[1]{0:T(128)} %bitcast.4.half, f32[3,1024,512]{2,1,0:T(8,128)} %records.3, bf16[512,512]{1,0:T(8,128)(2,1)} %constant.23.clone.band, f32[1,512]{1,0:T(1,128)} %constant.24.clone.share, bf16[512,512]{1,0:T(8,128)(2,1)} %constant.25.clone.fhi, bf16[512,512]{1,0:T(8,128)(2,1)} %constant.26.clone.flo, ...), custom_call_target="tpu_custom_call" | custom-call | flops 4429185024 | bytes 4718592 | tf_op jit(solution)/shard_map/whiten/pallas_call | solution.py:98
  26.4 0.0 collective-permute-start.1
  26.4 0.0 copy-done.9
  26.4 0.1 reshape.8
  26.5 0.0 copy-done.10
  26.5 0.7 dynamic-slice
  27.8 0.3 dynamic-update-slice
  28.1 66.7 %all-reduce.tab = s32[2048]{0:T(1024)} all-reduce(s32[2048]{0:T(1024)S(1)} %dynamic-update-slice), channel_id=1, replica_groups=mesh['seg'=4,'blk'=32] {'blk','seg'}, use_global_device_ids=true, to_apply=%add | all-reduce | flops 2048 | bytes 16384
  94.8 0.6 pad_add_fusion.meta
  95.4 0.0 collective-permute-done.got_ext
  95.4 0.0 copy-start
  95.4 0.0 collective-permute-done.1.got_int
  95.4 1.1 copy-done
  96.5 0.0 copy-start.1
  96.5 1.2 copy-done.1
  97.7 8.6 %correlate.1 = (f32[848,128]{1,0:T(8,128)}, bf16[848,128]{1,0:T(8,128)(2,1)}, bf16[848,128]{1,0:T(8,128)(2,1)}, bf16[848,128]{1,0:T(8,128)(2,1)}, s32[128]{0:T(128)}) custom-call(s32[3]{0:T(128)} %pad_add_fusion.meta, s32[2048]{0:T(1024)} %all-reduce.tab, bf16[4,3,128,512]{3,2,1,0:T(8,128)(2,1)} %whiten.2.own_ext, bf16[4,3,128,512]{3,2,1,0:T(8,128)(2,1)} %whiten.3.own_int, ...), custom_call_target="tpu_custom_call" | custom-call | tf_op jit(solution)/shard_map/correlate/pallas_call | solution.py:210
  106.3 0.1 collective-permute-start.2
  106.4 1.7 %collective-permute-start.3 = (bf16[848,128]{1,0:T(8,128)(2,1)}, bf16[848,128]{1,0:T(8,128)(2,1)S(1)}, u32[]{:S(2)}, u32[]{:S(2)}) collective-permute-start(bf16[848,128]{1,0:T(8,128)(2,1)} %get-tuple-element.15), channel_id=1, source_target_pairs={{0,64},{32,96},{64,0},{96,32},{1,65},{33,97},{65,1},{97,33},{2,66}... | collective-permute-start | bytes 651272 | tf_op jit(solution)/shard_map/ppermute | solution.py:410
  108.1 2.4 %collective-permute-start.4 = (bf16[848,128]{1,0:T(8,128)(2,1)}, bf16[848,128]{1,0:T(8,128)(2,1)S(1)}, u32[]{:S(2)}, u32[]{:S(2)}) collective-permute-start(bf16[848,128]{1,0:T(8,128)(2,1)} %get-tuple-element.16), channel_id=1, source_target_pairs={{0,96},{32,0},{64,32},{96,64},{1,97},{33,1},{65,33},{97,65},{2,98}... | collective-permute-start | bytes 651272 | tf_op jit(solution)/shard_map/ppermute | solution.py:410
  110.5 9.1 %collective-permute-done.2.got1 = bf16[848,128]{1,0:T(8,128)(2,1)S(1)} collective-permute-done((bf16[848,128]{1,0:T(8,128)(2,1)}, bf16[848,128]{1,0:T(8,128)(2,1)S(1)}, u32[]{:S(2)}, u32[]{:S(2)}) %collective-permute-start.2) | collective-permute-done | bytes 217120 | tf_op jit(solution)/shard_map/ppermute | solution.py:410
  119.6 0.0 copy-start.2
  119.6 0.0 collective-permute-done.3.got2
  119.6 0.0 copy-start.3
  119.6 0.6 collective-permute-done.4.got3
  120.2 0.0 copy-start.4
  120.2 0.0 copy-done.2
  120.2 0.1 copy-done.3
  120.3 0.5 copy-done.4
  120.9 2.5 %combine.1 = (f32[848,128]{1,0:T(8,128)}, bf16[528,128]{1,0:T(8,128)(2,1)}, bf16[272,128]{1,0:T(8,128)(2,1)}, bf16[272,128]{1,0:T(8,128)(2,1)}, bf16[272,128]{1,0:T(8,128)(2,1)}) custom-call(s32[3]{0:T(128)} %pad_add_fusion.meta, s32[2048]{0:T(1024)} %all-reduce.tab, s32[128]{0:T(128)} %get-tuple-element.12.slots, f32[848,128]{1,0:T(8,128)} %get-tuple-element.13.keep, ...), custom_call_target="tpu_custom_call" | custom-call | tf_op jit(solution)/shard_map/combine/pallas_call | solution.py:287
  123.4 0.0 collective-permute-start.5
  123.4 1.0 collective-permute-start.6
  124.4 6.9 %collective-permute-start.7 = (bf16[272,128]{1,0:T(8,128)(2,1)}, bf16[272,128]{1,0:T(8,128)(2,1)S(1)}, u32[]{:S(2)}, u32[]{:S(2)}) collective-permute-start(bf16[272,128]{1,0:T(8,128)(2,1)} %get-tuple-element.20), channel_id=1, source_target_pairs={{0,64},{32,96},{64,0},{96,32},{1,65},{33,97},{65,1},{97,33},{2,66}... | collective-permute-start | bytes 208904 | tf_op jit(solution)/shard_map/ppermute | solution.py:410
  131.3 0.0 collective-permute-start.8
  131.3 1.0 collective-permute-done.6.got31
  132.3 0.0 copy-start.6
  132.3 2.2 %collective-permute-done.7.got32 = bf16[272,128]{1,0:T(8,128)(2,1)S(1)} collective-permute-done((bf16[272,128]{1,0:T(8,128)(2,1)}, bf16[272,128]{1,0:T(8,128)(2,1)S(1)}, u32[]{:S(2)}, u32[]{:S(2)}) %collective-permute-start.7) | collective-permute-done | bytes 69664 | tf_op jit(solution)/shard_map/ppermute | solution.py:410
  134.5 0.0 copy-start.7
  134.5 1.3 collective-permute-done.8.got33
  135.8 0.0 copy-start.8
  135.8 0.0 collective-permute-done.5.got2
  135.8 0.0 copy-start.5
  135.8 0.0 copy-done.6
  135.8 0.0 copy-done.7
  135.8 0.6 copy-done.8
  136.4 0.1 copy-done.5
  136.5 3.0 %finish.1 = (f32[2,8,65,128]{3,2,1,0:T(8,128)}, f32[2,8,65,128]{3,2,1,0:T(8,128)}) custom-call(s32[3]{0:T(128)} %pad_add_fusion.meta, s32[2048]{0:T(1024)} %all-reduce.tab, s32[128]{0:T(128)} %get-tuple-element.12.slots, f32[848,128]{1,0:T(8,128)} %get-tuple-element.17.full, bf16[528,128]{1,0:T(8,128)(2,1)} %copy-done.5, bf16[272,128]{1,0:T(8,128)(2,1)} %copy-done.6, ...), custom_call_target="tpu_custom_call" | custom-call | tf_op jit(solution)/shard_map/finish/pallas_call | solution.py:380
  139.5 2.0 %copy.10 = f32[2,8,65,128]{3,1,2,0:T(8,128)} copy(f32[2,8,65,128]{3,2,1,0:T(8,128)} %get-tuple-element.22) | data formatting | bytes 1064960 | tf_op jit(solution)/shard_map/finish/pallas_call | solution.py:380
  141.5 2.0 %copy.11 = f32[2,8,65,128]{3,1,2,0:T(8,128)} copy(f32[2,8,65,128]{3,2,1,0:T(8,128)} %get-tuple-element.23) | data formatting | bytes 1064960 | tf_op jit(solution)/shard_map/finish/pallas_call | solution.py:380
  (1 shorter events, 0.0 us)
Async XLA Ops:
  11.1 84.2 %collective-permute-start = (bf16[4,3,128,512]{3,2,1,0:T(8,128)(2,1)}, bf16[4,3,128,512]{3,2,1,0:T(8,128)(2,1)S(1)}, u32[]{:S(2)}, u32[]{:S(2)}) collective-permute-start(bf16[4,3,128,512]{3,2,1,0:T(8,128)(2,1)} %whiten.2.own_ext), channel_id=1, source_target_pairs={{0,31},{1,2},{2,1},{3,4},{4,3},{5,6},{6,5},{7,8},{8,7},{9,10},{10,... | collective-permute-start | bytes 4718600 | tf_op jit(solution)/shard_map/ppermute | solution.py:404
  15.9 10.5 %copy-start.9 = (s32[2,8]{1,0:T(2,128)S(1)}, s32[2,8]{1,0:T(2,128)}, u32[]{:S(2)}) copy-start(s32[2,8]{1,0:T(2,128)} %param.9) | copy-start | bytes 196
  15.9 10.6 %copy-start.10 = (u32[128]{0:T(128)S(1)}, u32[128]{0:T(128)}, u32[]{:S(2)}) copy-start(u32[128]{0:T(128)} %constant.33) | copy-start | bytes 1540
  26.4 69.0 %collective-permute-start.1 = (bf16[4,3,128,512]{3,2,1,0:T(8,128)(2,1)}, bf16[4,3,128,512]{3,2,1,0:T(8,128)(2,1)S(1)}, u32[]{:S(2)}, u32[]{:S(2)}) collective-permute-start(bf16[4,3,128,512]{3,2,1,0:T(8,128)(2,1)} %whiten.3.own_int), channel_id=1, source_target_pairs={{0,1},{1,0},{2,3},{3,2},{4,5},{5,4},{6,7},{7,6},{8,9},{9,8},{10,11... | collective-permute-start | bytes 4718600 | tf_op jit(solution)/shard_map/ppermute | solution.py:406
  95.4 1.2 copy-start
  96.5 1.2 copy-start.1
  106.3 13.2 %collective-permute-start.2 = (bf16[848,128]{1,0:T(8,128)(2,1)}, bf16[848,128]{1,0:T(8,128)(2,1)S(1)}, u32[]{:S(2)}, u32[]{:S(2)}) collective-permute-start(bf16[848,128]{1,0:T(8,128)(2,1)} %get-tuple-element.14), channel_id=1, source_target_pairs={{0,32},{32,64},{64,96},{96,0},{1,33},{33,65},{65,97},{97,1},{2,34}... | collective-permute-start | bytes 651272 | tf_op jit(solution)/shard_map/ppermute | solution.py:410
  106.4 13.2 %collective-permute-start.3 = (bf16[848,128]{1,0:T(8,128)(2,1)}, bf16[848,128]{1,0:T(8,128)(2,1)S(1)}, u32[]{:S(2)}, u32[]{:S(2)}) collective-permute-start(bf16[848,128]{1,0:T(8,128)(2,1)} %get-tuple-element.15), channel_id=1, source_target_pairs={{0,64},{32,96},{64,0},{96,32},{1,65},{33,97},{65,1},{97,33},{2,66}... | collective-permute-start | bytes 651272 | tf_op jit(solution)/shard_map/ppermute | solution.py:410
  108.1 12.1 %collective-permute-start.4 = (bf16[848,128]{1,0:T(8,128)(2,1)}, bf16[848,128]{1,0:T(8,128)(2,1)S(1)}, u32[]{:S(2)}, u32[]{:S(2)}) collective-permute-start(bf16[848,128]{1,0:T(8,128)(2,1)} %get-tuple-element.16), channel_id=1, source_target_pairs={{0,96},{32,0},{64,32},{96,64},{1,97},{33,1},{65,33},{97,65},{2,98}... | collective-permute-start | bytes 651272 | tf_op jit(solution)/shard_map/ppermute | solution.py:410
  119.6 0.7 copy-start.2
  119.6 0.8 copy-start.3
  120.2 0.7 copy-start.4
  123.4 12.4 %collective-permute-start.5 = (bf16[528,128]{1,0:T(8,128)(2,1)}, bf16[528,128]{1,0:T(8,128)(2,1)S(1)}, u32[]{:S(2)}, u32[]{:S(2)}) collective-permute-start(bf16[528,128]{1,0:T(8,128)(2,1)} %get-tuple-element.18), channel_id=1, source_target_pairs={{0,1},{1,2},{2,3},{3,4},{4,5},{5,6},{6,7},{7,8},{8,9},{9,10},{10,1... | collective-permute-start | bytes 405512 | tf_op jit(solution)/shard_map/ppermute | solution.py:420
  123.4 8.9 %collective-permute-start.6 = (bf16[272,128]{1,0:T(8,128)(2,1)}, bf16[272,128]{1,0:T(8,128)(2,1)S(1)}, u32[]{:S(2)}, u32[]{:S(2)}) collective-permute-start(bf16[272,128]{1,0:T(8,128)(2,1)} %get-tuple-element.19), channel_id=1, source_target_pairs={{0,32},{32,64},{64,96},{96,0},{1,33},{33,65},{65,97},{97,1},{2,34}... | collective-permute-start | bytes 208904 | tf_op jit(solution)/shard_map/ppermute | solution.py:410
  124.4 10.1 %collective-permute-start.7 = (bf16[272,128]{1,0:T(8,128)(2,1)}, bf16[272,128]{1,0:T(8,128)(2,1)S(1)}, u32[]{:S(2)}, u32[]{:S(2)}) collective-permute-start(bf16[272,128]{1,0:T(8,128)(2,1)} %get-tuple-element.20), channel_id=1, source_target_pairs={{0,64},{32,96},{64,0},{96,32},{1,65},{33,97},{65,1},{97,33},{2,66}... | collective-permute-start | bytes 208904 | tf_op jit(solution)/shard_map/ppermute | solution.py:410
  131.3 4.5 %collective-permute-start.8 = (bf16[272,128]{1,0:T(8,128)(2,1)}, bf16[272,128]{1,0:T(8,128)(2,1)S(1)}, u32[]{:S(2)}, u32[]{:S(2)}) collective-permute-start(bf16[272,128]{1,0:T(8,128)(2,1)} %get-tuple-element.21), channel_id=1, source_target_pairs={{0,96},{32,0},{64,32},{96,64},{1,97},{33,1},{65,33},{97,65},{2,98}... | collective-permute-start | bytes 208904 | tf_op jit(solution)/shard_map/ppermute | solution.py:410
  132.3 3.5 %copy-start.6 = (bf16[272,128]{1,0:T(8,128)(2,1)}, bf16[272,128]{1,0:T(8,128)(2,1)S(1)}, u32[]{:S(2)}) copy-start(bf16[272,128]{1,0:T(8,128)(2,1)S(1)} %collective-permute-done.6.got31) | copy-start | bytes 208900
  134.5 1.3 copy-start.7
  135.8 0.6 copy-start.8
  135.8 0.7 copy-start.5

commit v2 on v1

v2 whole, which is shorter than its diff:
```python
import functools

import jax
import jax.numpy as jnp
import ml_dtypes
import numpy as np
from jax import lax
from jax.experimental import pallas as pl
from jax.experimental.pallas import tpu as pltpu
from jax.sharding import PartitionSpec as P

BINS = 256
LENGTH = 512
CHANS = 128
MAXLAG = 32
LAGS = 2 * MAXLAG + 1
REACH = 8
SMOOTH = 32
BAND = 64
GROUP = 8
HALF = GROUP // 2
ROWS = 512
SUB = 256
SLOTS = 8
BODY = 64
CHUNK = SLOTS * BODY + 16
SEND = 4 * BODY + 16
MIB = 1024 * 1024
BF = jnp.bfloat16
F32 = jnp.float32


def split(array):
    high = array.astype(ml_dtypes.bfloat16)
    low = (array - high.astype(np.float32)).astype(ml_dtypes.bfloat16)
    return high, low


def tables():
    times = np.arange(LENGTH)
    inside = (np.abs(times[:, None] - times[None, :]) <= SMOOTH).astype(np.float32)
    share = (1.0 / inside.sum(0, keepdims=True)).astype(np.float32)
    band = inside.astype(ml_dtypes.bfloat16)
    phase = (times[:, None] * np.arange(BINS)[None, :] % LENGTH) * (2.0 * np.pi / LENGTH)
    fourier = np.concatenate([np.cos(phase), -np.sin(phase)], axis=1).astype(np.float32)
    fhi, flo = split(fourier)
    which = np.arange(BINS) // BAND
    same = ((which[:, None] == which[None, :]) / (2.0 * BAND)).astype(ml_dtypes.bfloat16)
    return band, share, fhi, flo, same


def lag_rows(segments):
    shifts = np.arange(-MAXLAG, MAXLAG + 1)
    phase = (shifts[:, None] * np.arange(BINS)[None, :] % LENGTH) * (2.0 * np.pi / LENGTH)
    table = np.concatenate([np.cos(phase), -np.sin(phase)], axis=1) / np.sqrt(segments * BINS)
    table = np.concatenate([table, np.zeros((80 - LAGS, LENGTH))], axis=0).astype(np.float32)
    return np.concatenate(split(table), axis=0)


def dot(a, b):
    return jnp.dot(a, b, preferred_element_type=F32)


def dot_nt(a, b):
    return lax.dot_general(a, b, (((1,), (1,)), ((), ())), preferred_element_type=F32)


def halves(x):
    high = x.astype(BF)
    return high, (x - high.astype(F32)).astype(BF)


def inverse(y):
    r = pl.reciprocal(y, approx=True)
    return r * (2.0 - y * r)


def whiten_body(half, records, band, share, fhi, flo, same, white):
    del half
    parts = range(ROWS // SUB)
    xs = [records[0, pl.ds(k * SUB, SUB), :] for k in parts]
    levels = []
    for x in xs:
        ahi, alo = halves(jnp.abs(x))
        levels.append((dot(ahi, band[...]) + dot(alo, band[...])) * share[...])
    spectra = []
    for x, level in zip(xs, levels):
        nhi, nlo = halves(x * inverse(level + 1e-06))
        spectra.append(dot(nhi, fhi[...]) + dot(nlo, fhi[...]) + dot(nhi, flo[...]))
    for k in parts:
        re = spectra[k][:, :BINS]
        im = spectra[k][:, BINS:]
        power = dot((re * re + im * im).astype(BF), same[...])
        factor = lax.rsqrt(power + 1e-05)
        per = SUB // CHANS
        white[pl.ds(k * per, per), 0, :, :BINS] = (re * factor).astype(BF).reshape(per, CHANS, BINS)
        white[pl.ds(k * per, per), 0, :, BINS:] = (im * factor).astype(BF).reshape(per, CHANS, BINS)


def whiten(half, records, consts):
    segs = records.shape[0]
    steps = HALF * CHANS // ROWS
    per = ROWS // CHANS

    def whole(array):
        return pl.BlockSpec(array.shape, lambda s, i, h: (0, 0))

    return pl.pallas_call(
        whiten_body,
        grid_spec=pltpu.PrefetchScalarGridSpec(
            num_scalar_prefetch=1,
            grid=(segs, steps),
            in_specs=[pl.BlockSpec((1, ROWS, LENGTH), lambda s, i, h: (s, h[0] * steps + i, 0))]
            + [whole(c) for c in consts],
            out_specs=pl.BlockSpec((per, 1, CHANS, LENGTH), lambda s, i, h: (i, s, 0, 0)),
        ),
        out_shape=jax.ShapeDtypeStruct((HALF, segs, CHANS, LENGTH), BF),
        compiler_params=pltpu.CompilerParams(vmem_limit_bytes=57 * MIB),
        cost_estimate=pl.CostEstimate(
            flops=segs * HALF * CHANS * LENGTH * LENGTH * 11,
            bytes_accessed=segs * HALF * CHANS * LENGTH * 6,
            transcendentals=0,
        ),
        name="whiten",
    )(half, records, *consts)


def is_live(tab, s, p, d):
    row = jnp.where(p < HALF, p + HALF, p - HALF)
    base = jnp.where(p < HALF, 0, 4 * CHANS)
    return tab[base + jnp.bitwise_and(s - row // 2, 3) * CHANS + (row % 2) * REACH + d - 1] != 0


INTRA = [(p, d) for p in range(HALF, 12) for d in range(1, REACH + 1) if p + d < 12]
CROSSING = [(p, d) for p in range(HALF) for d in range(1, REACH + 1) if p + d >= HALF] + [
    (p, d) for p in range(HALF, GROUP) for d in range(1, REACH + 1) if p + d >= 12
]


def correlate_body(crossing, meta, codes, tab, *refs):
    s = meta[0]
    core = meta[1]
    if crossing:
        own_ext, own_int, got_ext, got_int = refs[:4]
        refs = refs[4:]
        sources = [(own_ext, 1 + core), (own_int, 2 - core), (got_ext, 3 * core), (got_int, 3 - 3 * core)]
    else:
        own_ext, own_int = refs[:2]
        refs = refs[2:]
        sources = [(own_ext, 1 + core), (own_int, 2 - core)]
    lag, keep, out1, out2, out3, slots, low, high, stk, pq, cnt = refs
    segs = low.shape[0]
    for k in range(4):
        cnt[k] = 0
    cnt[4] = -1

    def grab(dest, block):
        for ref, quad in sources:

            @pl.when(block // HALF == quad)
            def _(ref=ref):
                dest[...] = ref[block % HALF]

    def put(owner, entry, stack):
        n = cnt[owner]
        cnt[owner] = n + 1
        slots[entry] = n
        r = jnp.bitwise_and(owner - s, 3)
        stk[r, pl.ds(pl.multiple_of(n * BODY, BODY), BODY), :] = stack[:BODY]
        stk[r, pl.ds(SLOTS * BODY + n, 1), :] = stack[BODY:LAGS]

    def pair(p, d):
        q = p + d

        @pl.when(cnt[4] != p)
        def _():
            grab(low, p)
            cnt[4] = p

        grab(high, q)
        for chunk in range(CHANS // 16):
            rows = pl.ds(chunk * 16, 16)
            real = jnp.zeros((16, BINS), F32)
            imag = jnp.zeros((16, BINS), F32)
            for k in range(segs):
                are = low[k, rows, :BINS].astype(F32)
                aim = low[k, rows, BINS:].astype(F32)
                bre = high[k, rows, :BINS].astype(F32)
                bim = high[k, rows, BINS:].astype(F32)
                real += are * bre + aim * bim
                imag += are * bim - aim * bre
            rhi, rlo = halves(real)
            ihi, ilo = halves(imag)
            pq[0, rows, :BINS] = rhi
            pq[0, rows, BINS:] = ihi
            pq[1, rows, :BINS] = rlo
            pq[1, rows, BINS:] = ilo
        both = dot_nt(lag[...], pq[0])
        stack = both[:80] + both[80:] + dot_nt(lag[:80], pq[1])
        put(jnp.where(p < HALF, 2 + p // 2, (p - HALF) // 2), p * REACH + d - 1, stack)
        if crossing:
            @pl.when((p >= 6) & (p < 8) & (q >= 12) & (q < 14))
            def _():
                put(0, 96 + (p - 6) * 2 + q - 12, stack)

    def visit(n, carry):
        p = codes[n] // 16
        d = codes[n] % 16

        @pl.when(is_live(tab, s, p, d))
        def _():
            pair(p, d)

        return carry

    lax.fori_loop(0, len(CROSSING if crossing else INTRA), visit, 0)
    keep[...] = stk[0]
    out1[...] = stk[1].astype(BF)
    out2[...] = stk[2].astype(BF)
    out3[...] = stk[3].astype(BF)


SMEM = pl.BlockSpec(memory_space=pltpu.SMEM)
VMEM = pl.BlockSpec(memory_space=pltpu.VMEM)


def correlate(crossing, meta, tab, whites, lag):
    segs = whites[0].shape[1]
    chunk = jax.ShapeDtypeStruct((CHUNK, CHANS), BF)
    entries = CROSSING if crossing else INTRA
    codes = jnp.asarray(np.array([p * 16 + d for p, d in entries] + [0] * (64 - len(entries)), np.int32))
    block = segs * CHANS * LENGTH
    return pl.pallas_call(
        functools.partial(correlate_body, crossing),
        in_specs=[SMEM, SMEM, SMEM] + [VMEM] * (len(whites) + 1),
        out_specs=[VMEM, VMEM, VMEM, VMEM, SMEM],
        out_shape=[
            jax.ShapeDtypeStruct((CHUNK, CHANS), F32),
            chunk,
            chunk,
            chunk,
            jax.ShapeDtypeStruct((128,), jnp.int32),
        ],
        scratch_shapes=[
            pltpu.VMEM((segs, CHANS, LENGTH), BF),
            pltpu.VMEM((segs, CHANS, LENGTH), BF),
            pltpu.VMEM((4, CHUNK, CHANS), F32),
            pltpu.VMEM((2, CHANS, LENGTH), BF),
            pltpu.SMEM((8,), jnp.int32),
        ],
        compiler_params=pltpu.CompilerParams(vmem_limit_bytes=20 * MIB),
        cost_estimate=pl.CostEstimate(flops=8 * 10 * block, bytes_accessed=8 * block, transcendentals=0),
        name="correlate",
    )(meta, codes, tab, *whites, lag)


UPWARD = (
    ((0, 0), (1, 0), (1, 1), (2, 0), (2, 1), (3, 0), (3, 1)),
    ((2, 2), (3, 2), (3, 3)),
)


def combine_body(meta, tab, slots_in, slots_x, keep_in, in1, in2, in3, keep_x, x1, x2, x3, *refs):
    full_in, full_x, send2, out1, out2, out3, stage2, stage3 = refs
    s = meta[0]
    full_in[...] = (keep_in[...] + in1[...].astype(F32)) + (in2[...].astype(F32) + in3[...].astype(F32))
    full_x[...] = (keep_x[...] + x1[...].astype(F32)) + (x2[...].astype(F32) + x3[...].astype(F32))

    def move(full, n, dest, size, k):
        dest[pl.ds(k * BODY, BODY), :] = full[pl.ds(pl.multiple_of(n * BODY, BODY), BODY), :]
        dest[pl.ds(size * BODY + k, 1), :] = full[pl.ds(SLOTS * BODY + n, 1), :]

    @pl.when(s >= 2)
    def _():
        send2[...] = full_x[...].astype(BF)

    for owner in (0, 1):

        @pl.when(s == owner)
        def _(owner=owner):
            for k, (i, j) in enumerate(UPWARD[owner]):
                p, d = HALF + i, GROUP + j - i
                entry = p * REACH + d - 1 if i // 2 == owner else 96 + (i - 2) * 2 + j

                @pl.when(is_live(tab, s, jnp.int32(p), d))
                def _(entry=entry, k=k):
                    move(full_x, slots_x[entry], stage2, SLOTS, k)

            send2[...] = stage2[...].astype(BF)

    for r, out in ((1, out1), (2, out2), (3, out3)):
        to = jnp.bitwise_and(s + r, 3)
        for i in range(2):
            for j in range(2):
                row = 2 * s + i
                d = 2 * to + j - row

                @pl.when((s < to) & is_live(tab, s, HALF + row, d))
                def _(r=r, k=2 * i + j, row=row, d=d):
                    move(full_in, slots_in[(HALF + row) * REACH + d - 1], stage3.at[r - 1], 4, k)

                @pl.when((s > to) & (s >= 2) & is_live(tab, s, row - HALF, d + GROUP))
                def _(r=r, k=2 * i + j, row=row, d=d):
                    move(full_x, slots_x[(row - HALF) * REACH + d + GROUP - 1], stage3.at[r - 1], 4, k)

        out[...] = stage3[r - 1].astype(BF)


def combine(*args):
    third = jax.ShapeDtypeStruct((SEND, CHANS), BF)
    full = jax.ShapeDtypeStruct((CHUNK, CHANS), F32)
    return pl.pallas_call(
        combine_body,
        in_specs=[SMEM] * 4 + [VMEM] * 8,
        out_specs=[VMEM] * 6,
        out_shape=[full, full, jax.ShapeDtypeStruct((CHUNK, CHANS), BF), third, third, third],
        scratch_shapes=[
            pltpu.VMEM((CHUNK, CHANS), F32),
            pltpu.VMEM((3, SEND, CHANS), F32),
        ],
        compiler_params=pltpu.CompilerParams(vmem_limit_bytes=8 * MIB),
        name="combine",
    )(*args)


def finish_body(meta, tab, slots_in, slots_x, full_in, full_x, got2, got31, got32, got33, fwd, bwd, two, three):
    s = meta[0]
    two[...] = got2[...].astype(F32)
    three[0] = got31[...].astype(F32)
    three[1] = got32[...].astype(F32)
    three[2] = got33[...].astype(F32)
    fwd[...] = jnp.zeros(fwd.shape, F32)
    bwd[...] = jnp.zeros(bwd.shape, F32)

    def ahead(source, size, n, i, d):
        fwd[i, BODY, pl.ds(d - 1, 1), :] = source[pl.ds(size * BODY + n, 1), :]
        for m in range(BODY):
            fwd[i, m, pl.ds(d - 1, 1), :] = source[pl.ds(n * BODY + m, 1), :]

    def behind(source, size, n, j, d):
        bwd[j, 0, pl.ds(d - 1, 1), :] = source[pl.ds(size * BODY + n, 1), :]
        for m in range(BODY):
            bwd[j, BODY - m, pl.ds(d - 1, 1), :] = source[pl.ds(n * BODY + m, 1), :]

    from_above = jnp.int32(0)
    for i in range(2):
        for d in range(1, REACH + 1):
            row = 2 * s + i
            p = HALF + row
            entry = p * REACH + d - 1
            on = is_live(tab, s, p, d)
            crossed = row + d >= GROUP

            @pl.when(on & jnp.logical_not(crossed))
            def _(i=i, d=d, entry=entry):
                ahead(full_in, SLOTS, slots_in[entry], i, d)

            @pl.when(on & crossed & (s < 2))
            def _(i=i, d=d, entry=entry):
                ahead(full_x, SLOTS, slots_x[entry], i, d)

            @pl.when(on & crossed & (s >= 2))
            def _(i=i, d=d, n=from_above):
                ahead(two, SLOTS, n, i, d)

            from_above = from_above + jnp.where(on & crossed, 1, 0)

    for j in range(2):
        for d in range(1, REACH + 1):
            low = 2 * s + j - d
            p = HALF + low
            entry = p * REACH + d - 1
            on = is_live(tab, s, p, d)
            before = low < 0
            row = jnp.where(before, low + GROUP, low)
            owner = row // 2
            up = before & (owner < 2)
            mine = (owner == s) & jnp.logical_not(up)

            @pl.when(on & mine & jnp.logical_not(before))
            def _(j=j, d=d, entry=entry):
                behind(full_in, SLOTS, slots_in[entry], j, d)

            @pl.when(on & mine & before)
            def _(j=j, d=d, entry=entry):
                behind(full_x, SLOTS, slots_x[entry], j, d)

            @pl.when(on & up)
            def _(j=j, d=d, row=row):
                k0 = jnp.where(row == 0, 0, 2 * row - 1) + j
                k1 = jnp.where(row == 2, 0, 1) + j
                behind(two, SLOTS, jnp.where(s == 0, k0, k1), j, d)

            @pl.when(on & jnp.logical_not(mine) & jnp.logical_not(up))
            def _(j=j, d=d, row=row, owner=owner):
                r = jnp.bitwise_and(s - owner, 3)
                behind(three.at[r - 1], 4, (row - 2 * owner) * 2 + j, j, d)


def finish(blocks, *args):
    out = jax.ShapeDtypeStruct((blocks, LAGS, REACH, CHANS), F32)
    return pl.pallas_call(
        finish_body,
        in_specs=[SMEM] * 4 + [VMEM] * 6,
        out_specs=[VMEM, VMEM],
        out_shape=[out, out],
        scratch_shapes=[
            pltpu.VMEM((CHUNK, CHANS), F32),
            pltpu.VMEM((3, SEND, CHANS), F32),
        ],
        compiler_params=pltpu.CompilerParams(vmem_limit_bytes=8 * MIB),
        name="finish",
    )(*args)


def shards(groups, planes, consts, lag, records, pairs):
    b = lax.axis_index("blk").astype(jnp.int32)
    s = lax.axis_index("seg").astype(jnp.int32)
    core = jnp.bitwise_and(b, 1)
    meta = jnp.stack([s, core])

    def ring(x, r):
        return lax.ppermute(x, "seg", [(z, (z + r) % planes) for z in range(planes)])

    outer = [(g, (g + 1) % groups if g % 2 else (g - 1) % groups) for g in range(groups)]
    inner = [(g, g ^ 1) for g in range(groups)]
    upward = [(g, (g + 1) % groups) for g in range(groups)]
    own_ext = whiten(core[None], records, consts)
    got_ext = lax.ppermute(own_ext, "blk", outer)
    row, _ = lax.optimization_barrier((jnp.pad(pairs.reshape(-1), (0, CHANS - pairs.size)), own_ext))
    own_tab = jnp.concatenate([row, ring(row, 1), ring(row, 2), ring(row, 3)])
    tab = jnp.concatenate([lax.ppermute(own_tab, "blk", upward), own_tab])
    own_int = whiten((1 - core)[None], records, consts)
    got_int = lax.ppermute(own_int, "blk", inner)

    keep_in, in1, in2, in3, slots_in = correlate(
        False, meta, jnp.concatenate([own_tab, own_tab]), (own_ext, own_int), lag
    )
    in1, in2, in3 = ring(in1, 1), ring(in2, 2), ring(in3, 3)
    keep_x, x1, x2, x3, slots_x = correlate(True, meta, tab, (own_ext, own_int, got_ext, got_int), lag)
    x1, x2, x3 = ring(x1, 1), ring(x2, 2), ring(x3, 3)
    full_in, full_x, send2, s31, s32, s33 = combine(
        meta, tab, slots_in, slots_x, keep_in, in1, in2, in3, keep_x, x1, x2, x3
    )
    shift = [
        (z * groups + g, z * groups + (g + (1 if z < 2 else -1)) % groups)
        for z in range(planes)
        for g in range(groups)
    ]
    got2 = lax.ppermute(send2, ("seg", "blk"), shift)
    outs = finish(
        pairs.shape[0], meta, tab, slots_in, slots_x, full_in, full_x, got2, ring(s31, 1), ring(s32, 2), ring(s33, 3)
    )
    return tuple(jnp.transpose(out, (0, 2, 1, 3)) for out in outs)


def solution(mesh):
    groups = mesh.shape["blk"]
    planes = mesh.shape["seg"]
    consts = tables()

    def run(records, pairs):
        body = functools.partial(
            shards,
            groups,
            planes,
            tuple(jnp.asarray(c) for c in consts),
            jnp.asarray(lag_rows(records.shape[0])),
        )
        return jax.shard_map(
            body,
            mesh=mesh,
            in_specs=(P("seg", "blk", None), P(("blk", "seg"), None)),
            out_specs=(P(("blk", "seg"), None, None, None), P(("blk", "seg"), None, None, None)),
            check_vma=False,
        )(records, pairs)

    return run
```

time: 143 us -> 72.3 us (0.51)
  blocking collectives: 66.7 us -> 0 us
  Pallas kernels: 35.2 us -> 26.9 us
  starting transfers between devices: 16.7 us -> 24.1 us
  local copies, waits for them, and re-layouts: 8.65 us -> 1.57 us
  waiting for transfers between devices: 14.3 us -> 18.5 us
    unnamed x1 -> x0, blocking collectives: 66.7 us -> none
    ppermute x6 -> x12, starting transfers between devices: 12 us -> 19.2 us  [ring(): lax.ppermute(x, 'seg', [(z, (z + r) % planes) for z in range(planes)])]
    ppermute x0 -> x1, waiting for transfers between devices: none -> 6.28 us  [shards(): tab = jnp.concatenate([lax.ppermute(own_tab, 'blk', upward), own_tab])]
    pallas_call x2, Pallas kernels: 21 us -> 16.2 us  [whiten(): pl.pallas_call(whiten_body, grid_spec=pltpu.PrefetchScalarGridSpec(num_sc...]
    pallas_call x2 -> x0, local copies, waits for them, and re-layouts: 3.93 us -> none  [finish(): pl.pallas_call(finish_body, in_specs=[smem, smem, smem] + [vmem] * 5, out...]
    pallas_call x3 -> x4, Pallas kernels: 14.1 us -> 10.6 us  [the longest x2 6.75 us: correlate(): pl.pallas_call(functools.partial(correlate_body, crossing), in_specs=[SME...]
    unnamed x25 -> x22, local copies, waits for them, and re-layouts: 4.64 us -> 1.47 us
    ppermute x6 -> x12, waiting for transfers between devices: 14.2 us -> 11.6 us  [ring(): lax.ppermute(x, 'seg', [(z, (z + r) % planes) for z in range(planes)])]
  transfers between devices with their start and end apart: 9 -> 16, of which waited for: 5 -> 9; matrix products, arithmetic and copies ran while one was open for 1% -> 0% of each run, Pallas kernels for 7% -> 21%
where the time goes in v2:
time: 72.3 us; the launch traced here: 71.9 us
  Pallas kernels  26.9 us (37%)
  starting transfers between devices  24.1 us (33%)
  waiting for transfers between devices  18.5 us (26%)
  local copies, waits for them, and re-layouts  1.57 us (2%)
  between operations  0.82 us (1%)
    ppermute x12, starting transfers between devices, ring(): lax.ppermute(x, 'seg', [(z, (z + r) % planes) for z in range(planes)])  19.2 us
    pallas_call x2, Pallas kernels, whiten(): pl.pallas_call(whiten_body, grid_spec=pltpu.PrefetchScalarGridSpec(num_sc...  16.2 us
    ppermute x12, waiting for transfers between devices, ring(): lax.ppermute(x, 'seg', [(z, (z + r) % planes) for z in range(planes)])  11.6 us
    pallas_call x2, Pallas kernels, correlate(): pl.pallas_call(functools.partial(correlate_body, crossing), in_specs=[SME...  6.75 us
    ppermute x1, waiting for transfers between devices, shards(): tab = jnp.concatenate([lax.ppermute(own_tab, 'blk', upward), own_tab])  6.28 us
    ppermute x1, starting transfers between devices, shards(): got_ext = lax.ppermute(own_ext, 'blk', outer)  4.74 us
    pallas_call x1, Pallas kernels, finish(): pl.pallas_call(finish_body, in_specs=[SMEM] * 4 + [VMEM] * 6, out_specs=[...  2.73 us
    unnamed x22, local copies, waits for them, and re-layouts  1.47 us
  transfers between devices with their start and end apart: 16, of which 9 were waited for; matrix products, arithmetic and copies ran while one was open for 0% of the time, Pallas kernels for 21%

profile of v2, /device:TPU:0, one launch (start us, length us, event | category | flops | bytes accessed | tf_op | source)
XLA Modules:
  0.0 71.9 jit_solution(13197135823997165987)
XLA Ops:
  0.6 8.1 %whiten.2.refs_0_ = bf16[4,3,128,512]{3,2,1,0:T(8,128)(2,1)} custom-call(s32[1]{0:T(128)} %bitcast.1.half, f32[3,1024,512]{2,1,0:T(8,128)} %records.3, bf16[512,512]{1,0:T(8,128)(2,1)} %constant.29.clone.band, f32[1,512]{1,0:T(1,128)} %constant.30.clone.share, bf16[512,512]{1,0:T(8,128)(2,1)} %constant.31.clone.fhi, bf16[512,512]{1,0:T(8,128)(2,1)} %constant.32.clone.flo, ...), custom_call_target="tpu_custom_call" | custom-call | flops 4429185024 | bytes 4718592 | tf_op jit(solution)/shard_map/whiten/pallas_call | solution.py:108
  8.7 4.7 %collective-permute-start.4 = (bf16[4,3,128,512]{3,2,1,0:T(8,128)(2,1)}, bf16[4,3,128,512]{3,2,1,0:T(8,128)(2,1)S(1)}, u32[]{:S(2)}, u32[]{:S(2)}) collective-permute-start(bf16[4,3,128,512]{3,2,1,0:T(8,128)(2,1)} %whiten.2.refs_0_), channel_id=1, source_target_pairs={{0,31},{1,2},{2,1},{3,4},{4,3},{5,6},{6,5},{7,8},{8,7},{9,10},{10,... | collective-permute-start | bytes 4718600 | tf_op jit(solution)/shard_map/ppermute | solution.py:429
  13.4 0.0 copy-start.6
  13.4 0.0 copy-start
  13.4 0.0 copy-start.3
  13.4 0.0 copy-start.5
  13.5 8.2 %whiten.3.refs_1_ = bf16[4,3,128,512]{3,2,1,0:T(8,128)(2,1)} custom-call(s32[1]{0:T(128)} %bitcast.2.half, f32[3,1024,512]{2,1,0:T(8,128)} %records.3, bf16[512,512]{1,0:T(8,128)(2,1)} %constant.29.clone.band, f32[1,512]{1,0:T(1,128)} %constant.30.clone.share, bf16[512,512]{1,0:T(8,128)(2,1)} %constant.31.clone.fhi, bf16[512,512]{1,0:T(8,128)(2,1)} %constant.32.clone.flo, ...), custom_call_target="tpu_custom_call" | custom-call | flops 4429185024 | bytes 4718592 | tf_op jit(solution)/shard_map/whiten/pallas_call | solution.py:108
  21.6 0.0 collective-permute-start.5
  21.6 0.0 copy-done.6
  21.6 0.1 reshape.7
  21.7 1.9 %collective-permute-start = (s32[128]{0:T(128)S(1)}, s32[128]{0:T(128)S(1)}, u32[]{:S(2)}, u32[]{:S(2)}) collective-permute-start(s32[128]{0:T(128)S(1)} %pad.4), channel_id=1, source_target_pairs={{0,32},{32,64},{64,96},{96,0},{1,33},{33,65},{65,97},{97,1},{2,34}... | collective-permute-start | bytes 1544 | tf_op jit(solution)/shard_map/ppermute | solution.py:423
  23.6 3.6 %collective-permute-start.1 = (s32[128]{0:T(128)S(1)}, s32[128]{0:T(128)S(1)}, u32[]{:S(2)}, u32[]{:S(2)}) collective-permute-start(s32[128]{0:T(128)S(1)} %pad.4), channel_id=1, source_target_pairs={{0,64},{32,96},{64,0},{96,32},{1,65},{33,97},{65,1},{97,33},{2,66}... | collective-permute-start | bytes 1544 | tf_op jit(solution)/shard_map/ppermute | solution.py:423
  27.3 1.0 %collective-permute-start.2 = (s32[128]{0:T(128)S(1)}, s32[128]{0:T(128)S(1)}, u32[]{:S(2)}, u32[]{:S(2)}) collective-permute-start(s32[128]{0:T(128)S(1)} %pad.4), channel_id=1, source_target_pairs={{0,96},{32,0},{64,32},{96,64},{1,97},{33,1},{65,33},{97,65},{2,98}... | collective-permute-start | bytes 1544 | tf_op jit(solution)/shard_map/ppermute | solution.py:423
  28.2 0.1 pad_add_fusion.1.meta
  28.3 0.0 collective-permute-done
  28.3 0.4 collective-permute-done.1
  28.8 2.0 %collective-permute-done.2 = s32[128]{0:T(128)S(1)} collective-permute-done((s32[128]{0:T(128)S(1)}, s32[128]{0:T(128)S(1)}, u32[]{:S(2)}, u32[]{:S(2)}) %collective-permute-start.2) | collective-permute-done | bytes 544 | tf_op jit(solution)/shard_map/ppermute | solution.py:423
  30.8 0.1 collective-permute-start.3
  30.9 6.3 %collective-permute-done.3 = s32[512]{0:T(512)S(1)} collective-permute-done((s32[512]{0:T(512)S(1)}, s32[512]{0:T(512)S(1)}, u32[]{:S(2)}, u32[]{:S(2)}) %collective-permute-start.3) | collective-permute-done | bytes 2080 | tf_op jit(solution)/shard_map/ppermute | solution.py:432
  37.3 0.0 copy-done
  37.3 0.0 copy-done.3
  37.3 0.0 copy-done.5
  37.3 0.0 copy-start.1
  37.3 1.4 %copy-done.1 = bf16[4,3,128,512]{3,2,1,0:T(8,128)(2,1)S(1)} copy-done((bf16[4,3,128,512]{3,2,1,0:T(8,128)(2,1)S(1)}, bf16[4,3,128,512]{3,2,1,0:T(8,128)(2,1)}, u32[]{:S(2)}) %copy-start.1) | copy-done | bytes 1572888
  38.7 0.0 copy-start.2
  38.7 0.0 copy-start.4
  38.7 3.5 %correlate.2 = (f32[528,128]{1,0:T(8,128)S(1)}, bf16[528,128]{1,0:T(8,128)(2,1)S(1)}, bf16[528,128]{1,0:T(8,128)(2,1)S(1)}, bf16[528,128]{1,0:T(8,128)(2,1)S(1)}, s32[128]{0:T(128)S(1)}) custom-call(s32[2]{0:T(128)S(1)} %pad_add_fusion.1.meta, s32[64]{0:T(128)S(1)} %copy-done.5, s32[1024]{0:T(1024)S(1)} %get-tuple-element.40.tab, ...), custom_call_target="tpu_custom_call" | custom-call | flops 15728640 | bytes 1572864 | tf_op jit(solution)/shard_map/correlate/pallas_call | solution.py:233
  42.2 0.1 collective-permute-start.6
  42.3 3.6 %collective-permute-start.7 = (bf16[528,128]{1,0:T(8,128)(2,1)S(1)}, bf16[528,128]{1,0:T(8,128)(2,1)S(1)}, u32[]{:S(2)}, u32[]{:S(2)}) collective-permute-start(bf16[528,128]{1,0:T(8,128)(2,1)S(1)} %get-tuple-element.26), channel_id=1, source_target_pairs={{0,64},{32,96},{64,0},{96,32},{1,65},{33,97},{65,1},{97,33},{2,66}... | collective-permute-start | bytes 405512 | tf_op jit(solution)/shard_map/ppermute | solution.py:423
  45.9 0.5 collective-permute-start.8
  46.4 0.0 collective-permute-done.4.refs_2_
  46.4 0.0 collective-permute-done.5.refs_3_
  46.4 0.0 copy-done.2
  46.4 0.0 copy-done.4
  46.4 3.3 %correlate.3 = (f32[528,128]{1,0:T(8,128)S(1)}, bf16[528,128]{1,0:T(8,128)(2,1)S(1)}, bf16[528,128]{1,0:T(8,128)(2,1)S(1)}, bf16[528,128]{1,0:T(8,128)(2,1)S(1)}, s32[128]{0:T(128)S(1)}) custom-call(s32[2]{0:T(128)S(1)} %pad_add_fusion.1.meta, s32[64]{0:T(128)S(1)} %copy-done.4, s32[1024]{0:T(1024)S(1)} %get-tuple-element.41.tab, ...), custom_call_target="tpu_custom_call" | custom-call | flops 15728640 | bytes 1572864 | tf_op jit(solution)/shard_map/correlate/pallas_call | solution.py:233
  49.7 2.1 %collective-permute-start.10 = (bf16[528,128]{1,0:T(8,128)(2,1)S(1)}, bf16[528,128]{1,0:T(8,128)(2,1)S(1)}, u32[]{:S(2)}, u32[]{:S(2)}) collective-permute-start(bf16[528,128]{1,0:T(8,128)(2,1)S(1)} %get-tuple-element.30), channel_id=1, source_target_pairs={{0,64},{32,96},{64,0},{96,32},{1,65},{33,97},{65,1},{97,33},{2,66}... | collective-permute-start | bytes 405512 | tf_op jit(solution)/shard_map/ppermute | solution.py:423
  51.8 2.2 %collective-permute-start.11 = (bf16[528,128]{1,0:T(8,128)(2,1)S(1)}, bf16[528,128]{1,0:T(8,128)(2,1)S(1)}, u32[]{:S(2)}, u32[]{:S(2)}) collective-permute-start(bf16[528,128]{1,0:T(8,128)(2,1)S(1)} %get-tuple-element.31), channel_id=1, source_target_pairs={{0,96},{32,0},{64,32},{96,64},{1,97},{33,1},{65,33},{97,65},{2,98}... | collective-permute-start | bytes 405512 | tf_op jit(solution)/shard_map/ppermute | solution.py:423
  54.0 0.0 collective-permute-done.6.in1
  54.0 0.0 collective-permute-start.9
  54.0 0.0 collective-permute-done.7.in2
  54.0 0.0 collective-permute-done.8.in3
  54.0 2.6 %collective-permute-done.10.x2 = bf16[528,128]{1,0:T(8,128)(2,1)S(1)} collective-permute-done((bf16[528,128]{1,0:T(8,128)(2,1)S(1)}, bf16[528,128]{1,0:T(8,128)(2,1)S(1)}, u32[]{:S(2)}, u32[]{:S(2)}) %collective-permute-start.10) | collective-permute-done | bytes 135200 | tf_op jit(solution)/shard_map/ppermute | solution.py:423
  56.6 0.2 collective-permute-done.11.x3
  56.8 3.4 %collective-permute-done.9.x1 = bf16[528,128]{1,0:T(8,128)(2,1)S(1)} collective-permute-done((bf16[528,128]{1,0:T(8,128)(2,1)S(1)}, bf16[528,128]{1,0:T(8,128)(2,1)S(1)}, u32[]{:S(2)}, u32[]{:S(2)}) %collective-permute-start.9) | collective-permute-done | bytes 135200 | tf_op jit(solution)/shard_map/ppermute | solution.py:423
  60.2 1.1 %combine.1 = (f32[528,128]{1,0:T(8,128)S(1)}, f32[528,128]{1,0:T(8,128)S(1)}, bf16[528,128]{1,0:T(8,128)(2,1)S(1)}, bf16[272,128]{1,0:T(8,128)(2,1)S(1)}, bf16[2...) custom-call(s32[2]{0:T(128)S(1)} %pad_add_fusion.1.meta, s32[1024]{0:T(1024)S(1)} %get-tuple-element.41.tab, ...), custom_call_target="tpu_custom_call" | custom-call | tf_op jit(solution)/shard_map/combine/pallas_call | solution.py:312
  61.4 0.1 collective-permute-start.12
  61.4 0.1 collective-permute-start.13
  61.5 1.8 %collective-permute-start.14 = (bf16[272,128]{1,0:T(8,128)(2,1)S(1)}, bf16[272,128]{1,0:T(8,128)(2,1)S(1)}, u32[]{:S(2)}, u32[]{:S(2)}) collective-permute-start(bf16[272,128]{1,0:T(8,128)(2,1)S(1)} %get-tuple-element.36), channel_id=1, source_target_pairs={{0,64},{32,96},{64,0},{96,32},{1,65},{33,97},{65,1},{97,33},{2,66}... | collective-permute-start | bytes 208904 | tf_op jit(solution)/shard_map/ppermute | solution.py:423
  63.4 2.3 %collective-permute-start.15 = (bf16[272,128]{1,0:T(8,128)(2,1)S(1)}, bf16[272,128]{1,0:T(8,128)(2,1)S(1)}, u32[]{:S(2)}, u32[]{:S(2)}) collective-permute-start(bf16[272,128]{1,0:T(8,128)(2,1)S(1)} %get-tuple-element.37), channel_id=1, source_target_pairs={{0,96},{32,0},{64,32},{96,64},{1,97},{33,1},{65,33},{97,65},{2,98}... | collective-permute-start | bytes 208904 | tf_op jit(solution)/shard_map/ppermute | solution.py:423
  65.7 2.1 %collective-permute-done.13.got31 = bf16[272,128]{1,0:T(8,128)(2,1)S(1)} collective-permute-done((bf16[272,128]{1,0:T(8,128)(2,1)S(1)}, bf16[272,128]{1,0:T(8,128)(2,1)S(1)}, u32[]{:S(2)}, u32[]{:S(2)}) %collective-permute-start.13) | collective-permute-done | bytes 69664 | tf_op jit(solution)/shard_map/ppermute | solution.py:423
  67.8 0.0 collective-permute-done.14.got32
  67.8 0.9 %collective-permute-done.15.got33 = bf16[272,128]{1,0:T(8,128)(2,1)S(1)} collective-permute-done((bf16[272,128]{1,0:T(8,128)(2,1)S(1)}, bf16[272,128]{1,0:T(8,128)(2,1)S(1)}, u32[]{:S(2)}, u32[]{:S(2)}) %collective-permute-start.15) | collective-permute-done | bytes 69664 | tf_op jit(solution)/shard_map/ppermute | solution.py:423
  68.6 0.5 collective-permute-done.12.got2
  69.2 2.7 %finish.1 = (f32[2,65,8,128]{3,2,1,0:T(8,128)}, f32[2,65,8,128]{3,2,1,0:T(8,128)}) custom-call(s32[2]{0:T(128)S(1)} %pad_add_fusion.1.meta, s32[1024]{0:T(1024)S(1)} %get-tuple-element.41.tab, s32[128]{0:T(128)S(1)} %get-tuple-element.22.slots_in, s32[128]{0:T(128)S(1)} %get-tuple-element.23.slots_x, f32[528,128]{1,0:T(8,128)S(1)} %get-tuple-element.32.full_in, ...), custom_call_target="tpu_custom_call" | custom-call | tf_op jit(solution)/shard_map/finish/pallas_call | solution.py:402
  (13 shorter events, 0.1 us)
Async XLA Ops:
  8.7 37.7 %collective-permute-start.4 = (bf16[4,3,128,512]{3,2,1,0:T(8,128)(2,1)}, bf16[4,3,128,512]{3,2,1,0:T(8,128)(2,1)S(1)}, u32[]{:S(2)}, u32[]{:S(2)}) collective-permute-start(bf16[4,3,128,512]{3,2,1,0:T(8,128)(2,1)} %whiten.2.refs_0_), channel_id=1, source_target_pairs={{0,31},{1,2},{2,1},{3,4},{4,3},{5,6},{6,5},{7,8},{8,7},{9,10},{10,... | collective-permute-start | bytes 4718600 | tf_op jit(solution)/shard_map/ppermute | solution.py:429
  13.4 8.2 %copy-start.6 = (s32[2,8]{1,0:T(2,128)S(1)}, s32[2,8]{1,0:T(2,128)}, u32[]{:S(2)}) copy-start(s32[2,8]{1,0:T(2,128)} %param.11) | copy-start | bytes 196
  13.4 23.8 %copy-start = (bf16[4,3,128,512]{3,2,1,0:T(8,128)(2,1)S(1)}, bf16[4,3,128,512]{3,2,1,0:T(8,128)(2,1)}, u32[]{:S(2)}) copy-start(bf16[4,3,128,512]{3,2,1,0:T(8,128)(2,1)} %whiten.2.refs_0_) | copy-start | bytes 4718596
  13.4 23.8 %copy-start.3 = (bf16[160,512]{1,0:T(8,128)(2,1)S(1)}, bf16[160,512]{1,0:T(8,128)(2,1)}, u32[]{:S(2)}) copy-start(bf16[160,512]{1,0:T(8,128)(2,1)} %constant.35.clone.refs_2_.refs_4_) | copy-start | bytes 491524
  13.4 23.8 %copy-start.5 = (s32[64]{0:T(128)S(1)}, s32[64]{0:T(128)}, u32[]{:S(2)}) copy-start(s32[64]{0:T(128)} %constant.34.clone.codes) | copy-start | bytes 772
  21.6 24.8 %collective-permute-start.5 = (bf16[4,3,128,512]{3,2,1,0:T(8,128)(2,1)}, bf16[4,3,128,512]{3,2,1,0:T(8,128)(2,1)}, u32[]{:S(2)}, u32[]{:S(2)}) collective-permute-start(bf16[4,3,128,512]{3,2,1,0:T(8,128)(2,1)} %whiten.3.refs_1_), channel_id=1, source_target_pairs={{0,1},{1,0},{2,3},{3,2},{4,5},{5,4},{6,7},{7,6},{8,9},{9,8},{10,11... | collective-permute-start | bytes 4718600 | tf_op jit(solution)/shard_map/ppermute | solution.py:434
  21.7 6.6 %collective-permute-start = (s32[128]{0:T(128)S(1)}, s32[128]{0:T(128)S(1)}, u32[]{:S(2)}, u32[]{:S(2)}) collective-permute-start(s32[128]{0:T(128)S(1)} %pad.4), channel_id=1, source_target_pairs={{0,32},{32,64},{64,96},{96,0},{1,33},{33,65},{65,97},{97,1},{2,34}... | collective-permute-start | bytes 1544 | tf_op jit(solution)/shard_map/ppermute | solution.py:423
  23.6 5.1 %collective-permute-start.1 = (s32[128]{0:T(128)S(1)}, s32[128]{0:T(128)S(1)}, u32[]{:S(2)}, u32[]{:S(2)}) collective-permute-start(s32[128]{0:T(128)S(1)} %pad.4), channel_id=1, source_target_pairs={{0,64},{32,96},{64,0},{96,32},{1,65},{33,97},{65,1},{97,33},{2,66}... | collective-permute-start | bytes 1544 | tf_op jit(solution)/shard_map/ppermute | solution.py:423
  27.3 3.5 %collective-permute-start.2 = (s32[128]{0:T(128)S(1)}, s32[128]{0:T(128)S(1)}, u32[]{:S(2)}, u32[]{:S(2)}) collective-permute-start(s32[128]{0:T(128)S(1)} %pad.4), channel_id=1, source_target_pairs={{0,96},{32,0},{64,32},{96,64},{1,97},{33,1},{65,33},{97,65},{2,98}... | collective-permute-start | bytes 1544 | tf_op jit(solution)/shard_map/ppermute | solution.py:423
  30.8 6.4 %collective-permute-start.3 = (s32[512]{0:T(512)S(1)}, s32[512]{0:T(512)S(1)}, u32[]{:S(2)}, u32[]{:S(2)}) collective-permute-start(s32[512]{0:T(512)S(1)} %pad_add_fusion), channel_id=1, source_target_pairs={{0,1},{1,2},{2,3},{3,4},{4,5},{5,6},{6,7},{7,8},{8,9},{9,10},{10,1... | collective-permute-start | bytes 6152 | tf_op jit(solution)/shard_map/ppermute | solution.py:432
  37.3 1.4 %copy-start.1 = (bf16[4,3,128,512]{3,2,1,0:T(8,128)(2,1)S(1)}, bf16[4,3,128,512]{3,2,1,0:T(8,128)(2,1)}, u32[]{:S(2)}) copy-start(bf16[4,3,128,512]{3,2,1,0:T(8,128)(2,1)} %whiten.3.refs_1_) | copy-start | bytes 4718596
  38.7 7.7 %copy-start.2 = (bf16[4,3,128,512]{3,2,1,0:T(8,128)(2,1)S(1)}, bf16[4,3,128,512]{3,2,1,0:T(8,128)(2,1)}, u32[]{:S(2)}) copy-start(bf16[4,3,128,512]{3,2,1,0:T(8,128)(2,1)} %whiten.3.refs_1_) | copy-start | bytes 4718596
  38.7 7.7 %copy-start.4 = (s32[64]{0:T(128)S(1)}, s32[64]{0:T(128)}, u32[]{:S(2)}) copy-start(s32[64]{0:T(128)} %constant.36.clone.codes) | copy-start | bytes 772
  42.2 11.8 %collective-permute-start.6 = (bf16[528,128]{1,0:T(8,128)(2,1)S(1)}, bf16[528,128]{1,0:T(8,128)(2,1)S(1)}, u32[]{:S(2)}, u32[]{:S(2)}) collective-permute-start(bf16[528,128]{1,0:T(8,128)(2,1)S(1)} %get-tuple-element.25), channel_id=1, source_target_pairs={{0,32},{32,64},{64,96},{96,0},{1,33},{33,65},{65,97},{97,1},{2,34}... | collective-permute-start | bytes 405512 | tf_op jit(solution)/shard_map/ppermute | solution.py:423
  42.3 11.7 %collective-permute-start.7 = (bf16[528,128]{1,0:T(8,128)(2,1)S(1)}, bf16[528,128]{1,0:T(8,128)(2,1)S(1)}, u32[]{:S(2)}, u32[]{:S(2)}) collective-permute-start(bf16[528,128]{1,0:T(8,128)(2,1)S(1)} %get-tuple-element.26), channel_id=1, source_target_pairs={{0,64},{32,96},{64,0},{96,32},{1,65},{33,97},{65,1},{97,33},{2,66}... | collective-permute-start | bytes 405512 | tf_op jit(solution)/shard_map/ppermute | solution.py:423
  45.9 8.1 %collective-permute-start.8 = (bf16[528,128]{1,0:T(8,128)(2,1)S(1)}, bf16[528,128]{1,0:T(8,128)(2,1)S(1)}, u32[]{:S(2)}, u32[]{:S(2)}) collective-permute-start(bf16[528,128]{1,0:T(8,128)(2,1)S(1)} %get-tuple-element.27), channel_id=1, source_target_pairs={{0,96},{32,0},{64,32},{96,64},{1,97},{33,1},{65,33},{97,65},{2,98}... | collective-permute-start | bytes 405512 | tf_op jit(solution)/shard_map/ppermute | solution.py:423
  49.7 6.9 %collective-permute-start.10 = (bf16[528,128]{1,0:T(8,128)(2,1)S(1)}, bf16[528,128]{1,0:T(8,128)(2,1)S(1)}, u32[]{:S(2)}, u32[]{:S(2)}) collective-permute-start(bf16[528,128]{1,0:T(8,128)(2,1)S(1)} %get-tuple-element.30), channel_id=1, source_target_pairs={{0,64},{32,96},{64,0},{96,32},{1,65},{33,97},{65,1},{97,33},{2,66}... | collective-permute-start | bytes 405512 | tf_op jit(solution)/shard_map/ppermute | solution.py:423
  51.8 5.0 %collective-permute-start.11 = (bf16[528,128]{1,0:T(8,128)(2,1)S(1)}, bf16[528,128]{1,0:T(8,128)(2,1)S(1)}, u32[]{:S(2)}, u32[]{:S(2)}) collective-permute-start(bf16[528,128]{1,0:T(8,128)(2,1)S(1)} %get-tuple-element.31), channel_id=1, source_target_pairs={{0,96},{32,0},{64,32},{96,64},{1,97},{33,1},{65,33},{97,65},{2,98}... | collective-permute-start | bytes 405512 | tf_op jit(solution)/shard_map/ppermute | solution.py:423
  54.0 6.2 %collective-permute-start.9 = (bf16[528,128]{1,0:T(8,128)(2,1)S(1)}, bf16[528,128]{1,0:T(8,128)(2,1)S(1)}, u32[]{:S(2)}, u32[]{:S(2)}) collective-permute-start(bf16[528,128]{1,0:T(8,128)(2,1)S(1)} %get-tuple-element.29), channel_id=1, source_target_pairs={{0,32},{32,64},{64,96},{96,0},{1,33},{33,65},{65,97},{97,1},{2,34}... | collective-permute-start | bytes 405512 | tf_op jit(solution)/shard_map/ppermute | solution.py:423
  61.4 7.8 %collective-permute-start.12 = (bf16[528,128]{1,0:T(8,128)(2,1)S(1)}, bf16[528,128]{1,0:T(8,128)(2,1)S(1)}, u32[]{:S(2)}, u32[]{:S(2)}) collective-permute-start(bf16[528,128]{1,0:T(8,128)(2,1)S(1)} %get-tuple-element.34), channel_id=1, source_target_pairs={{0,1},{1,2},{2,3},{3,4},{4,5},{5,6},{6,7},{7,8},{8,9},{9,10},{10,1... | collective-permute-start | bytes 405512 | tf_op jit(solution)/shard_map/ppermute | solution.py:450
  61.4 6.3 %collective-permute-start.13 = (bf16[272,128]{1,0:T(8,128)(2,1)S(1)}, bf16[272,128]{1,0:T(8,128)(2,1)S(1)}, u32[]{:S(2)}, u32[]{:S(2)}) collective-permute-start(bf16[272,128]{1,0:T(8,128)(2,1)S(1)} %get-tuple-element.35), channel_id=1, source_target_pairs={{0,32},{32,64},{64,96},{96,0},{1,33},{33,65},{65,97},{97,1},{2,34}... | collective-permute-start | bytes 208904 | tf_op jit(solution)/shard_map/ppermute | solution.py:423
  61.5 6.3 %collective-permute-start.14 = (bf16[272,128]{1,0:T(8,128)(2,1)S(1)}, bf16[272,128]{1,0:T(8,128)(2,1)S(1)}, u32[]{:S(2)}, u32[]{:S(2)}) collective-permute-start(bf16[272,128]{1,0:T(8,128)(2,1)S(1)} %get-tuple-element.36), channel_id=1, source_target_pairs={{0,64},{32,96},{64,0},{96,32},{1,65},{33,97},{65,1},{97,33},{2,66}... | collective-permute-start | bytes 208904 | tf_op jit(solution)/shard_map/ppermute | solution.py:423
  63.4 5.3 %collective-permute-start.15 = (bf16[272,128]{1,0:T(8,128)(2,1)S(1)}, bf16[272,128]{1,0:T(8,128)(2,1)S(1)}, u32[]{:S(2)}, u32[]{:S(2)}) collective-permute-start(bf16[272,128]{1,0:T(8,128)(2,1)S(1)} %get-tuple-element.37), channel_id=1, source_target_pairs={{0,96},{32,0},{64,32},{96,64},{1,97},{33,1},{65,33},{97,65},{2,98}... | collective-permute-start | bytes 208904 | tf_op jit(solution)/shard_map/ppermute | solution.py:423

commit v3 on v2

v3 whole, which is shorter than its diff:
```python
import functools

import jax
import jax.numpy as jnp
import ml_dtypes
import numpy as np
from jax import lax
from jax.experimental import pallas as pl
from jax.experimental.pallas import tpu as pltpu
from jax.sharding import PartitionSpec as P

BINS = 256
LENGTH = 512
CHANS = 128
MAXLAG = 32
LAGS = 2 * MAXLAG + 1
REACH = 8
SMOOTH = 32
BAND = 64
GROUP = 8
HALF = GROUP // 2
BATCH = 2
SUB = BATCH * CHANS
REACHED = 384
SLOTS = 13
BODY = 64
CHUNK = SLOTS * BODY + 16
SHIFTED = 8
SEND2 = SHIFTED * BODY + 16
SEND3 = 4 * BODY + 16
MIB = 1024 * 1024
TINY = pl.CostEstimate(flops=1, bytes_accessed=1, transcendentals=0)
BF = jnp.bfloat16
F32 = jnp.float32


def split(array):
    high = array.astype(ml_dtypes.bfloat16)
    low = (array - high.astype(np.float32)).astype(ml_dtypes.bfloat16)
    return high, low


def tables():
    times = np.arange(LENGTH)
    inside = (np.abs(times[:, None] - times[None, :]) <= SMOOTH).astype(np.float32)
    share = (1.0 / inside.sum(0, keepdims=True)).astype(np.float32)
    first, second = inside[:REACHED, :BINS], inside[LENGTH - REACHED :, BINS:]
    first = np.concatenate([first, first], axis=0).astype(ml_dtypes.bfloat16)
    second = np.concatenate([second, second], axis=0).astype(ml_dtypes.bfloat16)
    phase = (times[:, None] * np.arange(BINS)[None, :] % LENGTH) * (2.0 * np.pi / LENGTH)
    fourier = np.concatenate([np.cos(phase), -np.sin(phase)], axis=1).astype(np.float32)
    fhi, flo = split(fourier)
    fourier = np.concatenate([fhi, fhi, flo], axis=0)
    which = np.arange(BINS) // BAND
    same = ((which[:, None] == which[None, :]) / (2.0 * BAND)).astype(ml_dtypes.bfloat16)
    return first, second, share, fourier, same


def lag_rows(segments):
    shifts = np.arange(-MAXLAG, MAXLAG + 1)
    phase = (shifts[:, None] * np.arange(BINS)[None, :] % LENGTH) * (2.0 * np.pi / LENGTH)
    table = np.concatenate([np.cos(phase), -np.sin(phase)], axis=1) / np.sqrt(segments * BINS)
    table = np.concatenate([table, np.zeros((CHANS - LAGS, LENGTH))], axis=0).T.astype(np.float32)
    return np.concatenate(split(table), axis=1)


def dot(a, b):
    return jnp.dot(a, b, preferred_element_type=F32)


def halves(x):
    high = x.astype(BF)
    return high, (x - high.astype(F32)).astype(BF)


def inverse(y):
    r = pl.reciprocal(y, approx=True)
    return r * (2.0 - y * r)


def whiten_body(start, records, first, second, share, fourier, same, *whites):
    del start
    parts = range(records.shape[1] // SUB)
    xs = [records[0, pl.ds(k * SUB, SUB), :] for k in parts]
    levels = []
    for x in xs:
        ahi, alo = halves(jnp.abs(x))
        left = dot(jnp.concatenate([ahi[:, :REACHED], alo[:, :REACHED]], axis=1), first[...])
        right = dot(jnp.concatenate([ahi[:, LENGTH - REACHED :], alo[:, LENGTH - REACHED :]], axis=1), second[...])
        levels.append(jnp.concatenate([left, right], axis=1) * share[...])
    spectra = []
    for x, level in zip(xs, levels):
        nhi, nlo = halves(x * inverse(level + 1e-06))
        spectra.append(dot(jnp.concatenate([nhi, nlo, nhi], axis=1), fourier[...]))
    for k in parts:
        re = spectra[k][:, :BINS]
        im = spectra[k][:, BINS:]
        power = dot((re * re + im * im).astype(BF), same[...])
        factor = lax.rsqrt(power + 1e-05)
        whites[k][:, 0, :, :BINS] = (re * factor).astype(BF).reshape(BATCH, CHANS, BINS)
        whites[k][:, 0, :, BINS:] = (im * factor).astype(BF).reshape(BATCH, CHANS, BINS)


def whiten(first_block, blocks, records, consts):
    segs = records.shape[0]
    rows = blocks * CHANS
    return pl.pallas_call(
        whiten_body,
        grid_spec=pltpu.PrefetchScalarGridSpec(
            num_scalar_prefetch=1,
            grid=(segs,),
            in_specs=[pl.BlockSpec((1, rows, LENGTH), lambda s, at: (s, at[0] // blocks, 0))]
            + [pl.BlockSpec(memory_space=pltpu.VMEM)] * len(consts),
            out_specs=[pl.BlockSpec((BATCH, 1, CHANS, LENGTH), lambda s, at: (0, s, 0, 0))] * (blocks // BATCH),
        ),
        out_shape=[jax.ShapeDtypeStruct((BATCH, segs, CHANS, LENGTH), BF)] * (blocks // BATCH),
        compiler_params=pltpu.CompilerParams(vmem_limit_bytes=56 * MIB),
        cost_estimate=TINY,
        name="whiten",
    )(first_block[None], records, *consts)


CODES, OWN, BEFORE = 64, CHANS, 5 * CHANS


def is_live(info, s, p, d):
    row = jnp.where(p < HALF, p + HALF, p - HALF)
    base = jnp.where(p < HALF, BEFORE, OWN)
    return info[base + jnp.bitwise_and(s - row // 2, 3) * CHANS + (row % 2) * REACH + d - 1] != 0


VISITS = [(p, d) for p in range(HALF) for d in range(1, REACH + 1) if p + d >= HALF] + [
    (p, d) for p in range(HALF, 12) for d in range(1, REACH + 1) if p < GROUP or p + d < 12
]


def correlate_body(info, *refs):
    s = info[0]
    core = info[1]
    ext = HALF * (1 + core)
    inner = HALF * (2 - core)
    got_ext = 3 * HALF * core
    got_inner = 3 * HALF * (1 - core)
    sources = [at + k for at in (ext, inner, got_ext, got_inner) for k in (0, BATCH)]
    whites = refs[: len(sources)]
    lag, keep, out1, out2, out3, slots, low, high, stk, pq, cnt = refs[len(sources) :]
    segs = low.shape[0]
    for k in range(4):
        cnt[k] = 0
    cnt[4] = -1

    def grab(dest, block):
        for ref, begin in zip(whites, sources):

            @pl.when((block >= begin) & (block < begin + BATCH))
            def _(ref=ref, begin=begin):
                dest[...] = ref[block - begin]

    def put(owner, entry, stack):
        n = cnt[owner]
        cnt[owner] = n + 1
        slots[entry] = n
        r = jnp.bitwise_and(owner - s, 3)
        stk[r, pl.ds(pl.multiple_of(n * BODY, BODY), BODY), :] = stack[:BODY]
        stk[r, pl.ds(SLOTS * BODY + n, 1), :] = stack[BODY:LAGS]

    def pair(p, d):
        q = p + d

        @pl.when(cnt[4] != p)
        def _():
            grab(low, p)
            cnt[4] = p

        grab(high, q)
        for chunk in range(CHANS // 16):
            rows = pl.ds(chunk * 16, 16)
            real = jnp.zeros((16, BINS), F32)
            imag = jnp.zeros((16, BINS), F32)
            for k in range(segs):
                are = low[k, rows, :BINS].astype(F32)
                aim = low[k, rows, BINS:].astype(F32)
                bre = high[k, rows, :BINS].astype(F32)
                bim = high[k, rows, BINS:].astype(F32)
                real += are * bre + aim * bim
                imag += are * bim - aim * bre
            rhi, rlo = halves(real)
            ihi, ilo = halves(imag)
            pq[0, rows, :BINS] = rhi
            pq[0, rows, BINS:] = ihi
            pq[1, rows, :BINS] = rlo
            pq[1, rows, BINS:] = ilo
        both = dot(pq[0], lag[...])
        stack = (both[:, :CHANS] + both[:, CHANS:] + dot(pq[1], lag[:, :CHANS])).T
        put(jnp.where(p < HALF, 2 + p // 2, (p - HALF) // 2), p * REACH + d - 1, stack)

        @pl.when((p >= 6) & (p < 8) & (q >= 12) & (q < 14))
        def _():
            put(0, 96 + (p - 6) * 2 + q - 12, stack)

    def visit(n, carry):
        code = info[CODES + n]
        p = jnp.right_shift(code, 4)
        d = jnp.bitwise_and(code, 15)

        @pl.when(is_live(info, s, p, d))
        def _():
            pair(p, d)

        return carry

    lax.fori_loop(0, len(VISITS), visit, 0)
    keep[...] = stk[0]
    out1[...] = stk[1].astype(BF)
    out2[...] = stk[2].astype(BF)
    out3[...] = stk[3].astype(BF)


SMEM = pl.BlockSpec(memory_space=pltpu.SMEM)
VMEM = pl.BlockSpec(memory_space=pltpu.VMEM)


def correlate(info, whites, lag):
    segs = whites[0].shape[1]
    chunk = jax.ShapeDtypeStruct((CHUNK, CHANS), BF)
    return pl.pallas_call(
        correlate_body,
        in_specs=[SMEM] + [VMEM] * (len(whites) + 1),
        out_specs=[VMEM, VMEM, VMEM, VMEM, SMEM],
        out_shape=[
            jax.ShapeDtypeStruct((CHUNK, CHANS), F32),
            chunk,
            chunk,
            chunk,
            jax.ShapeDtypeStruct((128,), jnp.int32),
        ],
        scratch_shapes=[
            pltpu.VMEM((segs, CHANS, LENGTH), BF),
            pltpu.VMEM((segs, CHANS, LENGTH), BF),
            pltpu.VMEM((4, CHUNK, CHANS), F32),
            pltpu.VMEM((2, CHANS, LENGTH), BF),
            pltpu.SMEM((8,), jnp.int32),
        ],
        compiler_params=pltpu.CompilerParams(vmem_limit_bytes=20 * MIB),
        cost_estimate=TINY,
        name="correlate",
    )(info, *whites, lag)


UPWARD = (
    ((0, 0), (1, 0), (1, 1), (2, 0), (2, 1), (3, 0), (3, 1)),
    ((2, 2), (3, 2), (3, 3)),
)


def combine_body(info, slots, keep, got1, got2, got3, full, send2, out1, out2, out3, stage2, stage3):
    s = info[0]
    full[...] = (keep[...] + got1[...].astype(F32)) + (got2[...].astype(F32) + got3[...].astype(F32))

    def move(n, dest, size, k):
        dest[pl.ds(k * BODY, BODY), :] = full[pl.ds(pl.multiple_of(n * BODY, BODY), BODY), :]
        dest[pl.ds(size * BODY + k, 1), :] = full[pl.ds(SLOTS * BODY + n, 1), :]

    @pl.when(s >= 2)
    def _():
        send2[: SHIFTED * BODY, :] = full[: SHIFTED * BODY, :].astype(BF)
        send2[SHIFTED * BODY :, :] = full[SLOTS * BODY :, :].astype(BF)

    for owner in (0, 1):

        @pl.when(s == owner)
        def _(owner=owner):
            for k, (i, j) in enumerate(UPWARD[owner]):
                p, d = HALF + i, GROUP + j - i
                entry = p * REACH + d - 1 if i // 2 == owner else 96 + (i - 2) * 2 + j

                @pl.when(is_live(info, s, jnp.int32(p), d))
                def _(entry=entry, k=k):
                    move(slots[entry], stage2, SHIFTED, k)

            send2[...] = stage2[...].astype(BF)

    for r, out in ((1, out1), (2, out2), (3, out3)):
        to = jnp.bitwise_and(s + r, 3)
        for i in range(2):
            for j in range(2):
                row = 2 * s + i
                d = 2 * to + j - row

                @pl.when((s < to) & is_live(info, s, HALF + row, d))
                def _(r=r, k=2 * i + j, row=row, d=d):
                    move(slots[(HALF + row) * REACH + d - 1], stage3.at[r - 1], 4, k)

                @pl.when((s > to) & (s >= 2) & is_live(info, s, row - HALF, d + GROUP))
                def _(r=r, k=2 * i + j, row=row, d=d):
                    move(slots[(row - HALF) * REACH + d + GROUP - 1], stage3.at[r - 1], 4, k)

        out[...] = stage3[r - 1].astype(BF)


def combine(*args):
    third = jax.ShapeDtypeStruct((SEND3, CHANS), BF)
    full = jax.ShapeDtypeStruct((CHUNK, CHANS), F32)
    return pl.pallas_call(
        combine_body,
        in_specs=[SMEM] * 2 + [VMEM] * 4,
        out_specs=[VMEM] * 5,
        out_shape=[full, jax.ShapeDtypeStruct((SEND2, CHANS), BF), third, third, third],
        scratch_shapes=[
            pltpu.VMEM((SEND2, CHANS), F32),
            pltpu.VMEM((3, SEND3, CHANS), F32),
        ],
        compiler_params=pltpu.CompilerParams(vmem_limit_bytes=8 * MIB),
        cost_estimate=TINY,
        name="combine",
    )(*args)


def finish_body(info, slots, full, got2, got31, got32, got33, fwd, bwd, two, three):
    s = info[0]
    two[...] = got2[...].astype(F32)
    three[0] = got31[...].astype(F32)
    three[1] = got32[...].astype(F32)
    three[2] = got33[...].astype(F32)
    fwd[...] = jnp.zeros(fwd.shape, F32)
    bwd[...] = jnp.zeros(bwd.shape, F32)

    def ahead(source, size, n, i, d):
        fwd[i, BODY, pl.ds(d - 1, 1), :] = source[pl.ds(size * BODY + n, 1), :]
        for m in range(BODY):
            fwd[i, m, pl.ds(d - 1, 1), :] = source[pl.ds(n * BODY + m, 1), :]

    def behind(source, size, n, j, d):
        bwd[j, 0, pl.ds(d - 1, 1), :] = source[pl.ds(size * BODY + n, 1), :]
        for m in range(BODY):
            bwd[j, BODY - m, pl.ds(d - 1, 1), :] = source[pl.ds(n * BODY + m, 1), :]

    from_above = jnp.int32(0)
    for i in range(2):
        for d in range(1, REACH + 1):
            row = 2 * s + i
            p = HALF + row
            entry = p * REACH + d - 1
            on = is_live(info, s, p, d)
            crossed = row + d >= GROUP

            @pl.when(on)
            def _(i=i, d=d, entry=entry, crossed=crossed, n=from_above):
                @pl.when(jnp.logical_not(crossed) | (s < 2))
                def _():
                    ahead(full, SLOTS, slots[entry], i, d)

                @pl.when(crossed & (s >= 2))
                def _():
                    ahead(two, SHIFTED, n, i, d)

            from_above = from_above + jnp.where(on & crossed, 1, 0)

    for j in range(2):
        for d in range(1, REACH + 1):
            low = 2 * s + j - d
            p = HALF + low

            @pl.when(is_live(info, s, p, d))
            def _(j=j, d=d, low=low, p=p):
                entry = p * REACH + d - 1
                before = low < 0
                row = jnp.where(before, low + GROUP, low)
                owner = row // 2
                up = before & (owner < 2)
                mine = (owner == s) & jnp.logical_not(up)

                @pl.when(mine)
                def _():
                    behind(full, SLOTS, slots[entry], j, d)

                @pl.when(up)
                def _():
                    k0 = jnp.where(row == 0, 0, 2 * row - 1) + j
                    k1 = jnp.where(row == 2, 0, 1) + j
                    behind(two, SHIFTED, jnp.where(s == 0, k0, k1), j, d)

                @pl.when(jnp.logical_not(mine) & jnp.logical_not(up))
                def _():
                    r = jnp.bitwise_and(s - owner, 3)
                    behind(three.at[r - 1], 4, (row - 2 * owner) * 2 + j, j, d)


def finish(blocks, *args):
    out = jax.ShapeDtypeStruct((blocks, LAGS, REACH, CHANS), F32)
    return pl.pallas_call(
        finish_body,
        in_specs=[SMEM] * 2 + [VMEM] * 5,
        out_specs=[VMEM, VMEM],
        out_shape=[out, out],
        scratch_shapes=[
            pltpu.VMEM((SEND2, CHANS), F32),
            pltpu.VMEM((3, SEND3, CHANS), F32),
        ],
        compiler_params=pltpu.CompilerParams(vmem_limit_bytes=8 * MIB),
        cost_estimate=TINY,
        name="finish",
    )(*args)


def shards(groups, planes, consts, lag, records, pairs):
    b = lax.axis_index("blk").astype(jnp.int32)
    s = lax.axis_index("seg").astype(jnp.int32)
    core = jnp.bitwise_and(b, 1)
    codes = np.array([p * 16 + d for p, d in VISITS], np.int32)
    place = jnp.concatenate([jnp.stack([s, core]), jnp.zeros((CODES - 2,), jnp.int32), jnp.asarray(codes)])

    def ring(x, r):
        return lax.ppermute(x, "seg", [(z, (z + r) % planes) for z in range(planes)])

    outer = [(g, g + 1 if g % 2 else g - 1) for g in range(1, groups - 1)]
    inner = [(g, g ^ 1) for g in range(groups)]
    upward = [(g, g + 1) for g in range(groups - 1)]
    shift = [
        (z * groups + g, z * groups + g + step)
        for z in range(planes)
        for g in range(groups)
        for step in (1 if z < 2 else -1,)
        if 0 <= g + step < groups
    ]

    (ext1,) = whiten(core * HALF, BATCH, records, consts)
    got1 = lax.ppermute(ext1, "blk", outer)
    (ext2,) = whiten(core * HALF + BATCH, BATCH, records, consts)
    got2 = lax.ppermute(ext2, "blk", outer)
    row, _ = lax.optimization_barrier((jnp.pad(pairs.reshape(-1), (0, CHANS - pairs.size)), ext2))
    own = jnp.concatenate([place, row, ring(row, 1), ring(row, 2), ring(row, 3)])
    start, own, _ = lax.optimization_barrier(((1 - core) * HALF, own, ext2))
    in1, in2 = whiten(start, HALF, records, consts)
    info = jnp.concatenate([own, lax.ppermute(own[OWN:], "blk", upward)])
    got3, got4 = lax.ppermute(in1, "blk", inner), lax.ppermute(in2, "blk", inner)

    whites = (ext1, ext2, in1, in2, got1, got2, got3, got4)
    keep, out1, out2, out3, slots = correlate(info, whites, lag)
    full, send2, s31, s32, s33 = combine(info, slots, keep, ring(out1, 1), ring(out2, 2), ring(out3, 3))
    shifted = lax.ppermute(send2, ("seg", "blk"), shift)
    outs = finish(pairs.shape[0], info, slots, full, shifted, ring(s31, 1), ring(s32, 2), ring(s33, 3))
    return tuple(jnp.transpose(out, (0, 2, 1, 3)) for out in outs)


def solution(mesh):
    groups = mesh.shape["blk"]
    planes = mesh.shape["seg"]
    consts = tables()

    def run(records, pairs):
        body = functools.partial(
            shards,
            groups,
            planes,
            tuple(jnp.asarray(c) for c in consts),
            jnp.asarray(lag_rows(records.shape[0])),
        )
        return jax.shard_map(
            body,
            mesh=mesh,
            in_specs=(P("seg", "blk", None), P(("blk", "seg"), None)),
            out_specs=(P(("blk", "seg"), None, None, None), P(("blk", "seg"), None, None, None)),
            check_vma=False,
        )(records, pairs)

    return run
```

time: 72.3 us -> 79.3 us (1.097)
  the two profiles are of different devices: /device:TPU:0 before, /device:TPU:6 now
where the time goes in v3:
time: 79.3 us; the launch traced here: 79 us
  Pallas kernels  30.2 us (38%)
  starting transfers between devices  29.8 us (38%)
  waiting for transfers between devices  15 us (19%)
  local copies, waits for them, and re-layouts  3.13 us (4%)
  between operations  0.82 us (1%)
    pallas_call x3, Pallas kernels, whiten(): pl.pallas_call(whiten_body, grid_spec=pltpu.PrefetchScalarGridSpec(num_sc...  18.9 us
    ppermute x9, starting transfers between devices, ring(): lax.ppermute(x, 'seg', [(z, (z + r) % planes) for z in range(planes)])  17.7 us
    ppermute x9, waiting for transfers between devices, ring(): lax.ppermute(x, 'seg', [(z, (z + r) % planes) for z in range(planes)])  9.93 us
    pallas_call x1, Pallas kernels, correlate(): pl.pallas_call(correlate_body, in_specs=[SMEM] + [VMEM] * (len(whites) +...  7.92 us
    ppermute x1, waiting for transfers between devices, shards(): info = jnp.concatenate([own, lax.ppermute(own[OWN:], 'blk', upward)])  5.03 us
    ppermute x1, starting transfers between devices, shards(): got1 = lax.ppermute(ext1, 'blk', outer)  4.02 us
    ppermute x1, starting transfers between devices, shards(): got2 = lax.ppermute(ext2, 'blk', outer)  3.78 us
    unnamed x13, local copies, waits for them, and re-layouts  2.28 us
  transfers between devices with their start and end apart: 15, of which 7 were waited for; matrix products, arithmetic and copies ran while one was open for 0% of the time, Pallas kernels for 17%

profile of v3, /device:TPU:6, one launch (start us, length us, event | category | flops | bytes accessed | tf_op | source)
XLA Modules:
  0.0 79.0 jit_solution(10784567587476406294)
XLA Ops:
  0.6 0.8 reshape.7
  1.4 5.6 %whiten.3.refs_1_ = bf16[2,3,128,512]{3,2,1,0:T(8,128)(2,1)} custom-call(s32[1]{0:T(128)} %bitcast.2.start, f32[3,1024,512]{2,1,0:T(8,128)} %records.5, bf16[768,256]{1,0:T(8,128)(2,1)} %constant.33.clone.first, bf16[768,256]{1,0:T(8,128)(2,1)} %constant.34.clone.second, f32[1,512]{1,0:T(1,128)} %constant.35.clone.share, ...), custom_call_target="tpu_custom_call" | custom-call | flops 1 | bytes 1 | tf_op jit(solution)/shard_map/whiten/pallas_call | solution.py:107
  7.0 0.0 copy-start.5
  7.0 4.0 %collective-permute-start.2 = (s32[128]{0:T(128)S(1)}, s32[128]{0:T(128)S(1)}, u32[]{:S(2)}, u32[]{:S(2)}) collective-permute-start(s32[128]{0:T(128)S(1)} %pad.4), channel_id=1, source_target_pairs={{0,96},{32,0},{64,32},{96,64},{1,97},{33,1},{65,33},{97,65},{2,98}... | collective-permute-start | bytes 1544 | tf_op jit(solution)/shard_map/ppermute | solution.py:414
  11.0 0.0 collective-permute-start.1
  11.0 1.3 %collective-permute-start = (s32[128]{0:T(128)S(1)}, s32[128]{0:T(128)S(1)}, u32[]{:S(2)}, u32[]{:S(2)}) collective-permute-start(s32[128]{0:T(128)S(1)} %pad.4), channel_id=1, source_target_pairs={{0,32},{32,64},{64,96},{96,0},{1,33},{33,65},{65,97},{97,1},{2,34}... | collective-permute-start | bytes 1544 | tf_op jit(solution)/shard_map/ppermute | solution.py:414
  12.3 3.8 %collective-permute-start.5 = (bf16[2,3,128,512]{3,2,1,0:T(8,128)(2,1)}, bf16[2,3,128,512]{3,2,1,0:T(8,128)(2,1)S(1)}, u32[]{:S(2)}, u32[]{:S(2)}) collective-permute-start(bf16[2,3,128,512]{3,2,1,0:T(8,128)(2,1)} %whiten.3.refs_1_), channel_id=1, source_target_pairs={{1,2},{2,1},{3,4},{4,3},{5,6},{6,5},{7,8},{8,7},{9,10},{10,9},{11,... | collective-permute-start | bytes 2359304 | tf_op jit(solution)/shard_map/ppermute | solution.py:430
  16.1 5.6 %whiten.4.refs_0_ = bf16[2,3,128,512]{3,2,1,0:T(8,128)(2,1)} custom-call(s32[1]{0:T(128)} %bitcast.3.start, f32[3,1024,512]{2,1,0:T(8,128)} %records.5, bf16[768,256]{1,0:T(8,128)(2,1)} %constant.33.clone.first, bf16[768,256]{1,0:T(8,128)(2,1)} %constant.34.clone.second, f32[1,512]{1,0:T(1,128)} %constant.35.clone.share, ...), custom_call_target="tpu_custom_call" | custom-call | flops 1 | bytes 1 | tf_op jit(solution)/shard_map/whiten/pallas_call | solution.py:107
  21.7 0.0 copy-start
  21.7 0.0 copy-start.1
  21.7 0.0 copy-start.4
  21.7 4.0 %collective-permute-start.4 = (bf16[2,3,128,512]{3,2,1,0:T(8,128)(2,1)}, bf16[2,3,128,512]{3,2,1,0:T(8,128)(2,1)S(1)}, u32[]{:S(2)}, u32[]{:S(2)}) collective-permute-start(bf16[2,3,128,512]{3,2,1,0:T(8,128)(2,1)} %whiten.4.refs_0_), channel_id=1, source_target_pairs={{1,2},{2,1},{3,4},{4,3},{5,6},{6,5},{7,8},{8,7},{9,10},{10,9},{11,... | collective-permute-start | bytes 2359304 | tf_op jit(solution)/shard_map/ppermute | solution.py:428
  25.7 0.0 collective-permute-done.2
  25.7 0.0 collective-permute-done.1
  25.8 0.0 collective-permute-done
  25.8 0.0 copy-done.5
  25.8 0.1 concatenate.6
  25.9 7.7 %whiten.5 = (bf16[2,3,128,512]{3,2,1,0:T(8,128)(2,1)}, bf16[2,3,128,512]{3,2,1,0:T(8,128)(2,1)}) custom-call(s32[1]{0:T(128)} %bitcast.4.start, f32[3,1024,512]{2,1,0:T(8,128)} %records.5, bf16[768,256]{1,0:T(8,128)(2,1)} %constant.33.clone.first, bf16[768,256]{1,0:T(8,128)(2,1)} %constant.34.clone.second, f32[1,512]{1,0:T(1,128)} %constant.35.clone.share, ...), custom_call_target="tpu_custom_call" | custom-call | flops 1 | bytes 1 | tf_op jit(solution)/shard_map/whiten/pallas_call | solution.py:107
  33.6 0.0 collective-permute-start.6
  33.6 0.5 collective-permute-start.7
  34.1 1.9 %collective-permute-start.3 = (s32[512]{0:T(512)S(1)}, s32[512]{0:T(512)S(1)}, u32[]{:S(2)}, u32[]{:S(2)}) collective-permute-start(s32[512]{0:T(512)S(1)} %slice.3), channel_id=1, source_target_pairs={{0,1},{1,2},{2,3},{3,4},{4,5},{5,6},{6,7},{7,8},{8,9},{9,10},{10,1... | collective-permute-start | bytes 6152 | tf_op jit(solution)/shard_map/ppermute | solution.py:435
  36.1 5.0 %collective-permute-done.3 = s32[512]{0:T(512)S(1)} collective-permute-done((s32[512]{0:T(512)S(1)}, s32[512]{0:T(512)S(1)}, u32[]{:S(2)}, u32[]{:S(2)}) %collective-permute-start.3) | collective-permute-done | bytes 2080 | tf_op jit(solution)/shard_map/ppermute | solution.py:435
  41.1 0.0 collective-permute-done.4.refs_4_
  41.1 0.0 collective-permute-done.5.refs_5_
  41.1 0.0 collective-permute-done.6.refs_6_
  41.1 0.0 collective-permute-done.7.refs_7_
  41.1 0.0 copy-done
  41.1 0.0 copy-done.1
  41.2 0.0 copy-done.4
  41.2 0.0 copy-start.2
  41.2 1.1 %copy-done.2 = bf16[2,3,128,512]{3,2,1,0:T(8,128)(2,1)S(1)} copy-done((bf16[2,3,128,512]{3,2,1,0:T(8,128)(2,1)S(1)}, bf16[2,3,128,512]{3,2,1,0:T(8,128)(2,1)}, u32[]{:S(2)}) %copy-start.2) | copy-done | bytes 786456
  42.3 0.0 copy-start.3
  42.3 1.1 %copy-done.3 = bf16[2,3,128,512]{3,2,1,0:T(8,128)(2,1)S(1)} copy-done((bf16[2,3,128,512]{3,2,1,0:T(8,128)(2,1)S(1)}, bf16[2,3,128,512]{3,2,1,0:T(8,128)(2,1)}, u32[]{:S(2)}) %copy-start.3) | copy-done | bytes 786456
  43.4 7.9 %correlate.1 = (f32[848,128]{1,0:T(8,128)S(1)}, bf16[848,128]{1,0:T(8,128)(2,1)S(1)}, bf16[848,128]{1,0:T(8,128)(2,1)S(1)}, bf16[848,128]{1,0:T(8,128)(2,1)S(1)}, s32[128]{0:T(128)S(1)}) custom-call(s32[1152]{0:T(1024)S(1)} %constant_dynamic-update-slice_fusion.info, bf16[2,3,128,512]{3,2,1,0:T(8,128)(2,1)S(1)} %copy-done.1, ...), custom_call_target="tpu_custom_call" | custom-call | flops 1 | bytes 1 | tf_op jit(solution)/shard_map/correlate/pallas_call | solution.py:226
  51.4 2.3 %collective-permute-start.8 = (bf16[848,128]{1,0:T(8,128)(2,1)S(1)}, bf16[848,128]{1,0:T(8,128)(2,1)S(1)}, u32[]{:S(2)}, u32[]{:S(2)}) collective-permute-start(bf16[848,128]{1,0:T(8,128)(2,1)S(1)} %get-tuple-element.26), channel_id=1, source_target_pairs={{0,32},{32,64},{64,96},{96,0},{1,33},{33,65},{65,97},{97,1},{2,34}... | collective-permute-start | bytes 651272 | tf_op jit(solution)/shard_map/ppermute | solution.py:414
  53.7 1.2 %collective-permute-start.9 = (bf16[848,128]{1,0:T(8,128)(2,1)S(1)}, bf16[848,128]{1,0:T(8,128)(2,1)S(1)}, u32[]{:S(2)}, u32[]{:S(2)}) collective-permute-start(bf16[848,128]{1,0:T(8,128)(2,1)S(1)} %get-tuple-element.27), channel_id=1, source_target_pairs={{0,64},{32,96},{64,0},{96,32},{1,65},{33,97},{65,1},{97,33},{2,66}... | collective-permute-start | bytes 651272 | tf_op jit(solution)/shard_map/ppermute | solution.py:414
  54.9 1.6 %collective-permute-start.10 = (bf16[848,128]{1,0:T(8,128)(2,1)S(1)}, bf16[848,128]{1,0:T(8,128)(2,1)S(1)}, u32[]{:S(2)}, u32[]{:S(2)}) collective-permute-start(bf16[848,128]{1,0:T(8,128)(2,1)S(1)} %get-tuple-element.28), channel_id=1, source_target_pairs={{0,96},{32,0},{64,32},{96,64},{1,97},{33,1},{65,33},{97,65},{2,98}... | collective-permute-start | bytes 651272 | tf_op jit(solution)/shard_map/ppermute | solution.py:414
  56.4 3.7 %collective-permute-done.8.got1 = bf16[848,128]{1,0:T(8,128)(2,1)S(1)} collective-permute-done((bf16[848,128]{1,0:T(8,128)(2,1)S(1)}, bf16[848,128]{1,0:T(8,128)(2,1)S(1)}, u32[]{:S(2)}, u32[]{:S(2)}) %collective-permute-start.8) | collective-permute-done | bytes 217120 | tf_op jit(solution)/shard_map/ppermute | solution.py:414
  60.2 2.3 %collective-permute-done.9.got2 = bf16[848,128]{1,0:T(8,128)(2,1)S(1)} collective-permute-done((bf16[848,128]{1,0:T(8,128)(2,1)S(1)}, bf16[848,128]{1,0:T(8,128)(2,1)S(1)}, u32[]{:S(2)}, u32[]{:S(2)}) %collective-permute-start.9) | collective-permute-done | bytes 217120 | tf_op jit(solution)/shard_map/ppermute | solution.py:414
  62.5 0.4 collective-permute-done.10.got3
  62.9 1.1 %combine.1 = (f32[848,128]{1,0:T(8,128)S(1)}, bf16[528,128]{1,0:T(8,128)(2,1)S(1)}, bf16[272,128]{1,0:T(8,128)(2,1)S(1)}, bf16[272,128]{1,0:T(8,128)(2,1)S(1)}, bf16[272,128]{1,0:T(8,128)(2,1)S(1)}) custom-call(s32[1152]{0:T(1024)S(1)} %constant_dynamic-update-slice_fusion.info, s32[128]{0:T(128)S(1)} %get-tuple-element.24.slots, ...), custom_call_target="tpu_custom_call" | custom-call | flops 1 | bytes 1 | tf_op jit(solution)/shard_map/combine/pallas_call | solution.py:304
  64.0 1.9 %collective-permute-start.11 = (bf16[528,128]{1,0:T(8,128)(2,1)S(1)}, bf16[528,128]{1,0:T(8,128)(2,1)S(1)}, u32[]{:S(2)}, u32[]{:S(2)}) collective-permute-start(bf16[528,128]{1,0:T(8,128)(2,1)S(1)} %get-tuple-element.30), channel_id=1, source_target_pairs={{0,1},{1,2},{2,3},{3,4},{4,5},{5,6},{6,7},{7,8},{8,9},{9,10},{10,1... | collective-permute-start | bytes 405512 | tf_op jit(solution)/shard_map/ppermute | solution.py:441
  66.0 1.7 %collective-permute-start.12 = (bf16[272,128]{1,0:T(8,128)(2,1)S(1)}, bf16[272,128]{1,0:T(8,128)(2,1)S(1)}, u32[]{:S(2)}, u32[]{:S(2)}) collective-permute-start(bf16[272,128]{1,0:T(8,128)(2,1)S(1)} %get-tuple-element.31), channel_id=1, source_target_pairs={{0,32},{32,64},{64,96},{96,0},{1,33},{33,65},{65,97},{97,1},{2,34}... | collective-permute-start | bytes 208904 | tf_op jit(solution)/shard_map/ppermute | solution.py:414
  67.7 4.7 %collective-permute-start.13 = (bf16[272,128]{1,0:T(8,128)(2,1)S(1)}, bf16[272,128]{1,0:T(8,128)(2,1)S(1)}, u32[]{:S(2)}, u32[]{:S(2)}) collective-permute-start(bf16[272,128]{1,0:T(8,128)(2,1)S(1)} %get-tuple-element.32), channel_id=1, source_target_pairs={{0,64},{32,96},{64,0},{96,32},{1,65},{33,97},{65,1},{97,33},{2,66}... | collective-permute-start | bytes 208904 | tf_op jit(solution)/shard_map/ppermute | solution.py:414
  72.4 0.9 %collective-permute-start.14 = (bf16[272,128]{1,0:T(8,128)(2,1)S(1)}, bf16[272,128]{1,0:T(8,128)(2,1)S(1)}, u32[]{:S(2)}, u32[]{:S(2)}) collective-permute-start(bf16[272,128]{1,0:T(8,128)(2,1)S(1)} %get-tuple-element.33), channel_id=1, source_target_pairs={{0,96},{32,0},{64,32},{96,64},{1,97},{33,1},{65,33},{97,65},{2,98}... | collective-permute-start | bytes 208904 | tf_op jit(solution)/shard_map/ppermute | solution.py:414
  73.2 0.1 collective-permute-done.12.got31
  73.4 2.1 %collective-permute-done.13.got32 = bf16[272,128]{1,0:T(8,128)(2,1)S(1)} collective-permute-done((bf16[272,128]{1,0:T(8,128)(2,1)S(1)}, bf16[272,128]{1,0:T(8,128)(2,1)S(1)}, u32[]{:S(2)}, u32[]{:S(2)}) %collective-permute-start.13) | collective-permute-done | bytes 69664 | tf_op jit(solution)/shard_map/ppermute | solution.py:414
  75.4 1.3 %collective-permute-done.14.got33 = bf16[272,128]{1,0:T(8,128)(2,1)S(1)} collective-permute-done((bf16[272,128]{1,0:T(8,128)(2,1)S(1)}, bf16[272,128]{1,0:T(8,128)(2,1)S(1)}, u32[]{:S(2)}, u32[]{:S(2)}) %collective-permute-start.14) | collective-permute-done | bytes 69664 | tf_op jit(solution)/shard_map/ppermute | solution.py:414
  76.7 0.0 collective-permute-done.11.got2
  76.7 2.2 %finish.1 = (f32[2,65,8,128]{3,2,1,0:T(8,128)}, f32[2,65,8,128]{3,2,1,0:T(8,128)}) custom-call(s32[1152]{0:T(1024)S(1)} %constant_dynamic-update-slice_fusion.info, s32[128]{0:T(128)S(1)} %get-tuple-element.24.slots, f32[848,128]{1,0:T(8,128)S(1)} %get-tuple-element.29.full, bf16[528,128]{1,0:T(8,128)(2,1)S(1)} %collective-permute-done.11.got2, ...), custom_call_target="tpu_custom_call" | custom-call | flops 1 | bytes 1 | tf_op jit(solution)/shard_map/finish/pallas_call | solution.py:391
  (6 shorter events, 0.0 us)
Async XLA Ops:
  7.0 18.8 %copy-start.5 = (s32[64]{0:T(128)S(1)}, s32[64]{0:T(128)}, u32[]{:S(2)}) copy-start(s32[64]{0:T(128)} %constant.32.clone) | copy-start | bytes 772
  7.0 18.7 %collective-permute-start.2 = (s32[128]{0:T(128)S(1)}, s32[128]{0:T(128)S(1)}, u32[]{:S(2)}, u32[]{:S(2)}) collective-permute-start(s32[128]{0:T(128)S(1)} %pad.4), channel_id=1, source_target_pairs={{0,96},{32,0},{64,32},{96,64},{1,97},{33,1},{65,33},{97,65},{2,98}... | collective-permute-start | bytes 1544 | tf_op jit(solution)/shard_map/ppermute | solution.py:414
  11.0 14.7 %collective-permute-start.1 = (s32[128]{0:T(128)S(1)}, s32[128]{0:T(128)S(1)}, u32[]{:S(2)}, u32[]{:S(2)}) collective-permute-start(s32[128]{0:T(128)S(1)} %pad.4), channel_id=1, source_target_pairs={{0,64},{32,96},{64,0},{96,32},{1,65},{33,97},{65,1},{97,33},{2,66}... | collective-permute-start | bytes 1544 | tf_op jit(solution)/shard_map/ppermute | solution.py:414
  11.0 14.7 %collective-permute-start = (s32[128]{0:T(128)S(1)}, s32[128]{0:T(128)S(1)}, u32[]{:S(2)}, u32[]{:S(2)}) collective-permute-start(s32[128]{0:T(128)S(1)} %pad.4), channel_id=1, source_target_pairs={{0,32},{32,64},{64,96},{96,0},{1,33},{33,65},{65,97},{97,1},{2,34}... | collective-permute-start | bytes 1544 | tf_op jit(solution)/shard_map/ppermute | solution.py:414
  12.3 28.8 %collective-permute-start.5 = (bf16[2,3,128,512]{3,2,1,0:T(8,128)(2,1)}, bf16[2,3,128,512]{3,2,1,0:T(8,128)(2,1)S(1)}, u32[]{:S(2)}, u32[]{:S(2)}) collective-permute-start(bf16[2,3,128,512]{3,2,1,0:T(8,128)(2,1)} %whiten.3.refs_1_), channel_id=1, source_target_pairs={{1,2},{2,1},{3,4},{4,3},{5,6},{6,5},{7,8},{8,7},{9,10},{10,9},{11,... | collective-permute-start | bytes 2359304 | tf_op jit(solution)/shard_map/ppermute | solution.py:430
  21.7 19.4 %copy-start = (bf16[2,3,128,512]{3,2,1,0:T(8,128)(2,1)S(1)}, bf16[2,3,128,512]{3,2,1,0:T(8,128)(2,1)}, u32[]{:S(2)}) copy-start(bf16[2,3,128,512]{3,2,1,0:T(8,128)(2,1)} %whiten.3.refs_1_) | copy-start | bytes 2359300
  21.7 19.4 %copy-start.1 = (bf16[2,3,128,512]{3,2,1,0:T(8,128)(2,1)S(1)}, bf16[2,3,128,512]{3,2,1,0:T(8,128)(2,1)}, u32[]{:S(2)}) copy-start(bf16[2,3,128,512]{3,2,1,0:T(8,128)(2,1)} %whiten.4.refs_0_) | copy-start | bytes 2359300
  21.7 19.5 %copy-start.4 = (bf16[512,256]{1,0:T(8,128)(2,1)S(1)}, bf16[512,256]{1,0:T(8,128)(2,1)}, u32[]{:S(2)}) copy-start(bf16[512,256]{1,0:T(8,128)(2,1)} %constant.38.clone.refs_8_) | copy-start | bytes 786436
  21.7 19.4 %collective-permute-start.4 = (bf16[2,3,128,512]{3,2,1,0:T(8,128)(2,1)}, bf16[2,3,128,512]{3,2,1,0:T(8,128)(2,1)S(1)}, u32[]{:S(2)}, u32[]{:S(2)}) collective-permute-start(bf16[2,3,128,512]{3,2,1,0:T(8,128)(2,1)} %whiten.4.refs_0_), channel_id=1, source_target_pairs={{1,2},{2,1},{3,4},{4,3},{5,6},{6,5},{7,8},{8,7},{9,10},{10,9},{11,... | collective-permute-start | bytes 2359304 | tf_op jit(solution)/shard_map/ppermute | solution.py:428
  33.6 7.5 %collective-permute-start.6 = (bf16[2,3,128,512]{3,2,1,0:T(8,128)(2,1)}, bf16[2,3,128,512]{3,2,1,0:T(8,128)(2,1)}, u32[]{:S(2)}, u32[]{:S(2)}) collective-permute-start(bf16[2,3,128,512]{3,2,1,0:T(8,128)(2,1)} %get-tuple-element.22.refs_2_), channel_id=1, source_target_pairs={{0,1},{1,0},{2,3},{3,2},{4,5},{5,4},{6,7},{7,6},{8,9},{9,8},{10,11... | collective-permute-start | bytes 2359304 | tf_op jit(solution)/shard_map/ppermute | solution.py:436
  33.6 7.5 %collective-permute-start.7 = (bf16[2,3,128,512]{3,2,1,0:T(8,128)(2,1)}, bf16[2,3,128,512]{3,2,1,0:T(8,128)(2,1)}, u32[]{:S(2)}, u32[]{:S(2)}) collective-permute-start(bf16[2,3,128,512]{3,2,1,0:T(8,128)(2,1)} %get-tuple-element.23.refs_3_), channel_id=1, source_target_pairs={{0,1},{1,0},{2,3},{3,2},{4,5},{5,4},{6,7},{7,6},{8,9},{9,8},{10,11... | collective-permute-start | bytes 2359304 | tf_op jit(solution)/shard_map/ppermute | solution.py:436
  34.1 7.0 %collective-permute-start.3 = (s32[512]{0:T(512)S(1)}, s32[512]{0:T(512)S(1)}, u32[]{:S(2)}, u32[]{:S(2)}) collective-permute-start(s32[512]{0:T(512)S(1)} %slice.3), channel_id=1, source_target_pairs={{0,1},{1,2},{2,3},{3,4},{4,5},{5,6},{6,7},{7,8},{8,9},{9,10},{10,1... | collective-permute-start | bytes 6152 | tf_op jit(solution)/shard_map/ppermute | solution.py:435
  41.2 1.1 %copy-start.2 = (bf16[2,3,128,512]{3,2,1,0:T(8,128)(2,1)S(1)}, bf16[2,3,128,512]{3,2,1,0:T(8,128)(2,1)}, u32[]{:S(2)}) copy-start(bf16[2,3,128,512]{3,2,1,0:T(8,128)(2,1)} %get-tuple-element.22.refs_2_) | copy-start | bytes 2359300
  42.3 1.1 %copy-start.3 = (bf16[2,3,128,512]{3,2,1,0:T(8,128)(2,1)S(1)}, bf16[2,3,128,512]{3,2,1,0:T(8,128)(2,1)}, u32[]{:S(2)}) copy-start(bf16[2,3,128,512]{3,2,1,0:T(8,128)(2,1)} %get-tuple-element.23.refs_3_) | copy-start | bytes 2359300
  51.4 8.8 %collective-permute-start.8 = (bf16[848,128]{1,0:T(8,128)(2,1)S(1)}, bf16[848,128]{1,0:T(8,128)(2,1)S(1)}, u32[]{:S(2)}, u32[]{:S(2)}) collective-permute-start(bf16[848,128]{1,0:T(8,128)(2,1)S(1)} %get-tuple-element.26), channel_id=1, source_target_pairs={{0,32},{32,64},{64,96},{96,0},{1,33},{33,65},{65,97},{97,1},{2,34}... | collective-permute-start | bytes 651272 | tf_op jit(solution)/shard_map/ppermute | solution.py:414
  53.7 8.8 %collective-permute-start.9 = (bf16[848,128]{1,0:T(8,128)(2,1)S(1)}, bf16[848,128]{1,0:T(8,128)(2,1)S(1)}, u32[]{:S(2)}, u32[]{:S(2)}) collective-permute-start(bf16[848,128]{1,0:T(8,128)(2,1)S(1)} %get-tuple-element.27), channel_id=1, source_target_pairs={{0,64},{32,96},{64,0},{96,32},{1,65},{33,97},{65,1},{97,33},{2,66}... | collective-permute-start | bytes 651272 | tf_op jit(solution)/shard_map/ppermute | solution.py:414
  54.9 8.0 %collective-permute-start.10 = (bf16[848,128]{1,0:T(8,128)(2,1)S(1)}, bf16[848,128]{1,0:T(8,128)(2,1)S(1)}, u32[]{:S(2)}, u32[]{:S(2)}) collective-permute-start(bf16[848,128]{1,0:T(8,128)(2,1)S(1)} %get-tuple-element.28), channel_id=1, source_target_pairs={{0,96},{32,0},{64,32},{96,64},{1,97},{33,1},{65,33},{97,65},{2,98}... | collective-permute-start | bytes 651272 | tf_op jit(solution)/shard_map/ppermute | solution.py:414
  64.0 12.7 %collective-permute-start.11 = (bf16[528,128]{1,0:T(8,128)(2,1)S(1)}, bf16[528,128]{1,0:T(8,128)(2,1)S(1)}, u32[]{:S(2)}, u32[]{:S(2)}) collective-permute-start(bf16[528,128]{1,0:T(8,128)(2,1)S(1)} %get-tuple-element.30), channel_id=1, source_target_pairs={{0,1},{1,2},{2,3},{3,4},{4,5},{5,6},{6,7},{7,8},{8,9},{9,10},{10,1... | collective-permute-start | bytes 405512 | tf_op jit(solution)/shard_map/ppermute | solution.py:441
  66.0 7.4 %collective-permute-start.12 = (bf16[272,128]{1,0:T(8,128)(2,1)S(1)}, bf16[272,128]{1,0:T(8,128)(2,1)S(1)}, u32[]{:S(2)}, u32[]{:S(2)}) collective-permute-start(bf16[272,128]{1,0:T(8,128)(2,1)S(1)} %get-tuple-element.31), channel_id=1, source_target_pairs={{0,32},{32,64},{64,96},{96,0},{1,33},{33,65},{65,97},{97,1},{2,34}... | collective-permute-start | bytes 208904 | tf_op jit(solution)/shard_map/ppermute | solution.py:414
  67.7 7.7 %collective-permute-start.13 = (bf16[272,128]{1,0:T(8,128)(2,1)S(1)}, bf16[272,128]{1,0:T(8,128)(2,1)S(1)}, u32[]{:S(2)}, u32[]{:S(2)}) collective-permute-start(bf16[272,128]{1,0:T(8,128)(2,1)S(1)} %get-tuple-element.32), channel_id=1, source_target_pairs={{0,64},{32,96},{64,0},{96,32},{1,65},{33,97},{65,1},{97,33},{2,66}... | collective-permute-start | bytes 208904 | tf_op jit(solution)/shard_map/ppermute | solution.py:414
  72.4 4.3 %collective-permute-start.14 = (bf16[272,128]{1,0:T(8,128)(2,1)S(1)}, bf16[272,128]{1,0:T(8,128)(2,1)S(1)}, u32[]{:S(2)}, u32[]{:S(2)}) collective-permute-start(bf16[272,128]{1,0:T(8,128)(2,1)S(1)} %get-tuple-element.33), channel_id=1, source_target_pairs={{0,96},{32,0},{64,32},{96,64},{1,97},{33,1},{65,33},{97,65},{2,98}... | collective-permute-start | bytes 208904 | tf_op jit(solution)/shard_map/ppermute | solution.py:414

commit v4 on v3

v4 whole, which is shorter than its diff:
```python
import functools

import jax
import jax.numpy as jnp
import ml_dtypes
import numpy as np
from jax import lax
from jax.experimental import pallas as pl
from jax.experimental.pallas import tpu as pltpu
from jax.sharding import PartitionSpec as P

BINS = 256
LENGTH = 512
CHANS = 128
MAXLAG = 32
LAGS = 2 * MAXLAG + 1
REACH = 8
SMOOTH = 32
BAND = 64
GROUP = 8
HALF = GROUP // 2
PLANES = 4
ROWS = HALF * CHANS
SUB = 256
REACHED = 384
SLOTS = 13
SHIFTED = 8
BODY = 64
CHUNK = SLOTS * BODY + 16
SEND2 = SHIFTED * BODY + 16
SEND3 = 4 * BODY + 16
SEG, PAIRS, MOVES, WRITES, PLAN = 4, 16, 80, 112, 256
TWO = CHUNK
THREE = CHUNK + SEND2
POOL = THREE + 3 * SEND3
MIB = 1024 * 1024
TINY = pl.CostEstimate(flops=1, bytes_accessed=1, transcendentals=0)
BF = jnp.bfloat16
F32 = jnp.float32
SMEM = pl.BlockSpec(memory_space=pltpu.SMEM)
VMEM = pl.BlockSpec(memory_space=pltpu.VMEM)


def split(array):
    high = array.astype(ml_dtypes.bfloat16)
    low = (array - high.astype(np.float32)).astype(ml_dtypes.bfloat16)
    return high, low


def lag_rows(segments):
    shifts = np.arange(-MAXLAG, MAXLAG + 1)
    phase = (shifts[:, None] * np.arange(BINS)[None, :] % LENGTH) * (2.0 * np.pi / LENGTH)
    table = np.concatenate([np.cos(phase), -np.sin(phase)], axis=1) / np.sqrt(segments * BINS)
    table = np.concatenate([table, np.zeros((CHANS - LAGS, LENGTH))], axis=0).T.astype(np.float32)
    return np.concatenate(split(table), axis=1)


def dot(a, b):
    return jnp.dot(a, b, preferred_element_type=F32)


def halves(x):
    high = x.astype(BF)
    return high, (x - high.astype(F32)).astype(BF)


def inverse(y):
    r = pl.reciprocal(y, approx=True)
    return r * (2.0 - y * r)


def make_tables(tab):
    at = lax.broadcasted_iota(jnp.int32, (REACHED, LENGTH), 0)
    col = lax.broadcasted_iota(jnp.int32, (REACHED, LENGTH), 1)
    apart = at - col + jnp.where(col < BINS, 0, LENGTH - REACHED)
    tab[:REACHED] = jnp.where(jnp.abs(apart) <= SMOOTH, 1.0, 0.0).astype(BF)
    row = lax.broadcasted_iota(jnp.int32, (CHANS, LENGTH), 0)
    col = lax.broadcasted_iota(jnp.int32, (CHANS, LENGTH), 1)
    row = row + jnp.where(col < BINS, 0, CHANS)
    col = jnp.bitwise_and(col, BINS - 1)
    tab[REACHED:LENGTH] = jnp.where(row // BAND == col // BAND, 0.5 / BAND, 0.0).astype(BF)

    def cosine(step, shift, rows):
        k = lax.broadcasted_iota(jnp.int32, (rows, BINS), 0) * lax.broadcasted_iota(jnp.int32, (rows, BINS), 1)
        k = jnp.bitwise_and(k * step - shift + BINS, LENGTH - 1) - BINS
        square = jnp.square(k.astype(F32) * (2.0 * np.pi / LENGTH))
        value = jnp.ones_like(square)
        for n in range(20, 0, -2):
            value = 1.0 - value * square * (1.0 / (n * (n - 1)))
        return value

    quarter = LENGTH // 4
    fine_cos, fine_sin = cosine(1, 0, 16), cosine(1, quarter, 16)
    coarse_cos, coarse_sin = cosine(16, 0, 32), cosine(16, quarter, 32)
    for a in range(LENGTH // 16):
        c, s = coarse_cos[a : a + 1], coarse_sin[a : a + 1]
        for k, part in enumerate((c * fine_cos - s * fine_sin, -(s * fine_cos) - c * fine_sin)):
            high, low = halves(part)
            tab[LENGTH + 16 * a : LENGTH + 16 * a + 16, k * BINS : (k + 1) * BINS] = high
            tab[2 * LENGTH + 16 * a : 2 * LENGTH + 16 * a + 16, k * BINS : (k + 1) * BINS] = low


def whiten_body(outer, records, white, buf, tab, sems):
    segs = records.shape[0]
    core = jnp.bitwise_and(lax.axis_index("blk"), 1)
    begin = pl.multiple_of((core if outer else 1 - core) * ROWS, ROWS)

    def load(k):
        return pltpu.make_async_copy(records.at[k, pl.ds(begin, ROWS)], buf.at[k], sems.at[k])

    for k in range(segs):
        load(k).start()
    at = lax.broadcasted_iota(jnp.int32, (1, LENGTH), 1)
    count = jnp.minimum(at, SMOOTH) + jnp.minimum(LENGTH - 1 - at, SMOOTH) + 1
    share = 1.0 / count.astype(F32)
    make_tables(tab)

    def step(k, carry):
        load(k).wait()
        parts = range(ROWS // SUB)
        xs = [buf[k, pl.ds(n * SUB, SUB), :] for n in parts]
        levels = []
        first = tab[:REACHED, :BINS]
        second = tab[:REACHED, BINS:]
        for x in xs:
            ahi, alo = halves(jnp.abs(x))
            left = jnp.concatenate([ahi[:, :REACHED], alo[:, :REACHED]], axis=1)
            right = jnp.concatenate([ahi[:, LENGTH - REACHED :], alo[:, LENGTH - REACHED :]], axis=1)
            left = dot(left, jnp.concatenate([first, first], axis=0))
            right = dot(right, jnp.concatenate([second, second], axis=0))
            levels.append(jnp.concatenate([left, right], axis=1) * share)
        spectra = []
        fhi = tab[LENGTH : 2 * LENGTH]
        fourier = jnp.concatenate([fhi, fhi, tab[2 * LENGTH :]], axis=0)
        for x, level in zip(xs, levels):
            nhi, nlo = halves(x * inverse(level + 1e-06))
            spectra.append(dot(jnp.concatenate([nhi, nlo, nhi], axis=1), fourier))
        same = jnp.concatenate([tab[REACHED:LENGTH, :BINS], tab[REACHED:LENGTH, BINS:]], axis=0)
        for n in parts:
            re = spectra[n][:, :BINS]
            im = spectra[n][:, BINS:]
            power = dot((re * re + im * im).astype(BF), same)
            factor = lax.rsqrt(power + 1e-05)
            per = SUB // CHANS
            white[pl.ds(n * per, per), k, :, :BINS] = (re * factor).astype(BF).reshape(per, CHANS, BINS)
            white[pl.ds(n * per, per), k, :, BINS:] = (im * factor).astype(BF).reshape(per, CHANS, BINS)
        return carry

    lax.fori_loop(0, segs, step, 0)


def whiten(outer, records):
    segs = records.shape[0]
    return pl.pallas_call(
        functools.partial(whiten_body, outer),
        in_specs=[pl.BlockSpec(memory_space=pltpu.HBM)],
        out_specs=VMEM,
        out_shape=jax.ShapeDtypeStruct((HALF, segs, CHANS, LENGTH), BF),
        scratch_shapes=[
            pltpu.VMEM((segs, ROWS, LENGTH), F32),
            pltpu.VMEM((3 * LENGTH, LENGTH), BF),
            pltpu.SemaphoreType.DMA((segs,)),
        ],
        compiler_params=pltpu.CompilerParams(vmem_limit_bytes=50 * MIB),
        cost_estimate=TINY,
        name="whiten",
    )(records)


VISITS = [(p, d) for p in range(HALF) for d in range(1, REACH + 1) if p + d >= HALF] + [
    (p, d) for p in range(HALF, 12) for d in range(1, REACH + 1) if p < GROUP or p + d < 12
]
UPWARD = (
    ((0, 0), (1, 0), (1, 1), (2, 0), (2, 1), (3, 0), (3, 1)),
    ((2, 2), (3, 2), (3, 3)),
)


def plan_body(own, before, plan, slots):
    s = lax.axis_index("seg").astype(jnp.int32)
    plan[SEG] = s
    zero = jnp.int32(0)

    def behind(owner):
        return 2 * jnp.bitwise_and(s - owner, 3)

    used = [zero] * PLANES
    n = zero
    for p, d in VISITS:
        row = p + HALF if p < HALF else p - HALF
        owner = row // 2
        live = (before if p < HALF else own)[behind(owner) + row % 2, d - 1]
        code = p + d * 16 + jnp.bitwise_and(owner - s, 3) * 256 + used[owner] * 4096
        slots[p * REACH + d - 1] = used[owner]
        used[owner] = used[owner] + live
        if p in (6, 7) and p + d in (12, 13):
            slots[96 + (p - 6) * 2 + p + d - 12] = used[0]
            code = code + (used[0] + 1) * 65536
            used[0] = used[0] + live
        plan[PAIRS + n] = code
        n = n + live
    plan[0] = n

    n = zero
    for owner in (0, 1):
        for k, (i, j) in enumerate(UPWARD[owner]):
            p, d = HALF + i, GROUP + j - i
            entry = p * REACH + d - 1 if i // 2 == owner else 96 + (i - 2) * 2 + j
            plan[MOVES + n] = slots[entry] + k * 4096
            n = n + jnp.where(s == owner, own[behind(i // 2) + i % 2, d - 1], 0)
    for r in range(1, PLANES):
        to = jnp.bitwise_and(s + r, 3)
        ahead = s < to
        for i in range(2):
            for j in range(2):
                row = 2 * s + i
                p = jnp.where(ahead, row + HALF, jnp.maximum(row - HALF, 0))
                d = 2 * to + j - row + jnp.where(ahead, 0, GROUP)
                live = jnp.where(ahead, own[i, d - 1], jnp.where(s >= 2, before[i, d - 1], 0))
                plan[MOVES + n] = slots[p * REACH + d - 1] + r * 256 + (2 * i + j) * 4096
                n = n + live
    plan[1] = n

    def write(n, i, d, base, size, slot):
        plan[WRITES + n] = base + slot * BODY + (base + size * BODY + slot) * 4096 + (i * 8 + d - 1) * 16777216

    n = zero
    above = zero
    for i in range(2):
        for d in range(1, REACH + 1):
            row = 2 * s + i
            live = own[i, d - 1]
            shift = (row + d >= GROUP) & (s >= 2)
            slot = jnp.where(shift, above, slots[(HALF + row) * REACH + d - 1])
            write(n, i, d, jnp.where(shift, TWO, 0), jnp.where(shift, SHIFTED, SLOTS), slot)
            n = n + live
            above = above + jnp.where(shift, live, 0)
    plan[2] = n
    for j in range(2):
        for d in range(1, REACH + 1):
            low = 2 * s + j - d
            crossing = low < 0
            row = jnp.where(crossing, low + GROUP, low)
            owner = jnp.right_shift(row, 1)
            at = behind(owner) + jnp.bitwise_and(row, 1)
            live = jnp.where(crossing, before[at, d - 1], own[at, d - 1])
            up = crossing & (owner < 2)
            mine = (owner == s) & jnp.logical_not(up)
            k0 = jnp.where(row == 0, 0, 2 * row - 1) + j
            k1 = jnp.where(row == 2, 0, 1) + j
            entry = jnp.maximum((HALF + low) * REACH + d - 1, 0)
            slot = jnp.where(mine, slots[entry], 2 * (row - 2 * owner) + j)
            slot = jnp.where(up, jnp.where(s == 0, k0, k1), slot)
            base = jnp.where(mine, 0, THREE + (jnp.bitwise_and(s - owner, 3) - 1) * SEND3)
            base = jnp.where(up, TWO, base)
            size = jnp.where(mine, SLOTS, jnp.where(up, SHIFTED, 4))
            write(n, j, d, base, size, slot)
            n = n + live
    plan[3] = n


def make_plan(own, before):
    return pl.pallas_call(
        plan_body,
        in_specs=[SMEM, SMEM],
        out_specs=SMEM,
        out_shape=jax.ShapeDtypeStruct((PLAN,), jnp.int32),
        scratch_shapes=[pltpu.SMEM((128,), jnp.int32)],
        cost_estimate=TINY,
        name="plan",
    )(own, before)


def correlate_body(plan, own_ext, own_int, got_ext, got_int, lag, keep, out1, out2, out3, low, high, stk, pq, last):
    core = jnp.bitwise_and(lax.axis_index("blk"), 1)
    sources = (
        (own_ext, HALF * (1 + core)),
        (own_int, HALF * (2 - core)),
        (got_ext, 3 * HALF * core),
        (got_int, 3 * HALF * (1 - core)),
    )
    segs = low.shape[0]
    last[0] = -1

    def grab(dest, block):
        for ref, begin in sources:

            @pl.when((block >= begin) & (block < begin + HALF))
            def _(ref=ref, begin=begin):
                dest[...] = ref[block - begin]

    def put(r, n, stack):
        stk[r, pl.ds(pl.multiple_of(n * BODY, BODY), BODY), :] = stack[:BODY]
        stk[r, pl.ds(SLOTS * BODY + n, 1), :] = stack[BODY:LAGS]

    def pair(n, carry):
        code = plan[PAIRS + n]
        p = jnp.bitwise_and(code, 15)
        d = jnp.bitwise_and(jnp.right_shift(code, 4), 15)

        @pl.when(last[0] != p)
        def _():
            grab(low, p)
            last[0] = p

        grab(high, p + d)
        for chunk in range(CHANS // 16):
            rows = pl.ds(chunk * 16, 16)
            real = jnp.zeros((16, BINS), F32)
            imag = jnp.zeros((16, BINS), F32)
            for k in range(segs):
                are = low[k, rows, :BINS].astype(F32)
                aim = low[k, rows, BINS:].astype(F32)
                bre = high[k, rows, :BINS].astype(F32)
                bim = high[k, rows, BINS:].astype(F32)
                real += are * bre + aim * bim
                imag += are * bim - aim * bre
            rhi, rlo = halves(real)
            ihi, ilo = halves(imag)
            pq[0, rows, :BINS] = rhi
            pq[0, rows, BINS:] = ihi
            pq[1, rows, :BINS] = rlo
            pq[1, rows, BINS:] = ilo
        both = dot(pq[0], lag[...])
        stack = (both[:, :CHANS] + both[:, CHANS:] + dot(pq[1], lag[:, :CHANS])).T
        put(jnp.bitwise_and(jnp.right_shift(code, 8), 3), jnp.bitwise_and(jnp.right_shift(code, 12), 15), stack)
        second = jnp.right_shift(code, 16)

        @pl.when(second > 0)
        def _():
            put(jnp.bitwise_and(-plan[SEG], 3), second - 1, stack)

        return carry

    lax.fori_loop(0, plan[0], pair, 0)
    keep[...] = stk[0]
    out1[...] = stk[1].astype(BF)
    out2[...] = stk[2].astype(BF)
    out3[...] = stk[3].astype(BF)


def correlate(plan, whites, lag):
    segs = whites[0].shape[1]
    chunk = jax.ShapeDtypeStruct((CHUNK, CHANS), BF)
    return pl.pallas_call(
        correlate_body,
        in_specs=[SMEM] + [VMEM] * 5,
        out_specs=[VMEM] * 4,
        out_shape=[jax.ShapeDtypeStruct((CHUNK, CHANS), F32), chunk, chunk, chunk],
        scratch_shapes=[
            pltpu.VMEM((segs, CHANS, LENGTH), BF),
            pltpu.VMEM((segs, CHANS, LENGTH), BF),
            pltpu.VMEM((PLANES, CHUNK, CHANS), F32),
            pltpu.VMEM((2, CHANS, LENGTH), BF),
            pltpu.SMEM((1,), jnp.int32),
        ],
        compiler_params=pltpu.CompilerParams(vmem_limit_bytes=16 * MIB),
        cost_estimate=TINY,
        name="correlate",
    )(plan, *whites, lag)


def combine_body(plan, keep, got2, got1, got3, full, send, out1, out2, out3, stage):
    full[...] = (keep[...] + got1[...].astype(F32)) + (got2[...].astype(F32) + got3[...].astype(F32))

    def move(n, carry):
        code = plan[MOVES + n]
        slot = jnp.bitwise_and(code, 255)
        message = jnp.bitwise_and(jnp.right_shift(code, 8), 15)
        k = jnp.right_shift(code, 12)
        size = jnp.where(message == 0, SHIFTED, 4)
        body = pl.ds(pl.multiple_of(slot * BODY, BODY), BODY)
        stage[message, pl.ds(pl.multiple_of(k * BODY, BODY), BODY), :] = full[body, :]
        stage[message, pl.ds(size * BODY + k, 1), :] = full[pl.ds(SLOTS * BODY + slot, 1), :]
        return carry

    lax.fori_loop(0, plan[1], move, 0)

    @pl.when(plan[SEG] >= 2)
    def _():
        send[: SHIFTED * BODY, :] = full[: SHIFTED * BODY, :].astype(BF)
        send[SHIFTED * BODY :, :] = full[SLOTS * BODY :, :].astype(BF)

    @pl.when(plan[SEG] < 2)
    def _():
        send[...] = stage[0].astype(BF)

    for r, out in ((1, out1), (2, out2), (3, out3)):
        out[...] = stage[r, :SEND3].astype(BF)


def combine(*args):
    third = jax.ShapeDtypeStruct((SEND3, CHANS), BF)
    return pl.pallas_call(
        combine_body,
        in_specs=[SMEM] + [VMEM] * 4,
        out_specs=[VMEM] * 5,
        out_shape=[
            jax.ShapeDtypeStruct((CHUNK, CHANS), F32),
            jax.ShapeDtypeStruct((SEND2, CHANS), BF),
            third,
            third,
            third,
        ],
        scratch_shapes=[pltpu.VMEM((PLANES, SEND2, CHANS), F32)],
        compiler_params=pltpu.CompilerParams(vmem_limit_bytes=8 * MIB),
        cost_estimate=TINY,
        name="combine",
    )(*args)


def finish_body(plan, full, shifted, got2, got1, got3, fwd, bwd, pool):
    pool[:TWO, :] = full[...]
    pool[TWO:THREE, :] = shifted[...].astype(F32)
    for r, got in ((1, got1), (2, got2), (3, got3)):
        pool[THREE + (r - 1) * SEND3 : THREE + r * SEND3, :] = got[...].astype(F32)
    fwd[...] = jnp.zeros(fwd.shape, F32)
    bwd[...] = jnp.zeros(bwd.shape, F32)

    def write(out, place, n):
        code = plan[WRITES + n]
        body = jnp.bitwise_and(code, 4095)
        i = jnp.right_shift(code, 27)
        at = pl.ds(jnp.bitwise_and(jnp.right_shift(code, 24), 7), 1)
        out[i, place(BODY), at, :] = pool[pl.ds(jnp.bitwise_and(jnp.right_shift(code, 12), 4095), 1), :]
        for m in range(BODY):
            out[i, place(m), at, :] = pool[pl.ds(body + m, 1), :]

    def ahead(n, carry):
        write(fwd, lambda m: m, n)
        return carry

    def behind(n, carry):
        write(bwd, lambda m: BODY - m, n)
        return carry

    lax.fori_loop(0, plan[2], ahead, 0)
    lax.fori_loop(plan[2], plan[3], behind, 0)


def finish(blocks, *args):
    out = jax.ShapeDtypeStruct((blocks, LAGS, REACH, CHANS), F32)
    return pl.pallas_call(
        finish_body,
        in_specs=[SMEM] + [VMEM] * 5,
        out_specs=[VMEM, VMEM],
        out_shape=[out, out],
        scratch_shapes=[pltpu.VMEM((POOL, CHANS), F32)],
        compiler_params=pltpu.CompilerParams(vmem_limit_bytes=8 * MIB),
        cost_estimate=TINY,
        name="finish",
    )(*args)


def shards(groups, planes, lag, records, pairs):
    def ring(x, r):
        return lax.ppermute(x, "seg", [(z, (z + r) % planes) for z in range(planes)])

    outer = [(g, g + 1 if g % 2 else g - 1) for g in range(1, groups - 1)]
    inner = [(g, g ^ 1) for g in range(groups)]
    upward = [(g, g + 1) for g in range(groups - 1)]
    shift = [
        (z * groups + g, z * groups + g + step)
        for z in range(planes)
        for g in range(groups)
        for step in (1 if z < 2 else -1,)
        if 0 <= g + step < groups
    ]
    own_ext = whiten(True, records)
    got_ext = lax.ppermute(own_ext, "blk", outer)
    own_int = whiten(False, records)
    got_int = lax.ppermute(own_int, "blk", inner)
    rows, _ = lax.optimization_barrier((pairs, own_int))
    own = jnp.concatenate([rows, ring(rows, 1), ring(rows, 2), ring(rows, 3)])
    plan = make_plan(own, lax.ppermute(own, "blk", upward))

    keep, out1, out2, out3 = correlate(plan, (own_ext, own_int, got_ext, got_int), lag)
    full, send, out1, out2, out3 = combine(plan, keep, ring(out2, 2), ring(out1, 1), ring(out3, 3))
    shifted = lax.ppermute(send, ("seg", "blk"), shift)
    outs = finish(pairs.shape[0], plan, full, shifted, ring(out2, 2), ring(out1, 1), ring(out3, 3))
    return tuple(jnp.transpose(out, (0, 2, 1, 3)) for out in outs)


def solution(mesh):
    groups = mesh.shape["blk"]
    planes = mesh.shape["seg"]

    def run(records, pairs):
        body = functools.partial(
            shards,
            groups,
            planes,
            jnp.asarray(lag_rows(records.shape[0])),
        )
        return jax.shard_map(
            body,
            mesh=mesh,
            in_specs=(P("seg", "blk", None), P(("blk", "seg"), None)),
            out_specs=(P(("blk", "seg"), None, None, None), P(("blk", "seg"), None, None, None)),
            check_vma=False,
        )(records, pairs)

    return run
```

time: 79.3 us -> 67.5 us (0.85)
  Pallas kernels: 30.2 us -> 21.7 us
  starting transfers between devices: 29.8 us -> 27 us
  local copies, waits for them, and re-layouts: 3.13 us -> 1.28 us
  waiting for transfers between devices: 15 us -> 16.4 us
    pallas_call x6, Pallas kernels: 30.2 us -> 21.7 us  [the longest x2 12.2 us: whiten(): pl.pallas_call(functools.partial(whiten_body, outer), in_specs=[pl.BlockS...]
    ppermute x6 -> x4, starting transfers between devices: 12.2 us -> 8.68 us  [the longest x1 4.75 us: shards(): got_ext = lax.ppermute(own_ext, 'blk', outer)]
    ppermute x9, waiting for transfers between devices: 9.93 us -> 11.3 us  [ring(): lax.ppermute(x, 'seg', [(z, (z + r) % planes) for z in range(planes)])]
    unnamed x13 -> x10, local copies, waits for them, and re-layouts: 2.28 us -> 1.28 us
    ppermute x6 -> x4, waiting for transfers between devices: 5.05 us -> 5.12 us  [the longest x1 5.11 us: shards(): plan = make_plan(own, lax.ppermute(own, 'blk', upward))]
  transfers between devices with their start and end apart: 15 -> 13, of which waited for: 7 -> 5; matrix products, arithmetic and copies ran while one was open for 0% -> 0% of each run, Pallas kernels for 17% -> 12%
where the time goes in v4:
time: 67.5 us; the launch traced here: 67.1 us
  starting transfers between devices  27 us (40%)
  Pallas kernels  21.7 us (32%)
  waiting for transfers between devices  16.4 us (24%)
  local copies, waits for them, and re-layouts  1.28 us (2%)
  between operations  0.78 us (1%)
    ppermute x9, starting transfers between devices, ring(): lax.ppermute(x, 'seg', [(z, (z + r) % planes) for z in range(planes)])  18.3 us
    pallas_call x2, Pallas kernels, whiten(): pl.pallas_call(functools.partial(whiten_body, outer), in_specs=[pl.BlockS...  12.2 us
    ppermute x9, waiting for transfers between devices, ring(): lax.ppermute(x, 'seg', [(z, (z + r) % planes) for z in range(planes)])  11.3 us
    ppermute x1, waiting for transfers between devices, shards(): plan = make_plan(own, lax.ppermute(own, 'blk', upward))  5.11 us
    pallas_call x1, Pallas kernels, correlate(): pl.pallas_call(correlate_body, in_specs=[SMEM] + [VMEM] * 5, out_specs=[V...  5.08 us
    ppermute x1, starting transfers between devices, shards(): got_ext = lax.ppermute(own_ext, 'blk', outer)  4.75 us
    pallas_call x1, Pallas kernels, make_plan(): pl.pallas_call(plan_body, in_specs=[SMEM, SMEM], out_specs=SMEM, out_shap...  1.98 us
    ppermute x1, starting transfers between devices, shards(): plan = make_plan(own, lax.ppermute(own, 'blk', upward))  1.92 us
  transfers between devices with their start and end apart: 13, of which 5 were waited for; matrix products, arithmetic and copies ran while one was open for 0% of the time, Pallas kernels for 12%

profile of v4, /device:TPU:6, one launch (start us, length us, event | category | flops | bytes accessed | tf_op | source)
XLA Modules:
  0.0 67.1 jit_solution(742623400970577814)
XLA Ops:
  0.6 6.1 %whiten.3.own_ext = bf16[4,3,128,512]{3,2,1,0:T(8,128)(2,1)S(1)} custom-call(f32[3,1024,512]{2,1,0:T(8,128)} %records.3), custom_call_target="tpu_custom_call" | custom-call | flops 1 | bytes 1 | tf_op jit(solution)/shard_map/whiten/pallas_call | solution.py:154
  6.7 0.0 copy-start.4
  6.7 0.0 copy-start
  6.8 4.8 %collective-permute-start.4 = (bf16[4,3,128,512]{3,2,1,0:T(8,128)(2,1)S(1)}, bf16[4,3,128,512]{3,2,1,0:T(8,128)(2,1)}, u32[]{:S(2)}, u32[]{:S(2)}) collective-permute-start(bf16[4,3,128,512]{3,2,1,0:T(8,128)(2,1)S(1)} %whiten.3.own_ext), channel_id=1, source_target_pairs={{1,2},{2,1},{3,4},{4,3},{5,6},{6,5},{7,8},{8,7},{9,10},{10,9},{11,... | collective-permute-start | bytes 4718600 | tf_op jit(solution)/shard_map/ppermute | solution.py:470
  11.5 6.1 %whiten.2.own_int = bf16[4,3,128,512]{3,2,1,0:T(8,128)(2,1)S(1)} custom-call(f32[3,1024,512]{2,1,0:T(8,128)} %records.3), custom_call_target="tpu_custom_call" | custom-call | flops 1 | bytes 1 | tf_op jit(solution)/shard_map/whiten/pallas_call | solution.py:154
  17.6 0.1 collective-permute-start.5
  17.7 0.0 copy-done.4
  17.7 4.1 %collective-permute-start.2 = (s32[2,8]{1,0:T(2,128)S(1)}, s32[2,8]{1,0:T(2,128)S(1)}, u32[]{:S(2)}, u32[]{:S(2)}) collective-permute-start(s32[2,8]{1,0:T(2,128)S(1)} %copy-done.4), channel_id=1, source_target_pairs={{0,96},{32,0},{64,32},{96,64},{1,97},{33,1},{65,33},{97,65},{2,98}... | collective-permute-start | bytes 200 | tf_op jit(solution)/shard_map/ppermute | solution.py:457
  21.8 0.0 collective-permute-start.1
  21.8 1.3 %collective-permute-start = (s32[2,8]{1,0:T(2,128)S(1)}, s32[2,8]{1,0:T(2,128)S(1)}, u32[]{:S(2)}, u32[]{:S(2)}) collective-permute-start(s32[2,8]{1,0:T(2,128)S(1)} %copy-done.4), channel_id=1, source_target_pairs={{0,32},{32,64},{64,96},{96,0},{1,33},{33,65},{65,97},{97,1},{2,34}... | collective-permute-start | bytes 200 | tf_op jit(solution)/shard_map/ppermute | solution.py:457
  23.1 0.0 collective-permute-done.2
  23.1 3.8 %collective-permute-done.1 = s32[2,8]{1,0:T(2,128)S(1)} collective-permute-done((s32[2,8]{1,0:T(2,128)S(1)}, s32[2,8]{1,0:T(2,128)S(1)}, u32[]{:S(2)}, u32[]{:S(2)}) %collective-permute-start.1) | collective-permute-done | bytes 96 | tf_op jit(solution)/shard_map/ppermute | solution.py:457
  26.9 0.0 collective-permute-done
  26.9 0.0 copy-start.2
  26.9 1.9 %collective-permute-start.3 = (s32[8,8]{1,0:T(8,128)S(1)}, s32[8,8]{1,0:T(8,128)S(1)}, u32[]{:S(2)}, u32[]{:S(2)}) collective-permute-start(s32[8,8]{1,0:T(8,128)S(1)} %pad_add_fusion.own), channel_id=1, source_target_pairs={{0,1},{1,2},{2,3},{3,4},{4,5},{5,6},{6,7},{7,8},{8,9},{9,10},{10,1... | collective-permute-start | bytes 776 | tf_op jit(solution)/shard_map/ppermute | solution.py:475
  28.8 5.1 %collective-permute-done.3.before = s32[8,8]{1,0:T(8,128)S(1)} collective-permute-done((s32[8,8]{1,0:T(8,128)S(1)}, s32[8,8]{1,0:T(8,128)S(1)}, u32[]{:S(2)}, u32[]{:S(2)}) %collective-permute-start.3) | collective-permute-done | bytes 288 | tf_op jit(solution)/shard_map/ppermute | solution.py:475
  34.0 0.0 copy-done.2
  34.0 0.0 copy-start.3
  34.0 0.6 copy-done.3
  34.5 2.0 %plan.1 = s32[256]{0:T(256)} custom-call(s32[8,8]{1,0:T(8,128)} %copy-done.2, s32[8,8]{1,0:T(8,128)} %copy-done.3), custom_call_target="tpu_custom_call" | custom-call | flops 1 | bytes 1 | tf_op jit(solution)/shard_map/plan/pallas_call | solution.py:263
  36.5 0.0 collective-permute-done.4.got_ext
  36.5 0.0 collective-permute-done.5.got_int
  36.6 0.0 copy-done
  36.6 0.0 copy-start.1
  36.6 0.7 copy-done.1
  37.2 5.1 %correlate.1 = (f32[848,128]{1,0:T(8,128)S(1)}, bf16[848,128]{1,0:T(8,128)(2,1)S(1)}, bf16[848,128]{1,0:T(8,128)(2,1)S(1)}, bf16[848,128]{1,0:T(8,128)(2,1)S(1)}) custom-call(s32[256]{0:T(256)S(1)} %copy-done.1, bf16[4,3,128,512]{3,2,1,0:T(8,128)(2,1)S(1)} %whiten.3.own_ext, bf16[4,3,128,512]{3,2,1,0:T(8,128)(2,1)S(1)} %whiten.2.own_int, ...), custom_call_target="tpu_custom_call" | custom-call | flops 1 | bytes 1 | tf_op jit(solution)/shard_map/correlate/pallas_call | solution.py:345
  42.3 2.1 %collective-permute-start.6 = (bf16[848,128]{1,0:T(8,128)(2,1)S(1)}, bf16[848,128]{1,0:T(8,128)(2,1)S(1)}, u32[]{:S(2)}, u32[]{:S(2)}) collective-permute-start(bf16[848,128]{1,0:T(8,128)(2,1)S(1)} %get-tuple-element.16), channel_id=1, source_target_pairs={{0,64},{32,96},{64,0},{96,32},{1,65},{33,97},{65,1},{97,33},{2,66}... | collective-permute-start | bytes 651272 | tf_op jit(solution)/shard_map/ppermute | solution.py:457
  44.4 0.0 collective-permute-start.7
  44.4 3.2 %collective-permute-start.8 = (bf16[848,128]{1,0:T(8,128)(2,1)S(1)}, bf16[848,128]{1,0:T(8,128)(2,1)S(1)}, u32[]{:S(2)}, u32[]{:S(2)}) collective-permute-start(bf16[848,128]{1,0:T(8,128)(2,1)S(1)} %get-tuple-element.18), channel_id=1, source_target_pairs={{0,96},{32,0},{64,32},{96,64},{1,97},{33,1},{65,33},{97,65},{2,98}... | collective-permute-start | bytes 651272 | tf_op jit(solution)/shard_map/ppermute | solution.py:457
  47.7 3.0 %collective-permute-done.6.got2 = bf16[848,128]{1,0:T(8,128)(2,1)S(1)} collective-permute-done((bf16[848,128]{1,0:T(8,128)(2,1)S(1)}, bf16[848,128]{1,0:T(8,128)(2,1)S(1)}, u32[]{:S(2)}, u32[]{:S(2)}) %collective-permute-start.6) | collective-permute-done | bytes 217120 | tf_op jit(solution)/shard_map/ppermute | solution.py:457
  50.7 2.2 %collective-permute-done.7.got1 = bf16[848,128]{1,0:T(8,128)(2,1)S(1)} collective-permute-done((bf16[848,128]{1,0:T(8,128)(2,1)S(1)}, bf16[848,128]{1,0:T(8,128)(2,1)S(1)}, u32[]{:S(2)}, u32[]{:S(2)}) %collective-permute-start.7) | collective-permute-done | bytes 217120 | tf_op jit(solution)/shard_map/ppermute | solution.py:457
  52.9 0.0 collective-permute-done.8.got3
  52.9 0.7 %combine.1 = (f32[848,128]{1,0:T(8,128)S(1)}, bf16[528,128]{1,0:T(8,128)(2,1)S(1)}, bf16[272,128]{1,0:T(8,128)(2,1)S(1)}, bf16[272,128]{1,0:T(8,128)(2,1)S(1)}, bf16[272,128]{1,0:T(8,128)(2,1)S(1)}) custom-call(s32[256]{0:T(256)S(1)} %copy-done.1, f32[848,128]{1,0:T(8,128)S(1)} %get-tuple-element.15.keep, bf16[848,128]{1,0:T(8,128)(2,1)S(1)} %collective-permute-done.6.got2, ...), custom_call_target="tpu_custom_call" | custom-call | flops 1 | bytes 1 | tf_op jit(solution)/shard_map/combine/pallas_call | solution.py:394
  53.6 1.9 %collective-permute-start.9 = (bf16[528,128]{1,0:T(8,128)(2,1)S(1)}, bf16[528,128]{1,0:T(8,128)(2,1)S(1)}, u32[]{:S(2)}, u32[]{:S(2)}) collective-permute-start(bf16[528,128]{1,0:T(8,128)(2,1)S(1)} %get-tuple-element.20), channel_id=1, source_target_pairs={{0,1},{1,2},{2,3},{3,4},{4,5},{5,6},{6,7},{7,8},{8,9},{9,10},{10,1... | collective-permute-start | bytes 405512 | tf_op jit(solution)/shard_map/ppermute | solution.py:479
  55.5 4.3 %collective-permute-start.10 = (bf16[272,128]{1,0:T(8,128)(2,1)S(1)}, bf16[272,128]{1,0:T(8,128)(2,1)S(1)}, u32[]{:S(2)}, u32[]{:S(2)}) collective-permute-start(bf16[272,128]{1,0:T(8,128)(2,1)S(1)} %get-tuple-element.21), channel_id=1, source_target_pairs={{0,64},{32,96},{64,0},{96,32},{1,65},{33,97},{65,1},{97,33},{2,66}... | collective-permute-start | bytes 208904 | tf_op jit(solution)/shard_map/ppermute | solution.py:457
  59.9 0.2 collective-permute-start.11
  60.1 3.0 %collective-permute-start.12 = (bf16[272,128]{1,0:T(8,128)(2,1)S(1)}, bf16[272,128]{1,0:T(8,128)(2,1)S(1)}, u32[]{:S(2)}, u32[]{:S(2)}) collective-permute-start(bf16[272,128]{1,0:T(8,128)(2,1)S(1)} %get-tuple-element.23), channel_id=1, source_target_pairs={{0,96},{32,0},{64,32},{96,64},{1,97},{33,1},{65,33},{97,65},{2,98}... | collective-permute-start | bytes 208904 | tf_op jit(solution)/shard_map/ppermute | solution.py:457
  63.1 0.0 collective-permute-done.10.got2
  63.1 2.3 %collective-permute-done.11.got1 = bf16[272,128]{1,0:T(8,128)(2,1)S(1)} collective-permute-done((bf16[272,128]{1,0:T(8,128)(2,1)S(1)}, bf16[272,128]{1,0:T(8,128)(2,1)S(1)}, u32[]{:S(2)}, u32[]{:S(2)}) %collective-permute-start.11) | collective-permute-done | bytes 69664 | tf_op jit(solution)/shard_map/ppermute | solution.py:457
  65.4 0.0 collective-permute-done.12.got3
  65.4 0.0 collective-permute-done.9.shifted
  65.4 1.8 %finish.1 = (f32[2,65,8,128]{3,2,1,0:T(8,128)}, f32[2,65,8,128]{3,2,1,0:T(8,128)}) custom-call(s32[256]{0:T(256)S(1)} %copy-done.1, f32[848,128]{1,0:T(8,128)S(1)} %get-tuple-element.19.full, bf16[528,128]{1,0:T(8,128)(2,1)S(1)} %collective-permute-done.9.shifted, bf16[272,128]{1,0:T(8,128)(2,1)S(1)} %collective-permute-done.10.got2, ...), custom_call_target="tpu_custom_call" | custom-call | flops 1 | bytes 1 | tf_op jit(solution)/shard_map/finish/pallas_call | solution.py:443
  (1 shorter events, 0.0 us)
Async XLA Ops:
  6.7 10.9 %copy-start.4 = (s32[2,8]{1,0:T(2,128)S(1)}, s32[2,8]{1,0:T(2,128)}, u32[]{:S(2)}) copy-start(s32[2,8]{1,0:T(2,128)} %param.4) | copy-start | bytes 196
  6.7 29.8 %copy-start = (bf16[512,256]{1,0:T(8,128)(2,1)S(1)}, bf16[512,256]{1,0:T(8,128)(2,1)}, u32[]{:S(2)}) copy-start(bf16[512,256]{1,0:T(8,128)(2,1)} %constant.2.clone.lag) | copy-start | bytes 786436
  6.8 29.8 %collective-permute-start.4 = (bf16[4,3,128,512]{3,2,1,0:T(8,128)(2,1)S(1)}, bf16[4,3,128,512]{3,2,1,0:T(8,128)(2,1)}, u32[]{:S(2)}, u32[]{:S(2)}) collective-permute-start(bf16[4,3,128,512]{3,2,1,0:T(8,128)(2,1)S(1)} %whiten.3.own_ext), channel_id=1, source_target_pairs={{1,2},{2,1},{3,4},{4,3},{5,6},{6,5},{7,8},{8,7},{9,10},{10,9},{11,... | collective-permute-start | bytes 4718600 | tf_op jit(solution)/shard_map/ppermute | solution.py:470
  17.6 19.0 %collective-permute-start.5 = (bf16[4,3,128,512]{3,2,1,0:T(8,128)(2,1)S(1)}, bf16[4,3,128,512]{3,2,1,0:T(8,128)(2,1)}, u32[]{:S(2)}, u32[]{:S(2)}) collective-permute-start(bf16[4,3,128,512]{3,2,1,0:T(8,128)(2,1)S(1)} %whiten.2.own_int), channel_id=1, source_target_pairs={{0,1},{1,0},{2,3},{3,2},{4,5},{5,4},{6,7},{7,6},{8,9},{9,8},{10,11... | collective-permute-start | bytes 4718600 | tf_op jit(solution)/shard_map/ppermute | solution.py:472
  17.7 5.4 %collective-permute-start.2 = (s32[2,8]{1,0:T(2,128)S(1)}, s32[2,8]{1,0:T(2,128)S(1)}, u32[]{:S(2)}, u32[]{:S(2)}) collective-permute-start(s32[2,8]{1,0:T(2,128)S(1)} %copy-done.4), channel_id=1, source_target_pairs={{0,96},{32,0},{64,32},{96,64},{1,97},{33,1},{65,33},{97,65},{2,98}... | collective-permute-start | bytes 200 | tf_op jit(solution)/shard_map/ppermute | solution.py:457
  21.8 5.1 %collective-permute-start.1 = (s32[2,8]{1,0:T(2,128)S(1)}, s32[2,8]{1,0:T(2,128)S(1)}, u32[]{:S(2)}, u32[]{:S(2)}) collective-permute-start(s32[2,8]{1,0:T(2,128)S(1)} %copy-done.4), channel_id=1, source_target_pairs={{0,64},{32,96},{64,0},{96,32},{1,65},{33,97},{65,1},{97,33},{2,66}... | collective-permute-start | bytes 200 | tf_op jit(solution)/shard_map/ppermute | solution.py:457
  21.8 5.1 %collective-permute-start = (s32[2,8]{1,0:T(2,128)S(1)}, s32[2,8]{1,0:T(2,128)S(1)}, u32[]{:S(2)}, u32[]{:S(2)}) collective-permute-start(s32[2,8]{1,0:T(2,128)S(1)} %copy-done.4), channel_id=1, source_target_pairs={{0,32},{32,64},{64,96},{96,0},{1,33},{33,65},{65,97},{97,1},{2,34}... | collective-permute-start | bytes 200 | tf_op jit(solution)/shard_map/ppermute | solution.py:457
  26.9 7.1 %copy-start.2 = (s32[8,8]{1,0:T(8,128)}, s32[8,8]{1,0:T(8,128)S(1)}, u32[]{:S(2)}) copy-start(s32[8,8]{1,0:T(8,128)S(1)} %pad_add_fusion.own) | copy-start | bytes 772
  26.9 7.0 %collective-permute-start.3 = (s32[8,8]{1,0:T(8,128)S(1)}, s32[8,8]{1,0:T(8,128)S(1)}, u32[]{:S(2)}, u32[]{:S(2)}) collective-permute-start(s32[8,8]{1,0:T(8,128)S(1)} %pad_add_fusion.own), channel_id=1, source_target_pairs={{0,1},{1,2},{2,3},{3,4},{4,5},{5,6},{6,7},{7,8},{8,9},{9,10},{10,1... | collective-permute-start | bytes 776 | tf_op jit(solution)/shard_map/ppermute | solution.py:475
  34.0 0.6 copy-start.3
  36.6 0.7 %copy-start.1 = (s32[256]{0:T(256)S(1)}, s32[256]{0:T(256)}, u32[]{:S(2)}) copy-start(s32[256]{0:T(256)} %plan.1) | copy-start | bytes 3076
  42.3 8.3 %collective-permute-start.6 = (bf16[848,128]{1,0:T(8,128)(2,1)S(1)}, bf16[848,128]{1,0:T(8,128)(2,1)S(1)}, u32[]{:S(2)}, u32[]{:S(2)}) collective-permute-start(bf16[848,128]{1,0:T(8,128)(2,1)S(1)} %get-tuple-element.16), channel_id=1, source_target_pairs={{0,64},{32,96},{64,0},{96,32},{1,65},{33,97},{65,1},{97,33},{2,66}... | collective-permute-start | bytes 651272 | tf_op jit(solution)/shard_map/ppermute | solution.py:457
  44.4 8.4 %collective-permute-start.7 = (bf16[848,128]{1,0:T(8,128)(2,1)S(1)}, bf16[848,128]{1,0:T(8,128)(2,1)S(1)}, u32[]{:S(2)}, u32[]{:S(2)}) collective-permute-start(bf16[848,128]{1,0:T(8,128)(2,1)S(1)} %get-tuple-element.17), channel_id=1, source_target_pairs={{0,32},{32,64},{64,96},{96,0},{1,33},{33,65},{65,97},{97,1},{2,34}... | collective-permute-start | bytes 651272 | tf_op jit(solution)/shard_map/ppermute | solution.py:457
  44.4 8.4 %collective-permute-start.8 = (bf16[848,128]{1,0:T(8,128)(2,1)S(1)}, bf16[848,128]{1,0:T(8,128)(2,1)S(1)}, u32[]{:S(2)}, u32[]{:S(2)}) collective-permute-start(bf16[848,128]{1,0:T(8,128)(2,1)S(1)} %get-tuple-element.18), channel_id=1, source_target_pairs={{0,96},{32,0},{64,32},{96,64},{1,97},{33,1},{65,33},{97,65},{2,98}... | collective-permute-start | bytes 651272 | tf_op jit(solution)/shard_map/ppermute | solution.py:457
  53.6 11.8 %collective-permute-start.9 = (bf16[528,128]{1,0:T(8,128)(2,1)S(1)}, bf16[528,128]{1,0:T(8,128)(2,1)S(1)}, u32[]{:S(2)}, u32[]{:S(2)}) collective-permute-start(bf16[528,128]{1,0:T(8,128)(2,1)S(1)} %get-tuple-element.20), channel_id=1, source_target_pairs={{0,1},{1,2},{2,3},{3,4},{4,5},{5,6},{6,7},{7,8},{8,9},{9,10},{10,1... | collective-permute-start | bytes 405512 | tf_op jit(solution)/shard_map/ppermute | solution.py:479
  55.5 7.6 %collective-permute-start.10 = (bf16[272,128]{1,0:T(8,128)(2,1)S(1)}, bf16[272,128]{1,0:T(8,128)(2,1)S(1)}, u32[]{:S(2)}, u32[]{:S(2)}) collective-permute-start(bf16[272,128]{1,0:T(8,128)(2,1)S(1)} %get-tuple-element.21), channel_id=1, source_target_pairs={{0,64},{32,96},{64,0},{96,32},{1,65},{33,97},{65,1},{97,33},{2,66}... | collective-permute-start | bytes 208904 | tf_op jit(solution)/shard_map/ppermute | solution.py:457
  59.9 5.5 %collective-permute-start.11 = (bf16[272,128]{1,0:T(8,128)(2,1)S(1)}, bf16[272,128]{1,0:T(8,128)(2,1)S(1)}, u32[]{:S(2)}, u32[]{:S(2)}) collective-permute-start(bf16[272,128]{1,0:T(8,128)(2,1)S(1)} %get-tuple-element.22), channel_id=1, source_target_pairs={{0,32},{32,64},{64,96},{96,0},{1,33},{33,65},{65,97},{97,1},{2,34}... | collective-permute-start | bytes 208904 | tf_op jit(solution)/shard_map/ppermute | solution.py:457
  60.1 5.3 %collective-permute-start.12 = (bf16[272,128]{1,0:T(8,128)(2,1)S(1)}, bf16[272,128]{1,0:T(8,128)(2,1)S(1)}, u32[]{:S(2)}, u32[]{:S(2)}) collective-permute-start(bf16[272,128]{1,0:T(8,128)(2,1)S(1)} %get-tuple-element.23), channel_id=1, source_target_pairs={{0,96},{32,0},{64,32},{96,64},{1,97},{33,1},{65,33},{97,65},{2,98}... | collective-permute-start | bytes 208904 | tf_op jit(solution)/shard_map/ppermute | solution.py:457

commit v5 on v4

--- a/solution.py
+++ b/solution.py
@@ -100,7 +100,8 @@
             tab[2 * LENGTH + 16 * a : 2 * LENGTH + 16 * a + 16, k * BINS : (k + 1) * BINS] = low
 
 
-def whiten_body(outer, records, white, buf, tab, sems):
+def whiten_body(outer, after, records, white, buf, tab, sems):
+    del after
     segs = records.shape[0]
     core = jnp.bitwise_and(lax.axis_index("blk"), 1)
     begin = pl.multiple_of((core if outer else 1 - core) * ROWS, ROWS)
@@ -149,11 +150,11 @@
     lax.fori_loop(0, segs, step, 0)
 
 
-def whiten(outer, records):
+def whiten(outer, after, records):
     segs = records.shape[0]
     return pl.pallas_call(
         functools.partial(whiten_body, outer),
-        in_specs=[pl.BlockSpec(memory_space=pltpu.HBM)],
+        in_specs=[SMEM, pl.BlockSpec(memory_space=pltpu.HBM)],
         out_specs=VMEM,
         out_shape=jax.ShapeDtypeStruct((HALF, segs, CHANS, LENGTH), BF),
         scratch_shapes=[
@@ -164,7 +165,7 @@
         compiler_params=pltpu.CompilerParams(vmem_limit_bytes=50 * MIB),
         cost_estimate=TINY,
         name="whiten",
-    )(records)
+    )(after, records)
 
 
 VISITS = [(p, d) for p in range(HALF) for d in range(1, REACH + 1) if p + d >= HALF] + [
@@ -176,20 +177,20 @@
 )
 
 
-def plan_body(own, before, plan, slots):
+def plan_body(pairs, plan, slots):
     s = lax.axis_index("seg").astype(jnp.int32)
     plan[SEG] = s
     zero = jnp.int32(0)
 
-    def behind(owner):
-        return 2 * jnp.bitwise_and(s - owner, 3)
+    def look(row, before, d):
+        return pairs[4 * (row // 2) + row % 2 + 2 * before, d - 1]
 
     used = [zero] * PLANES
     n = zero
     for p, d in VISITS:
         row = p + HALF if p < HALF else p - HALF
         owner = row // 2
-        live = (before if p < HALF else own)[behind(owner) + row % 2, d - 1]
+        live = look(row, int(p < HALF), d)
         code = p + d * 16 + jnp.bitwise_and(owner - s, 3) * 256 + used[owner] * 4096
         slots[p * REACH + d - 1] = used[owner]
         used[owner] = used[owner] + live
@@ -207,7 +208,7 @@
             p, d = HALF + i, GROUP + j - i
             entry = p * REACH + d - 1 if i // 2 == owner else 96 + (i - 2) * 2 + j
             plan[MOVES + n] = slots[entry] + k * 4096
-            n = n + jnp.where(s == owner, own[behind(i // 2) + i % 2, d - 1], 0)
+            n = n + jnp.where(s == owner, look(i, 0, d), 0)
     for r in range(1, PLANES):
         to = jnp.bitwise_and(s + r, 3)
         ahead = s < to
@@ -216,7 +217,7 @@
                 row = 2 * s + i
                 p = jnp.where(ahead, row + HALF, jnp.maximum(row - HALF, 0))
                 d = 2 * to + j - row + jnp.where(ahead, 0, GROUP)
-                live = jnp.where(ahead, own[i, d - 1], jnp.where(s >= 2, before[i, d - 1], 0))
+                live = jnp.where(ahead, pairs[4 * s + i, d - 1], jnp.where(s >= 2, pairs[4 * s + 2 + i, d - 1], 0))
                 plan[MOVES + n] = slots[p * REACH + d - 1] + r * 256 + (2 * i + j) * 4096
                 n = n + live
     plan[1] = n
@@ -229,7 +230,7 @@
     for i in range(2):
         for d in range(1, REACH + 1):
             row = 2 * s + i
-            live = own[i, d - 1]
+            live = pairs[4 * s + i, d - 1]
             shift = (row + d >= GROUP) & (s >= 2)
             slot = jnp.where(shift, above, slots[(HALF + row) * REACH + d - 1])
             write(n, i, d, jnp.where(shift, TWO, 0), jnp.where(shift, SHIFTED, SLOTS), slot)
@@ -242,8 +243,7 @@
             crossing = low < 0
             row = jnp.where(crossing, low + GROUP, low)
             owner = jnp.right_shift(row, 1)
-            at = behind(owner) + jnp.bitwise_and(row, 1)
-            live = jnp.where(crossing, before[at, d - 1], own[at, d - 1])
+            live = pairs[4 * owner + jnp.bitwise_and(row, 1) + jnp.where(crossing, 2, 0), d - 1]
             up = crossing & (owner < 2)
             mine = (owner == s) & jnp.logical_not(up)
             k0 = jnp.where(row == 0, 0, 2 * row - 1) + j
@@ -259,16 +259,16 @@
     plan[3] = n
 
 
-def make_plan(own, before):
+def make_plan(pairs):
     return pl.pallas_call(
         plan_body,
-        in_specs=[SMEM, SMEM],
+        in_specs=[SMEM],
         out_specs=SMEM,
         out_shape=jax.ShapeDtypeStruct((PLAN,), jnp.int32),
         scratch_shapes=[pltpu.SMEM((128,), jnp.int32)],
         cost_estimate=TINY,
         name="plan",
-    )(own, before)
+    )(pairs)
 
 
 def correlate_body(plan, own_ext, own_int, got_ext, got_int, lag, keep, out1, out2, out3, low, high, stk, pq, last):
@@ -466,14 +466,18 @@
         for step in (1 if z < 2 else -1,)
         if 0 <= g + step < groups
     ]
-    own_ext = whiten(True, records)
+    before = lax.ppermute(pairs, "blk", upward)
+    both = jnp.concatenate([pairs, before]).astype(F32)
+    both = lax.optimization_barrier(jnp.broadcast_to(both[:, :, None, None], (4, REACH, 8, CHANS)))
+    both = lax.all_gather(both, "seg", axis=0, tiled=True)
+    both = both[:, :, 0, 0].astype(jnp.int32)
+
+    own_ext = whiten(True, before, records)
     got_ext = lax.ppermute(own_ext, "blk", outer)
-    own_int = whiten(False, records)
+    own_int = whiten(False, before, records)
+    own_int, both = lax.optimization_barrier((own_int, both))
     got_int = lax.ppermute(own_int, "blk", inner)
-    rows, _ = lax.optimization_barrier((pairs, own_int))
-    own = jnp.concatenate([rows, ring(rows, 1), ring(rows, 2), ring(rows, 3)])
-    plan = make_plan(own, lax.ppermute(own, "blk", upward))
-
+    plan = make_plan(both)
     keep, out1, out2, out3 = correlate(plan, (own_ext, own_int, got_ext, got_int), lag)
     full, send, out1, out2, out3 = combine(plan, keep, ring(out2, 2), ring(out1, 1), ring(out3, 3))
     shifted = lax.ppermute(send, ("seg", "blk"), shift)

time: 67.5 us -> 93.3 us (1.38)
  waiting for transfers between devices: 16.4 us -> 34.6 us
  blocking collectives: 0 us -> 14.7 us
  starting transfers between devices: 27 us -> 17.7 us
  Pallas kernels: 21.7 us -> 23.2 us
    ppermute x1, waiting for transfers between devices: 0.01 us -> 18.5 us  [shards(): got_ext = lax.ppermute(own_ext, 'blk', outer)]
    all_gather x0 -> x1, blocking collectives: none -> 14.7 us  [shards(): both = lax.all_gather(both, 'seg', axis=0, tiled=True)]
    ppermute x9 -> x6, starting transfers between devices: 18.3 us -> 11 us  [ring(): lax.ppermute(x, 'seg', [(z, (z + r) % planes) for z in range(planes)])]
    ppermute x1, starting transfers between devices: 4.75 us -> 2.78 us  [shards(): got_ext = lax.ppermute(own_ext, 'blk', outer)]
    pallas_call x3, Pallas kernels: 14.1 us -> 15.2 us  [the longest x2 13.2 us: whiten(): pl.pallas_call(functools.partial(whiten_body, outer), in_specs=[SMEM, pl....]
    ppermute x9 -> x6, waiting for transfers between devices: 11.3 us -> 10.8 us  [ring(): lax.ppermute(x, 'seg', [(z, (z + r) % planes) for z in range(planes)])]
  transfers between devices with their start and end apart: 13 -> 10, of which waited for: 5 -> 7; matrix products, arithmetic and copies ran while one was open for 0% -> 1% of each run, Pallas kernels for 12% -> 9%
where the time goes in v5:
time: 93.3 us; the launch traced here: 93.2 us
  waiting for transfers between devices  34.6 us (37%)
  Pallas kernels  23.2 us (25%)
  starting transfers between devices  17.7 us (19%)
  blocking collectives  14.7 us (16%)
  local copies, waits for them, and re-layouts  1.6 us (2%)
    ppermute x1, waiting for transfers between devices, shards(): got_ext = lax.ppermute(own_ext, 'blk', outer)  18.5 us
    all_gather x1, blocking collectives, shards(): both = lax.all_gather(both, 'seg', axis=0, tiled=True)  14.7 us
    pallas_call x2, Pallas kernels, whiten(): pl.pallas_call(functools.partial(whiten_body, outer), in_specs=[SMEM, pl....  13.2 us
    ppermute x6, starting transfers between devices, ring(): lax.ppermute(x, 'seg', [(z, (z + r) % planes) for z in range(planes)])  11 us
    ppermute x6, waiting for transfers between devices, ring(): lax.ppermute(x, 'seg', [(z, (z + r) % planes) for z in range(planes)])  10.8 us
    pallas_call x1, Pallas kernels, correlate(): pl.pallas_call(correlate_body, in_specs=[SMEM] + [VMEM] * 5, out_specs=[V...  5.53 us
    ppermute x1, waiting for transfers between devices, shards(): before = lax.ppermute(pairs, 'blk', upward)  5.28 us
    ppermute x1, starting transfers between devices, shards(): got_ext = lax.ppermute(own_ext, 'blk', outer)  2.78 us
  transfers between devices with their start and end apart: 10, of which 7 were waited for; matrix products, arithmetic and copies ran while one was open for 1% of the time, Pallas kernels for 9%

profile of v5, /device:TPU:6, one launch (start us, length us, event | category | flops | bytes accessed | tf_op | source)
XLA Modules:
  0.0 93.2 jit_solution(6356916514991757259)
XLA Ops:
  0.6 1.9 %collective-permute-start = (s32[2,8]{1,0:T(2,128)}, s32[2,8]{1,0:T(2,128)S(1)}, u32[]{:S(2)}, u32[]{:S(2)}) collective-permute-start(s32[2,8]{1,0:T(2,128)} %param.4), channel_id=1, source_target_pairs={{0,1},{1,2},{2,3},{3,4},{4,5},{5,6},{6,7},{7,8},{8,9},{9,10},{10,1... | collective-permute-start | bytes 200 | tf_op jit(solution)/shard_map/ppermute | solution.py:469
  2.6 5.3 %collective-permute-done.after = s32[2,8]{1,0:T(2,128)S(1)} collective-permute-done((s32[2,8]{1,0:T(2,128)}, s32[2,8]{1,0:T(2,128)S(1)}, u32[]{:S(2)}, u32[]{:S(2)}) %collective-permute-start) | collective-permute-done | bytes 96 | tf_op jit(solution)/shard_map/ppermute | solution.py:469
  7.8 0.7 add_convert_fusion
  8.5 0.1 broadcast_in_dim.2
  8.6 14.7 %all_gather.3 = f32[16,8,8,128]{3,2,1,0:T(8,128)S(1)} all-gather(f32[4,8,8,128]{3,2,1,0:T(8,128)S(1)} %broadcast_in_dim.2), channel_id=1, replica_groups=mesh['seg'=4,'blk'=32] {'seg'}, dimensions={0}, use_global_device_ids=true | all-gather | bytes 655360 | tf_op jit(solution)/shard_map/all_gather | solution.py:472
  23.3 0.1 copy.9
  23.5 6.6 %whiten.2.own_int = bf16[4,3,128,512]{3,2,1,0:T(8,128)(2,1)S(1)} custom-call(s32[2,8]{1,0:T(2,128)S(1)} %collective-permute-done.after, f32[3,1024,512]{2,1,0:T(8,128)} %records.3), custom_call_target="tpu_custom_call" | custom-call | flops 1 | bytes 1 | tf_op jit(solution)/shard_map/whiten/pallas_call | solution.py:155
  30.1 0.0 copy-start
  30.1 0.1 collective-permute-start.2
  30.2 6.6 %whiten.3.own_ext = bf16[4,3,128,512]{3,2,1,0:T(8,128)(2,1)S(1)} custom-call(s32[2,8]{1,0:T(2,128)S(1)} %collective-permute-done.after, f32[3,1024,512]{2,1,0:T(8,128)} %records.3), custom_call_target="tpu_custom_call" | custom-call | flops 1 | bytes 1 | tf_op jit(solution)/shard_map/whiten/pallas_call | solution.py:155
  36.8 2.8 %collective-permute-start.1 = (bf16[4,3,128,512]{3,2,1,0:T(8,128)(2,1)S(1)}, bf16[4,3,128,512]{3,2,1,0:T(8,128)(2,1)}, u32[]{:S(2)}, u32[]{:S(2)}) collective-permute-start(bf16[4,3,128,512]{3,2,1,0:T(8,128)(2,1)S(1)} %whiten.3.own_ext), channel_id=1, source_target_pairs={{1,2},{2,1},{3,4},{4,3},{5,6},{6,5},{7,8},{8,7},{9,10},{10,9},{11,... | collective-permute-start | bytes 4718600 | tf_op jit(solution)/shard_map/ppermute | solution.py:476
  39.6 0.7 copy.8.pairs
  40.3 2.0 %plan.1 = s32[256]{0:T(256)} custom-call(s32[16,8]{1,0:T(8,128)} %copy.8.pairs), custom_call_target="tpu_custom_call" | custom-call | flops 1 | bytes 1 | tf_op jit(solution)/shard_map/plan/pallas_call | solution.py:263
  42.3 0.0 collective-permute-done.2.got_int
  42.3 18.5 %collective-permute-done.1.got_ext = bf16[4,3,128,512]{3,2,1,0:T(8,128)(2,1)} collective-permute-done((bf16[4,3,128,512]{3,2,1,0:T(8,128)(2,1)S(1)}, bf16[4,3,128,512]{3,2,1,0:T(8,128)(2,1)}, u32[]{:S(2)}, u32[]{:S(2)}) %collective-permute-start.1) | collective-permute-done | bytes 1572896 | tf_op jit(solution)/shard_map/ppermute | solution.py:476
  60.8 0.0 copy-done
  60.8 0.0 copy-start.1
  60.8 0.7 copy-done.1
  61.5 5.5 %correlate.1 = (f32[848,128]{1,0:T(8,128)S(1)}, bf16[848,128]{1,0:T(8,128)(2,1)S(1)}, bf16[848,128]{1,0:T(8,128)(2,1)S(1)}, bf16[848,128]{1,0:T(8,128)(2,1)S(1)}) custom-call(s32[256]{0:T(256)S(1)} %copy-done.1, bf16[4,3,128,512]{3,2,1,0:T(8,128)(2,1)S(1)} %whiten.3.own_ext, bf16[4,3,128,512]{3,2,1,0:T(8,128)(2,1)S(1)} %whiten.2.own_int, ...), custom_call_target="tpu_custom_call" | custom-call | flops 1 | bytes 1 | tf_op jit(solution)/shard_map/correlate/pallas_call | solution.py:345
  67.0 1.6 %collective-permute-start.3 = (bf16[848,128]{1,0:T(8,128)(2,1)S(1)}, bf16[848,128]{1,0:T(8,128)(2,1)S(1)}, u32[]{:S(2)}, u32[]{:S(2)}) collective-permute-start(bf16[848,128]{1,0:T(8,128)(2,1)S(1)} %get-tuple-element.18), channel_id=1, source_target_pairs={{0,64},{32,96},{64,0},{96,32},{1,65},{33,97},{65,1},{97,33},{2,66}... | collective-permute-start | bytes 651272 | tf_op jit(solution)/shard_map/ppermute | solution.py:457
  68.6 1.6 %collective-permute-start.4 = (bf16[848,128]{1,0:T(8,128)(2,1)S(1)}, bf16[848,128]{1,0:T(8,128)(2,1)S(1)}, u32[]{:S(2)}, u32[]{:S(2)}) collective-permute-start(bf16[848,128]{1,0:T(8,128)(2,1)S(1)} %get-tuple-element.19), channel_id=1, source_target_pairs={{0,32},{32,64},{64,96},{96,0},{1,33},{33,65},{65,97},{97,1},{2,34}... | collective-permute-start | bytes 651272 | tf_op jit(solution)/shard_map/ppermute | solution.py:457
  70.1 1.7 %collective-permute-start.5 = (bf16[848,128]{1,0:T(8,128)(2,1)S(1)}, bf16[848,128]{1,0:T(8,128)(2,1)S(1)}, u32[]{:S(2)}, u32[]{:S(2)}) collective-permute-start(bf16[848,128]{1,0:T(8,128)(2,1)S(1)} %get-tuple-element.20), channel_id=1, source_target_pairs={{0,96},{32,0},{64,32},{96,64},{1,97},{33,1},{65,33},{97,65},{2,98}... | collective-permute-start | bytes 651272 | tf_op jit(solution)/shard_map/ppermute | solution.py:457
  71.8 5.1 %collective-permute-done.3.got2 = bf16[848,128]{1,0:T(8,128)(2,1)S(1)} collective-permute-done((bf16[848,128]{1,0:T(8,128)(2,1)S(1)}, bf16[848,128]{1,0:T(8,128)(2,1)S(1)}, u32[]{:S(2)}, u32[]{:S(2)}) %collective-permute-start.3) | collective-permute-done | bytes 217120 | tf_op jit(solution)/shard_map/ppermute | solution.py:457
  76.9 3.1 %collective-permute-done.4.got1 = bf16[848,128]{1,0:T(8,128)(2,1)S(1)} collective-permute-done((bf16[848,128]{1,0:T(8,128)(2,1)S(1)}, bf16[848,128]{1,0:T(8,128)(2,1)S(1)}, u32[]{:S(2)}, u32[]{:S(2)}) %collective-permute-start.4) | collective-permute-done | bytes 217120 | tf_op jit(solution)/shard_map/ppermute | solution.py:457
  80.0 0.0 collective-permute-done.5.got3
  80.0 0.7 combine.1
  80.8 1.9 %collective-permute-start.6 = (bf16[528,128]{1,0:T(8,128)(2,1)S(1)}, bf16[528,128]{1,0:T(8,128)(2,1)S(1)}, u32[]{:S(2)}, u32[]{:S(2)}) collective-permute-start(bf16[528,128]{1,0:T(8,128)(2,1)S(1)} %get-tuple-element.22), channel_id=1, source_target_pairs={{0,1},{1,2},{2,3},{3,4},{4,5},{5,6},{6,7},{7,8},{8,9},{9,10},{10,1... | collective-permute-start | bytes 405512 | tf_op jit(solution)/shard_map/ppermute | solution.py:483
  82.7 3.0 %collective-permute-start.7 = (bf16[272,128]{1,0:T(8,128)(2,1)S(1)}, bf16[272,128]{1,0:T(8,128)(2,1)S(1)}, u32[]{:S(2)}, u32[]{:S(2)}) collective-permute-start(bf16[272,128]{1,0:T(8,128)(2,1)S(1)} %get-tuple-element.23), channel_id=1, source_target_pairs={{0,64},{32,96},{64,0},{96,32},{1,65},{33,97},{65,1},{97,33},{2,66}... | collective-permute-start | bytes 208904 | tf_op jit(solution)/shard_map/ppermute | solution.py:457
  85.7 1.5 %collective-permute-start.8 = (bf16[272,128]{1,0:T(8,128)(2,1)S(1)}, bf16[272,128]{1,0:T(8,128)(2,1)S(1)}, u32[]{:S(2)}, u32[]{:S(2)}) collective-permute-start(bf16[272,128]{1,0:T(8,128)(2,1)S(1)} %get-tuple-element.24), channel_id=1, source_target_pairs={{0,32},{32,64},{64,96},{96,0},{1,33},{33,65},{65,97},{97,1},{2,34}... | collective-permute-start | bytes 208904 | tf_op jit(solution)/shard_map/ppermute | solution.py:457
  87.1 1.8 %collective-permute-start.9 = (bf16[272,128]{1,0:T(8,128)(2,1)S(1)}, bf16[272,128]{1,0:T(8,128)(2,1)S(1)}, u32[]{:S(2)}, u32[]{:S(2)}) collective-permute-start(bf16[272,128]{1,0:T(8,128)(2,1)S(1)} %get-tuple-element.25), channel_id=1, source_target_pairs={{0,96},{32,0},{64,32},{96,64},{1,97},{33,1},{65,33},{97,65},{2,98}... | collective-permute-start | bytes 208904 | tf_op jit(solution)/shard_map/ppermute | solution.py:457
  88.9 0.1 collective-permute-done.7.got2
  89.0 2.1 %collective-permute-done.8.got1 = bf16[272,128]{1,0:T(8,128)(2,1)S(1)} collective-permute-done((bf16[272,128]{1,0:T(8,128)(2,1)S(1)}, bf16[272,128]{1,0:T(8,128)(2,1)S(1)}, u32[]{:S(2)}, u32[]{:S(2)}) %collective-permute-start.8) | collective-permute-done | bytes 69664 | tf_op jit(solution)/shard_map/ppermute | solution.py:457
  91.2 0.2 collective-permute-done.9.got3
  91.4 0.0 collective-permute-done.6.shifted
  91.4 1.8 %finish.1 = (f32[2,65,8,128]{3,2,1,0:T(8,128)}, f32[2,65,8,128]{3,2,1,0:T(8,128)}) custom-call(s32[256]{0:T(256)S(1)} %copy-done.1, f32[848,128]{1,0:T(8,128)S(1)} %get-tuple-element.21.full, bf16[528,128]{1,0:T(8,128)(2,1)S(1)} %collective-permute-done.6.shifted, bf16[272,128]{1,0:T(8,128)(2,1)S(1)} %collective-permute-done.7.got2, ...), custom_call_target="tpu_custom_call" | custom-call | flops 1 | bytes 1 | tf_op jit(solution)/shard_map/finish/pallas_call | solution.py:443
  (2 shorter events, 0.0 us)
Async XLA Ops:
  0.6 7.2 %collective-permute-start = (s32[2,8]{1,0:T(2,128)}, s32[2,8]{1,0:T(2,128)S(1)}, u32[]{:S(2)}, u32[]{:S(2)}) collective-permute-start(s32[2,8]{1,0:T(2,128)} %param.4), channel_id=1, source_target_pairs={{0,1},{1,2},{2,3},{3,4},{4,5},{5,6},{6,7},{7,8},{8,9},{9,10},{10,1... | collective-permute-start | bytes 200 | tf_op jit(solution)/shard_map/ppermute | solution.py:469
  30.1 30.7 %copy-start = (bf16[512,256]{1,0:T(8,128)(2,1)S(1)}, bf16[512,256]{1,0:T(8,128)(2,1)}, u32[]{:S(2)}) copy-start(bf16[512,256]{1,0:T(8,128)(2,1)} %constant.2.clone.lag) | copy-start | bytes 786436
  30.1 12.2 %collective-permute-start.2 = (bf16[4,3,128,512]{3,2,1,0:T(8,128)(2,1)S(1)}, bf16[4,3,128,512]{3,2,1,0:T(8,128)(2,1)}, u32[]{:S(2)}, u32[]{:S(2)}) collective-permute-start(bf16[4,3,128,512]{3,2,1,0:T(8,128)(2,1)S(1)} %whiten.2.own_int), channel_id=1, source_target_pairs={{0,1},{1,0},{2,3},{3,2},{4,5},{5,4},{6,7},{7,6},{8,9},{9,8},{10,11... | collective-permute-start | bytes 4718600 | tf_op jit(solution)/shard_map/ppermute | solution.py:479
  36.8 24.0 %collective-permute-start.1 = (bf16[4,3,128,512]{3,2,1,0:T(8,128)(2,1)S(1)}, bf16[4,3,128,512]{3,2,1,0:T(8,128)(2,1)}, u32[]{:S(2)}, u32[]{:S(2)}) collective-permute-start(bf16[4,3,128,512]{3,2,1,0:T(8,128)(2,1)S(1)} %whiten.3.own_ext), channel_id=1, source_target_pairs={{1,2},{2,1},{3,4},{4,3},{5,6},{6,5},{7,8},{8,7},{9,10},{10,9},{11,... | collective-permute-start | bytes 4718600 | tf_op jit(solution)/shard_map/ppermute | solution.py:476
  60.8 0.7 copy-start.1
  67.0 9.9 %collective-permute-start.3 = (bf16[848,128]{1,0:T(8,128)(2,1)S(1)}, bf16[848,128]{1,0:T(8,128)(2,1)S(1)}, u32[]{:S(2)}, u32[]{:S(2)}) collective-permute-start(bf16[848,128]{1,0:T(8,128)(2,1)S(1)} %get-tuple-element.18), channel_id=1, source_target_pairs={{0,64},{32,96},{64,0},{96,32},{1,65},{33,97},{65,1},{97,33},{2,66}... | collective-permute-start | bytes 651272 | tf_op jit(solution)/shard_map/ppermute | solution.py:457
  68.6 11.5 %collective-permute-start.4 = (bf16[848,128]{1,0:T(8,128)(2,1)S(1)}, bf16[848,128]{1,0:T(8,128)(2,1)S(1)}, u32[]{:S(2)}, u32[]{:S(2)}) collective-permute-start(bf16[848,128]{1,0:T(8,128)(2,1)S(1)} %get-tuple-element.19), channel_id=1, source_target_pairs={{0,32},{32,64},{64,96},{96,0},{1,33},{33,65},{65,97},{97,1},{2,34}... | collective-permute-start | bytes 651272 | tf_op jit(solution)/shard_map/ppermute | solution.py:457
  70.1 9.9 %collective-permute-start.5 = (bf16[848,128]{1,0:T(8,128)(2,1)S(1)}, bf16[848,128]{1,0:T(8,128)(2,1)S(1)}, u32[]{:S(2)}, u32[]{:S(2)}) collective-permute-start(bf16[848,128]{1,0:T(8,128)(2,1)S(1)} %get-tuple-element.20), channel_id=1, source_target_pairs={{0,96},{32,0},{64,32},{96,64},{1,97},{33,1},{65,33},{97,65},{2,98}... | collective-permute-start | bytes 651272 | tf_op jit(solution)/shard_map/ppermute | solution.py:457
  80.8 10.7 %collective-permute-start.6 = (bf16[528,128]{1,0:T(8,128)(2,1)S(1)}, bf16[528,128]{1,0:T(8,128)(2,1)S(1)}, u32[]{:S(2)}, u32[]{:S(2)}) collective-permute-start(bf16[528,128]{1,0:T(8,128)(2,1)S(1)} %get-tuple-element.22), channel_id=1, source_target_pairs={{0,1},{1,2},{2,3},{3,4},{4,5},{5,6},{6,7},{7,8},{8,9},{9,10},{10,1... | collective-permute-start | bytes 405512 | tf_op jit(solution)/shard_map/ppermute | solution.py:483
  82.7 6.3 %collective-permute-start.7 = (bf16[272,128]{1,0:T(8,128)(2,1)S(1)}, bf16[272,128]{1,0:T(8,128)(2,1)S(1)}, u32[]{:S(2)}, u32[]{:S(2)}) collective-permute-start(bf16[272,128]{1,0:T(8,128)(2,1)S(1)} %get-tuple-element.23), channel_id=1, source_target_pairs={{0,64},{32,96},{64,0},{96,32},{1,65},{33,97},{65,1},{97,33},{2,66}... | collective-permute-start | bytes 208904 | tf_op jit(solution)/shard_map/ppermute | solution.py:457
  85.7 5.5 %collective-permute-start.8 = (bf16[272,128]{1,0:T(8,128)(2,1)S(1)}, bf16[272,128]{1,0:T(8,128)(2,1)S(1)}, u32[]{:S(2)}, u32[]{:S(2)}) collective-permute-start(bf16[272,128]{1,0:T(8,128)(2,1)S(1)} %get-tuple-element.24), channel_id=1, source_target_pairs={{0,32},{32,64},{64,96},{96,0},{1,33},{33,65},{65,97},{97,1},{2,34}... | collective-permute-start | bytes 208904 | tf_op jit(solution)/shard_map/ppermute | solution.py:457
  87.1 4.3 %collective-permute-start.9 = (bf16[272,128]{1,0:T(8,128)(2,1)S(1)}, bf16[272,128]{1,0:T(8,128)(2,1)S(1)}, u32[]{:S(2)}, u32[]{:S(2)}) collective-permute-start(bf16[272,128]{1,0:T(8,128)(2,1)S(1)} %get-tuple-element.25), channel_id=1, source_target_pairs={{0,96},{32,0},{64,32},{96,64},{1,97},{33,1},{65,33},{97,65},{2,98}... | collective-permute-start | bytes 208904 | tf_op jit(solution)/shard_map/ppermute | solution.py:457

commit v6 on v4

--- a/solution.py
+++ b/solution.py
@@ -29,7 +29,7 @@
 CHUNK = SLOTS * BODY + 16
 SEND2 = SHIFTED * BODY + 16
 SEND3 = 4 * BODY + 16
-SEG, PAIRS, MOVES, WRITES, PLAN = 4, 16, 80, 112, 256
+PAIRS, MOVES, WRITES = 48, 32, 8
 TWO = CHUNK
 THREE = CHUNK + SEND2
 POOL = THREE + 3 * SEND3
@@ -48,8 +48,9 @@
 
 
 def lag_rows(segments):
+    freqs = np.concatenate([np.arange(0, BINS, 2), np.arange(1, BINS, 2)])
     shifts = np.arange(-MAXLAG, MAXLAG + 1)
-    phase = (shifts[:, None] * np.arange(BINS)[None, :] % LENGTH) * (2.0 * np.pi / LENGTH)
+    phase = (shifts[:, None] * freqs[None, :] % LENGTH) * (2.0 * np.pi / LENGTH)
     table = np.concatenate([np.cos(phase), -np.sin(phase)], axis=1) / np.sqrt(segments * BINS)
     table = np.concatenate([table, np.zeros((CHANS - LAGS, LENGTH))], axis=0).T.astype(np.float32)
     return np.concatenate(split(table), axis=1)
@@ -74,14 +75,17 @@
     col = lax.broadcasted_iota(jnp.int32, (REACHED, LENGTH), 1)
     apart = at - col + jnp.where(col < BINS, 0, LENGTH - REACHED)
     tab[:REACHED] = jnp.where(jnp.abs(apart) <= SMOOTH, 1.0, 0.0).astype(BF)
+    half = BINS // 2
     row = lax.broadcasted_iota(jnp.int32, (CHANS, LENGTH), 0)
     col = lax.broadcasted_iota(jnp.int32, (CHANS, LENGTH), 1)
-    row = row + jnp.where(col < BINS, 0, CHANS)
-    col = jnp.bitwise_and(col, BINS - 1)
-    tab[REACHED:LENGTH] = jnp.where(row // BAND == col // BAND, 0.5 / BAND, 0.0).astype(BF)
-
-    def cosine(step, shift, rows):
-        k = lax.broadcasted_iota(jnp.int32, (rows, BINS), 0) * lax.broadcasted_iota(jnp.int32, (rows, BINS), 1)
+    row = jnp.bitwise_and(row, half - 1) // (BAND // 2)
+    col = jnp.bitwise_and(col, half - 1) // (BAND // 2)
+    tab[REACHED:LENGTH] = jnp.where(row == col, 0.5 / BAND, 0.0).astype(BF)
+
+    def cosine(step, shift):
+        col = lax.broadcasted_iota(jnp.int32, (16, BINS), 1)
+        freq = 2 * jnp.bitwise_and(col, half - 1) + jnp.right_shift(col, 7)
+        k = lax.broadcasted_iota(jnp.int32, (16, BINS), 0) * freq
         k = jnp.bitwise_and(k * step - shift + BINS, LENGTH - 1) - BINS
         square = jnp.square(k.astype(F32) * (2.0 * np.pi / LENGTH))
         value = jnp.ones_like(square)
@@ -90,14 +94,15 @@
         return value
 
     quarter = LENGTH // 4
-    fine_cos, fine_sin = cosine(1, 0, 16), cosine(1, quarter, 16)
-    coarse_cos, coarse_sin = cosine(16, 0, 32), cosine(16, quarter, 32)
-    for a in range(LENGTH // 16):
+    fine_cos, fine_sin = cosine(1, 0), cosine(1, quarter)
+    coarse_cos, coarse_sin = cosine(16, 0), cosine(16, quarter)
+    for a in range(16):
         c, s = coarse_cos[a : a + 1], coarse_sin[a : a + 1]
         for k, part in enumerate((c * fine_cos - s * fine_sin, -(s * fine_cos) - c * fine_sin)):
-            high, low = halves(part)
-            tab[LENGTH + 16 * a : LENGTH + 16 * a + 16, k * BINS : (k + 1) * BINS] = high
-            tab[2 * LENGTH + 16 * a : 2 * LENGTH + 16 * a + 16, k * BINS : (k + 1) * BINS] = low
+            for n, rounded in enumerate(halves(part)):
+                rows = pl.ds(LENGTH + n * BINS + 16 * a, 16)
+                tab[rows, k * half : (k + 1) * half] = rounded[:, :half]
+                tab[rows, BINS + k * half : BINS + (k + 1) * half] = rounded[:, half:]
 
 
 def whiten_body(outer, records, white, buf, tab, sems):
@@ -130,15 +135,23 @@
             right = dot(right, jnp.concatenate([second, second], axis=0))
             levels.append(jnp.concatenate([left, right], axis=1) * share)
         spectra = []
-        fhi = tab[LENGTH : 2 * LENGTH]
-        fourier = jnp.concatenate([fhi, fhi, tab[2 * LENGTH :]], axis=0)
+        products = []
+        for at in (0, BINS):
+            high = tab[LENGTH : LENGTH + BINS, at : at + BINS]
+            products.append(jnp.concatenate([high, high, tab[LENGTH + BINS :, at : at + BINS]], axis=0))
         for x, level in zip(xs, levels):
-            nhi, nlo = halves(x * inverse(level + 1e-06))
-            spectra.append(dot(jnp.concatenate([nhi, nlo, nhi], axis=1), fourier))
+            normed = x * inverse(level + 1e-06)
+            left, right = normed[:, :BINS], normed[:, BINS:]
+            pair = []
+            for part, product in zip((left + right, left - right), products):
+                high, low = halves(part)
+                pair.append(dot(jnp.concatenate([high, low, high], axis=1), product))
+            spectra.append(pair)
         same = jnp.concatenate([tab[REACHED:LENGTH, :BINS], tab[REACHED:LENGTH, BINS:]], axis=0)
         for n in parts:
-            re = spectra[n][:, :BINS]
-            im = spectra[n][:, BINS:]
+            even, odd = spectra[n]
+            re = jnp.concatenate([even[:, : BINS // 2], odd[:, : BINS // 2]], axis=1)
+            im = jnp.concatenate([even[:, BINS // 2 :], odd[:, BINS // 2 :]], axis=1)
             power = dot((re * re + im * im).astype(BF), same)
             factor = lax.rsqrt(power + 1e-05)
             per = SUB // CHANS
@@ -158,7 +171,7 @@
         out_shape=jax.ShapeDtypeStruct((HALF, segs, CHANS, LENGTH), BF),
         scratch_shapes=[
             pltpu.VMEM((segs, ROWS, LENGTH), F32),
-            pltpu.VMEM((3 * LENGTH, LENGTH), BF),
+            pltpu.VMEM((2 * LENGTH, LENGTH), BF),
             pltpu.SemaphoreType.DMA((segs,)),
         ],
         compiler_params=pltpu.CompilerParams(vmem_limit_bytes=50 * MIB),
@@ -176,16 +189,18 @@
 )
 
 
-def plan_body(own, before, plan, slots):
-    s = lax.axis_index("seg").astype(jnp.int32)
-    plan[SEG] = s
-    zero = jnp.int32(0)
-
-    def behind(owner):
-        return 2 * jnp.bitwise_and(s - owner, 3)
-
-    used = [zero] * PLANES
-    n = zero
+def seg_index():
+    return lax.axis_index("seg").astype(jnp.int32)
+
+
+def behind(owner):
+    return 2 * jnp.bitwise_and(seg_index() - owner, 3)
+
+
+def list_pairs(own, before, codes, slots):
+    s = seg_index()
+    used = [jnp.int32(0)] * PLANES
+    n = jnp.int32(0)
     for p, d in VISITS:
         row = p + HALF if p < HALF else p - HALF
         owner = row // 2
@@ -197,16 +212,19 @@
             slots[96 + (p - 6) * 2 + p + d - 12] = used[0]
             code = code + (used[0] + 1) * 65536
             used[0] = used[0] + live
-        plan[PAIRS + n] = code
+        codes[n] = code
         n = n + live
-    plan[0] = n
-
-    n = zero
+    return n
+
+
+def list_moves(own, before, slots, moves):
+    s = seg_index()
+    n = jnp.int32(0)
     for owner in (0, 1):
         for k, (i, j) in enumerate(UPWARD[owner]):
             p, d = HALF + i, GROUP + j - i
             entry = p * REACH + d - 1 if i // 2 == owner else 96 + (i - 2) * 2 + j
-            plan[MOVES + n] = slots[entry] + k * 4096
+            moves[n] = slots[entry] + k * 4096
             n = n + jnp.where(s == owner, own[behind(i // 2) + i % 2, d - 1], 0)
     for r in range(1, PLANES):
         to = jnp.bitwise_and(s + r, 3)
@@ -217,15 +235,19 @@
                 p = jnp.where(ahead, row + HALF, jnp.maximum(row - HALF, 0))
                 d = 2 * to + j - row + jnp.where(ahead, 0, GROUP)
                 live = jnp.where(ahead, own[i, d - 1], jnp.where(s >= 2, before[i, d - 1], 0))
-                plan[MOVES + n] = slots[p * REACH + d - 1] + r * 256 + (2 * i + j) * 4096
+                moves[n] = slots[p * REACH + d - 1] + r * 256 + (2 * i + j) * 4096
                 n = n + live
-    plan[1] = n
+    return n
+
+
+def list_writes(own, before, slots, writes):
+    s = seg_index()
 
     def write(n, i, d, base, size, slot):
-        plan[WRITES + n] = base + slot * BODY + (base + size * BODY + slot) * 4096 + (i * 8 + d - 1) * 16777216
-
-    n = zero
-    above = zero
+        writes[WRITES + n] = base + slot * BODY + (base + size * BODY + slot) * 4096 + (i * 8 + d - 1) * 16777216
+
+    n = jnp.int32(0)
+    above = jnp.int32(0)
     for i in range(2):
         for d in range(1, REACH + 1):
             row = 2 * s + i
@@ -235,7 +257,7 @@
             write(n, i, d, jnp.where(shift, TWO, 0), jnp.where(shift, SHIFTED, SLOTS), slot)
             n = n + live
             above = above + jnp.where(shift, live, 0)
-    plan[2] = n
+    writes[0] = n
     for j in range(2):
         for d in range(1, REACH + 1):
             low = 2 * s + j - d
@@ -256,22 +278,13 @@
             size = jnp.where(mine, SLOTS, jnp.where(up, SHIFTED, 4))
             write(n, j, d, base, size, slot)
             n = n + live
-    plan[3] = n
-
-
-def make_plan(own, before):
-    return pl.pallas_call(
-        plan_body,
-        in_specs=[SMEM, SMEM],
-        out_specs=SMEM,
-        out_shape=jax.ShapeDtypeStruct((PLAN,), jnp.int32),
-        scratch_shapes=[pltpu.SMEM((128,), jnp.int32)],
-        cost_estimate=TINY,
-        name="plan",
-    )(own, before)
-
-
-def correlate_body(plan, own_ext, own_int, got_ext, got_int, lag, keep, out1, out2, out3, low, high, stk, pq, last):
+    writes[1] = n
+
+
+def correlate_body(
+    own, before, own_ext, own_int, got_ext, got_int, lag, keep, out1, out2, out3, slots, low, high, stk, pq, codes, last
+):
+    count = list_pairs(own, before, codes, slots)
     core = jnp.bitwise_and(lax.axis_index("blk"), 1)
     sources = (
         (own_ext, HALF * (1 + core)),
@@ -294,7 +307,7 @@
         stk[r, pl.ds(SLOTS * BODY + n, 1), :] = stack[BODY:LAGS]
 
     def pair(n, carry):
-        code = plan[PAIRS + n]
+        code = codes[n]
         p = jnp.bitwise_and(code, 15)
         d = jnp.bitwise_and(jnp.right_shift(code, 4), 15)
 
@@ -328,43 +341,53 @@
 
         @pl.when(second > 0)
         def _():
-            put(jnp.bitwise_and(-plan[SEG], 3), second - 1, stack)
+            put(jnp.bitwise_and(-seg_index(), 3), second - 1, stack)
 
         return carry
 
-    lax.fori_loop(0, plan[0], pair, 0)
+    lax.fori_loop(0, count, pair, 0)
     keep[...] = stk[0]
     out1[...] = stk[1].astype(BF)
     out2[...] = stk[2].astype(BF)
     out3[...] = stk[3].astype(BF)
 
 
-def correlate(plan, whites, lag):
+def correlate(own, before, whites, lag):
     segs = whites[0].shape[1]
     chunk = jax.ShapeDtypeStruct((CHUNK, CHANS), BF)
     return pl.pallas_call(
         correlate_body,
-        in_specs=[SMEM] + [VMEM] * 5,
-        out_specs=[VMEM] * 4,
-        out_shape=[jax.ShapeDtypeStruct((CHUNK, CHANS), F32), chunk, chunk, chunk],
+        in_specs=[SMEM] * 2 + [VMEM] * 5,
+        out_specs=[VMEM] * 4 + [SMEM],
+        out_shape=[
+            jax.ShapeDtypeStruct((CHUNK, CHANS), F32),
+            chunk,
+            chunk,
+            chunk,
+            jax.ShapeDtypeStruct((128,), jnp.int32),
+        ],
         scratch_shapes=[
             pltpu.VMEM((segs, CHANS, LENGTH), BF),
             pltpu.VMEM((segs, CHANS, LENGTH), BF),
             pltpu.VMEM((PLANES, CHUNK, CHANS), F32),
             pltpu.VMEM((2, CHANS, LENGTH), BF),
+            pltpu.SMEM((PAIRS,), jnp.int32),
             pltpu.SMEM((1,), jnp.int32),
         ],
         compiler_params=pltpu.CompilerParams(vmem_limit_bytes=16 * MIB),
         cost_estimate=TINY,
         name="correlate",
-    )(plan, *whites, lag)
-
-
-def combine_body(plan, keep, got2, got1, got3, full, send, out1, out2, out3, stage):
+    )(own, before, *whites, lag)
+
+
+def combine_body(
+    own, before, slots, keep, got2, got1, got3, full, send, out1, out2, out3, writes, stage, moves
+):
+    count = list_moves(own, before, slots, moves)
     full[...] = (keep[...] + got1[...].astype(F32)) + (got2[...].astype(F32) + got3[...].astype(F32))
 
     def move(n, carry):
-        code = plan[MOVES + n]
+        code = moves[n]
         slot = jnp.bitwise_and(code, 255)
         message = jnp.bitwise_and(jnp.right_shift(code, 8), 15)
         k = jnp.right_shift(code, 12)
@@ -374,42 +397,44 @@
         stage[message, pl.ds(size * BODY + k, 1), :] = full[pl.ds(SLOTS * BODY + slot, 1), :]
         return carry
 
-    lax.fori_loop(0, plan[1], move, 0)
-
-    @pl.when(plan[SEG] >= 2)
+    lax.fori_loop(0, count, move, 0)
+
+    @pl.when(seg_index() >= 2)
     def _():
         send[: SHIFTED * BODY, :] = full[: SHIFTED * BODY, :].astype(BF)
         send[SHIFTED * BODY :, :] = full[SLOTS * BODY :, :].astype(BF)
 
-    @pl.when(plan[SEG] < 2)
+    @pl.when(seg_index() < 2)
     def _():
         send[...] = stage[0].astype(BF)
 
     for r, out in ((1, out1), (2, out2), (3, out3)):
         out[...] = stage[r, :SEND3].astype(BF)
+    list_writes(own, before, slots, writes)
 
 
 def combine(*args):
     third = jax.ShapeDtypeStruct((SEND3, CHANS), BF)
     return pl.pallas_call(
         combine_body,
-        in_specs=[SMEM] + [VMEM] * 4,
-        out_specs=[VMEM] * 5,
+        in_specs=[SMEM] * 3 + [VMEM] * 4,
+        out_specs=[VMEM] * 5 + [SMEM],
         out_shape=[
             jax.ShapeDtypeStruct((CHUNK, CHANS), F32),
             jax.ShapeDtypeStruct((SEND2, CHANS), BF),
             third,
             third,
             third,
+            jax.ShapeDtypeStruct((WRITES + 40,), jnp.int32),
         ],
-        scratch_shapes=[pltpu.VMEM((PLANES, SEND2, CHANS), F32)],
+        scratch_shapes=[pltpu.VMEM((PLANES, SEND2, CHANS), F32), pltpu.SMEM((MOVES,), jnp.int32)],
         compiler_params=pltpu.CompilerParams(vmem_limit_bytes=8 * MIB),
         cost_estimate=TINY,
         name="combine",
     )(*args)
 
 
-def finish_body(plan, full, shifted, got2, got1, got3, fwd, bwd, pool):
+def finish_body(writes, full, got2, got1, got3, shifted, fwd, bwd, pool):
     pool[:TWO, :] = full[...]
     pool[TWO:THREE, :] = shifted[...].astype(F32)
     for r, got in ((1, got1), (2, got2), (3, got3)):
@@ -418,7 +443,7 @@
     bwd[...] = jnp.zeros(bwd.shape, F32)
 
     def write(out, place, n):
-        code = plan[WRITES + n]
+        code = writes[WRITES + n]
         body = jnp.bitwise_and(code, 4095)
         i = jnp.right_shift(code, 27)
         at = pl.ds(jnp.bitwise_and(jnp.right_shift(code, 24), 7), 1)
@@ -434,8 +459,8 @@
         write(bwd, lambda m: BODY - m, n)
         return carry
 
-    lax.fori_loop(0, plan[2], ahead, 0)
-    lax.fori_loop(plan[2], plan[3], behind, 0)
+    lax.fori_loop(0, writes[0], ahead, 0)
+    lax.fori_loop(writes[0], writes[1], behind, 0)
 
 
 def finish(blocks, *args):
@@ -472,12 +497,14 @@
     got_int = lax.ppermute(own_int, "blk", inner)
     rows, _ = lax.optimization_barrier((pairs, own_int))
     own = jnp.concatenate([rows, ring(rows, 1), ring(rows, 2), ring(rows, 3)])
-    plan = make_plan(own, lax.ppermute(own, "blk", upward))
-
-    keep, out1, out2, out3 = correlate(plan, (own_ext, own_int, got_ext, got_int), lag)
-    full, send, out1, out2, out3 = combine(plan, keep, ring(out2, 2), ring(out1, 1), ring(out3, 3))
+    before = lax.ppermute(own, "blk", upward)
+
+    keep, out1, out2, out3, slots = correlate(own, before, (own_ext, own_int, got_ext, got_int), lag)
+    full, send, out1, out2, out3, writes = combine(
+        own, before, slots, keep, ring(out2, 2), ring(out1, 1), ring(out3, 3)
+    )
     shifted = lax.ppermute(send, ("seg", "blk"), shift)
-    outs = finish(pairs.shape[0], plan, full, shifted, ring(out2, 2), ring(out1, 1), ring(out3, 3))
+    outs = finish(pairs.shape[0], writes, full, ring(out2, 2), ring(out1, 1), ring(out3, 3), shifted)
     return tuple(jnp.transpose(out, (0, 2, 1, 3)) for out in outs)
 
 

time: 67.5 us -> 65.1 us (0.964)
  the two profiles are of different devices: /device:TPU:6 before, /device:TPU:4 now
where the time goes in v6:
time: 65.1 us; the launch traced here: 64 us
  starting transfers between devices  26.8 us (41%)
  waiting for transfers between devices  18.7 us (29%)
  Pallas kernels  17.8 us (27%)
  between operations  0.73 us (1%)
    ppermute x9, starting transfers between devices, ring(): lax.ppermute(x, 'seg', [(z, (z + r) % planes) for z in range(planes)])  18.4 us
    ppermute x9, waiting for transfers between devices, ring(): lax.ppermute(x, 'seg', [(z, (z + r) % planes) for z in range(planes)])  13.6 us
    pallas_call x2, Pallas kernels, whiten(): pl.pallas_call(functools.partial(whiten_body, outer), in_specs=[pl.BlockS...  10.2 us
    ppermute x1, waiting for transfers between devices, shards(): before = lax.ppermute(own, 'blk', upward)  5.11 us
    ppermute x1, starting transfers between devices, shards(): got_ext = lax.ppermute(own_ext, 'blk', outer)  4.46 us
    pallas_call x1, Pallas kernels, correlate(): pl.pallas_call(correlate_body, in_specs=[SMEM] * 2 + [VMEM] * 5, out_spec...  4.12 us
    ppermute x1, starting transfers between devices, shards(): shifted = lax.ppermute(send, ('seg', 'blk'), shift)  1.92 us
    ppermute x1, starting transfers between devices, shards(): before = lax.ppermute(own, 'blk', upward)  1.92 us
  transfers between devices with their start and end apart: 13, of which 7 were waited for; matrix products, arithmetic and copies ran while one was open for 0% of the time, Pallas kernels for 8%

profile of v6, /device:TPU:4, one launch (start us, length us, event | category | flops | bytes accessed | tf_op | source)
XLA Modules:
  0.0 64.0 jit_solution(10428372244537652120)
XLA Ops:
  0.6 5.1 %whiten.3.own_ext = bf16[4,3,128,512]{3,2,1,0:T(8,128)(2,1)S(1)} custom-call(f32[3,1024,512]{2,1,0:T(8,128)} %records.3), custom_call_target="tpu_custom_call" | custom-call | flops 1 | bytes 1 | tf_op jit(solution)/shard_map/whiten/pallas_call | solution.py:167
  5.7 0.0 copy-start.1
  5.7 0.0 copy-start
  5.7 4.5 %collective-permute-start.4 = (bf16[4,3,128,512]{3,2,1,0:T(8,128)(2,1)S(1)}, bf16[4,3,128,512]{3,2,1,0:T(8,128)(2,1)S(1)}, u32[]{:S(2)}, u32[]{:S(2)}) collective-permute-start(bf16[4,3,128,512]{3,2,1,0:T(8,128)(2,1)S(1)} %whiten.3.own_ext), channel_id=1, source_target_pairs={{1,2},{2,1},{3,4},{4,3},{5,6},{6,5},{7,8},{8,7},{9,10},{10,9},{11,... | collective-permute-start | bytes 4718600 | tf_op jit(solution)/shard_map/ppermute | solution.py:495
  10.2 5.1 %whiten.2.own_int = bf16[4,3,128,512]{3,2,1,0:T(8,128)(2,1)S(1)} custom-call(f32[3,1024,512]{2,1,0:T(8,128)} %records.3), custom_call_target="tpu_custom_call" | custom-call | flops 1 | bytes 1 | tf_op jit(solution)/shard_map/whiten/pallas_call | solution.py:167
  15.3 0.1 collective-permute-start.5
  15.4 0.0 copy-done.1
  15.4 4.1 %collective-permute-start.2 = (s32[2,8]{1,0:T(2,128)S(1)}, s32[2,8]{1,0:T(2,128)S(1)}, u32[]{:S(2)}, u32[]{:S(2)}) collective-permute-start(s32[2,8]{1,0:T(2,128)S(1)} %copy-done.1), channel_id=1, source_target_pairs={{0,96},{32,0},{64,32},{96,64},{1,97},{33,1},{65,33},{97,65},{2,98}... | collective-permute-start | bytes 200 | tf_op jit(solution)/shard_map/ppermute | solution.py:482
  19.5 0.0 collective-permute-start.1
  19.5 1.3 %collective-permute-start = (s32[2,8]{1,0:T(2,128)S(1)}, s32[2,8]{1,0:T(2,128)S(1)}, u32[]{:S(2)}, u32[]{:S(2)}) collective-permute-start(s32[2,8]{1,0:T(2,128)S(1)} %copy-done.1), channel_id=1, source_target_pairs={{0,32},{32,64},{64,96},{96,0},{1,33},{33,65},{65,97},{97,1},{2,34}... | collective-permute-start | bytes 200 | tf_op jit(solution)/shard_map/ppermute | solution.py:482
  20.8 0.0 collective-permute-done.2
  20.8 3.8 %collective-permute-done.1 = s32[2,8]{1,0:T(2,128)S(1)} collective-permute-done((s32[2,8]{1,0:T(2,128)S(1)}, s32[2,8]{1,0:T(2,128)S(1)}, u32[]{:S(2)}, u32[]{:S(2)}) %collective-permute-start.1) | collective-permute-done | bytes 96 | tf_op jit(solution)/shard_map/ppermute | solution.py:482
  24.6 0.0 collective-permute-done
  24.6 1.9 %collective-permute-start.3 = (s32[8,8]{1,0:T(8,128)S(1)}, s32[8,8]{1,0:T(8,128)S(1)}, u32[]{:S(2)}, u32[]{:S(2)}) collective-permute-start(s32[8,8]{1,0:T(8,128)S(1)} %pad_add_fusion.own), channel_id=1, source_target_pairs={{0,1},{1,2},{2,3},{3,4},{4,5},{5,6},{6,7},{7,8},{8,9},{9,10},{10,1... | collective-permute-start | bytes 776 | tf_op jit(solution)/shard_map/ppermute | solution.py:500
  26.5 5.1 %collective-permute-done.3.before = s32[8,8]{1,0:T(8,128)S(1)} collective-permute-done((s32[8,8]{1,0:T(8,128)S(1)}, s32[8,8]{1,0:T(8,128)S(1)}, u32[]{:S(2)}, u32[]{:S(2)}) %collective-permute-start.3) | collective-permute-done | bytes 288 | tf_op jit(solution)/shard_map/ppermute | solution.py:500
  31.6 0.0 collective-permute-done.4.got_ext
  31.6 0.0 collective-permute-done.5.got_int
  31.6 0.0 copy-done
  31.6 4.1 %correlate.1 = (f32[848,128]{1,0:T(8,128)S(1)}, bf16[848,128]{1,0:T(8,128)(2,1)S(1)}, bf16[848,128]{1,0:T(8,128)(2,1)S(1)}, bf16[848,128]{1,0:T(8,128)(2,1)S(1)}, s32[128]{0:T(128)S(1)}) custom-call(s32[8,8]{1,0:T(8,128)S(1)} %pad_add_fusion.own, s32[8,8]{1,0:T(8,128)S(1)} %collective-permute-done.3.before, bf16[4,3,128,512]{3,2,1,0:T(8,128)(2,1)S(1)} %whiten.3.own_ext, ...), custom_call_target="tpu_custom_call" | custom-call | flops 1 | bytes 1 | tf_op jit(solution)/shard_map/correlate/pallas_call | solution.py:358
  35.8 2.1 %collective-permute-start.6 = (bf16[848,128]{1,0:T(8,128)(2,1)S(1)}, bf16[848,128]{1,0:T(8,128)(2,1)S(1)}, u32[]{:S(2)}, u32[]{:S(2)}) collective-permute-start(bf16[848,128]{1,0:T(8,128)(2,1)S(1)} %get-tuple-element.19), channel_id=1, source_target_pairs={{0,64},{32,96},{64,0},{96,32},{1,65},{33,97},{65,1},{97,33},{2,66}... | collective-permute-start | bytes 651272 | tf_op jit(solution)/shard_map/ppermute | solution.py:482
  37.9 1.0 %collective-permute-start.7 = (bf16[848,128]{1,0:T(8,128)(2,1)S(1)}, bf16[848,128]{1,0:T(8,128)(2,1)S(1)}, u32[]{:S(2)}, u32[]{:S(2)}) collective-permute-start(bf16[848,128]{1,0:T(8,128)(2,1)S(1)} %get-tuple-element.20), channel_id=1, source_target_pairs={{0,32},{32,64},{64,96},{96,0},{1,33},{33,65},{65,97},{97,1},{2,34}... | collective-permute-start | bytes 651272 | tf_op jit(solution)/shard_map/ppermute | solution.py:482
  38.9 2.2 %collective-permute-start.8 = (bf16[848,128]{1,0:T(8,128)(2,1)S(1)}, bf16[848,128]{1,0:T(8,128)(2,1)S(1)}, u32[]{:S(2)}, u32[]{:S(2)}) collective-permute-start(bf16[848,128]{1,0:T(8,128)(2,1)S(1)} %get-tuple-element.21), channel_id=1, source_target_pairs={{0,96},{32,0},{64,32},{96,64},{1,97},{33,1},{65,33},{97,65},{2,98}... | collective-permute-start | bytes 651272 | tf_op jit(solution)/shard_map/ppermute | solution.py:482
  41.1 4.2 %collective-permute-done.6.got2 = bf16[848,128]{1,0:T(8,128)(2,1)S(1)} collective-permute-done((bf16[848,128]{1,0:T(8,128)(2,1)S(1)}, bf16[848,128]{1,0:T(8,128)(2,1)S(1)}, u32[]{:S(2)}, u32[]{:S(2)}) %collective-permute-start.6) | collective-permute-done | bytes 217120 | tf_op jit(solution)/shard_map/ppermute | solution.py:482
  45.3 2.6 %collective-permute-done.7.got1 = bf16[848,128]{1,0:T(8,128)(2,1)S(1)} collective-permute-done((bf16[848,128]{1,0:T(8,128)(2,1)S(1)}, bf16[848,128]{1,0:T(8,128)(2,1)S(1)}, u32[]{:S(2)}, u32[]{:S(2)}) %collective-permute-start.7) | collective-permute-done | bytes 217120 | tf_op jit(solution)/shard_map/ppermute | solution.py:482
  47.9 0.4 collective-permute-done.8.got3
  48.2 1.7 %combine.1 = (f32[848,128]{1,0:T(8,128)S(1)}, bf16[528,128]{1,0:T(8,128)(2,1)S(1)}, bf16[272,128]{1,0:T(8,128)(2,1)S(1)}, bf16[272,128]{1,0:T(8,128)(2,1)S(1)}, ...) custom-call(s32[8,8]{1,0:T(8,128)S(1)} %pad_add_fusion.own, s32[8,8]{1,0:T(8,128)S(1)} %collective-permute-done.3.before, ...), custom_call_target="tpu_custom_call" | custom-call | flops 1 | bytes 1 | tf_op jit(solution)/shard_map/combine/pallas_call | solution.py:418
  50.0 1.9 %collective-permute-start.12 = (bf16[528,128]{1,0:T(8,128)(2,1)S(1)}, bf16[528,128]{1,0:T(8,128)(2,1)S(1)}, u32[]{:S(2)}, u32[]{:S(2)}) collective-permute-start(bf16[528,128]{1,0:T(8,128)(2,1)S(1)} %get-tuple-element.27), channel_id=1, source_target_pairs={{0,1},{1,2},{2,3},{3,4},{4,5},{5,6},{6,7},{7,8},{8,9},{9,10},{10,1... | collective-permute-start | bytes 405512 | tf_op jit(solution)/shard_map/ppermute | solution.py:506
  51.9 4.4 %collective-permute-start.9 = (bf16[272,128]{1,0:T(8,128)(2,1)S(1)}, bf16[272,128]{1,0:T(8,128)(2,1)S(1)}, u32[]{:S(2)}, u32[]{:S(2)}) collective-permute-start(bf16[272,128]{1,0:T(8,128)(2,1)S(1)} %get-tuple-element.24), channel_id=1, source_target_pairs={{0,64},{32,96},{64,0},{96,32},{1,65},{33,97},{65,1},{97,33},{2,66}... | collective-permute-start | bytes 208904 | tf_op jit(solution)/shard_map/ppermute | solution.py:482
  56.4 1.6 %collective-permute-start.10 = (bf16[272,128]{1,0:T(8,128)(2,1)S(1)}, bf16[272,128]{1,0:T(8,128)(2,1)S(1)}, u32[]{:S(2)}, u32[]{:S(2)}) collective-permute-start(bf16[272,128]{1,0:T(8,128)(2,1)S(1)} %get-tuple-element.25), channel_id=1, source_target_pairs={{0,32},{32,64},{64,96},{96,0},{1,33},{33,65},{65,97},{97,1},{2,34}... | collective-permute-start | bytes 208904 | tf_op jit(solution)/shard_map/ppermute | solution.py:482
  57.9 1.7 %collective-permute-start.11 = (bf16[272,128]{1,0:T(8,128)(2,1)S(1)}, bf16[272,128]{1,0:T(8,128)(2,1)S(1)}, u32[]{:S(2)}, u32[]{:S(2)}) collective-permute-start(bf16[272,128]{1,0:T(8,128)(2,1)S(1)} %get-tuple-element.26), channel_id=1, source_target_pairs={{0,96},{32,0},{64,32},{96,64},{1,97},{33,1},{65,33},{97,65},{2,98}... | collective-permute-start | bytes 208904 | tf_op jit(solution)/shard_map/ppermute | solution.py:482
  59.6 0.0 collective-permute-done.9.got2
  59.6 2.3 %collective-permute-done.10.got1 = bf16[272,128]{1,0:T(8,128)(2,1)S(1)} collective-permute-done((bf16[272,128]{1,0:T(8,128)(2,1)S(1)}, bf16[272,128]{1,0:T(8,128)(2,1)S(1)}, u32[]{:S(2)}, u32[]{:S(2)}) %collective-permute-start.10) | collective-permute-done | bytes 69664 | tf_op jit(solution)/shard_map/ppermute | solution.py:482
  61.9 0.4 collective-permute-done.11.got3
  62.2 0.0 collective-permute-done.12.shifted
  62.2 1.8 %finish.1 = (f32[2,65,8,128]{3,2,1,0:T(8,128)}, f32[2,65,8,128]{3,2,1,0:T(8,128)}) custom-call(s32[48]{0:T(128)S(1)} %get-tuple-element.22.writes, f32[848,128]{1,0:T(8,128)S(1)} %get-tuple-element.23.full, bf16[272,128]{1,0:T(8,128)(2,1)S(1)} %collective-permute-done.9.got2, bf16[272,128]{1,0:T(8,128)(2,1)S(1)} %collective-permute-done.10.got1, ...), custom_call_target="tpu_custom_call" | custom-call | flops 1 | bytes 1 | tf_op jit(solution)/shard_map/finish/pallas_call | solution.py:468
  (1 shorter events, 0.0 us)
Async XLA Ops:
  5.7 9.7 %copy-start.1 = (s32[2,8]{1,0:T(2,128)S(1)}, s32[2,8]{1,0:T(2,128)}, u32[]{:S(2)}) copy-start(s32[2,8]{1,0:T(2,128)} %param.4) | copy-start | bytes 196
  5.7 25.9 %copy-start = (bf16[512,256]{1,0:T(8,128)(2,1)S(1)}, bf16[512,256]{1,0:T(8,128)(2,1)}, u32[]{:S(2)}) copy-start(bf16[512,256]{1,0:T(8,128)(2,1)} %constant.2.clone.lag) | copy-start | bytes 786436
  5.7 25.9 %collective-permute-start.4 = (bf16[4,3,128,512]{3,2,1,0:T(8,128)(2,1)S(1)}, bf16[4,3,128,512]{3,2,1,0:T(8,128)(2,1)S(1)}, u32[]{:S(2)}, u32[]{:S(2)}) collective-permute-start(bf16[4,3,128,512]{3,2,1,0:T(8,128)(2,1)S(1)} %whiten.3.own_ext), channel_id=1, source_target_pairs={{1,2},{2,1},{3,4},{4,3},{5,6},{6,5},{7,8},{8,7},{9,10},{10,9},{11,... | collective-permute-start | bytes 4718600 | tf_op jit(solution)/shard_map/ppermute | solution.py:495
  15.3 16.3 %collective-permute-start.5 = (bf16[4,3,128,512]{3,2,1,0:T(8,128)(2,1)S(1)}, bf16[4,3,128,512]{3,2,1,0:T(8,128)(2,1)S(1)}, u32[]{:S(2)}, u32[]{:S(2)}) collective-permute-start(bf16[4,3,128,512]{3,2,1,0:T(8,128)(2,1)S(1)} %whiten.2.own_int), channel_id=1, source_target_pairs={{0,1},{1,0},{2,3},{3,2},{4,5},{5,4},{6,7},{7,6},{8,9},{9,8},{10,11... | collective-permute-start | bytes 4718600 | tf_op jit(solution)/shard_map/ppermute | solution.py:497
  15.4 5.4 %collective-permute-start.2 = (s32[2,8]{1,0:T(2,128)S(1)}, s32[2,8]{1,0:T(2,128)S(1)}, u32[]{:S(2)}, u32[]{:S(2)}) collective-permute-start(s32[2,8]{1,0:T(2,128)S(1)} %copy-done.1), channel_id=1, source_target_pairs={{0,96},{32,0},{64,32},{96,64},{1,97},{33,1},{65,33},{97,65},{2,98}... | collective-permute-start | bytes 200 | tf_op jit(solution)/shard_map/ppermute | solution.py:482
  19.5 5.1 %collective-permute-start.1 = (s32[2,8]{1,0:T(2,128)S(1)}, s32[2,8]{1,0:T(2,128)S(1)}, u32[]{:S(2)}, u32[]{:S(2)}) collective-permute-start(s32[2,8]{1,0:T(2,128)S(1)} %copy-done.1), channel_id=1, source_target_pairs={{0,64},{32,96},{64,0},{96,32},{1,65},{33,97},{65,1},{97,33},{2,66}... | collective-permute-start | bytes 200 | tf_op jit(solution)/shard_map/ppermute | solution.py:482
  19.5 5.1 %collective-permute-start = (s32[2,8]{1,0:T(2,128)S(1)}, s32[2,8]{1,0:T(2,128)S(1)}, u32[]{:S(2)}, u32[]{:S(2)}) collective-permute-start(s32[2,8]{1,0:T(2,128)S(1)} %copy-done.1), channel_id=1, source_target_pairs={{0,32},{32,64},{64,96},{96,0},{1,33},{33,65},{65,97},{97,1},{2,34}... | collective-permute-start | bytes 200 | tf_op jit(solution)/shard_map/ppermute | solution.py:482
  24.6 7.0 %collective-permute-start.3 = (s32[8,8]{1,0:T(8,128)S(1)}, s32[8,8]{1,0:T(8,128)S(1)}, u32[]{:S(2)}, u32[]{:S(2)}) collective-permute-start(s32[8,8]{1,0:T(8,128)S(1)} %pad_add_fusion.own), channel_id=1, source_target_pairs={{0,1},{1,2},{2,3},{3,4},{4,5},{5,6},{6,7},{7,8},{8,9},{9,10},{10,1... | collective-permute-start | bytes 776 | tf_op jit(solution)/shard_map/ppermute | solution.py:500
  35.8 9.5 %collective-permute-start.6 = (bf16[848,128]{1,0:T(8,128)(2,1)S(1)}, bf16[848,128]{1,0:T(8,128)(2,1)S(1)}, u32[]{:S(2)}, u32[]{:S(2)}) collective-permute-start(bf16[848,128]{1,0:T(8,128)(2,1)S(1)} %get-tuple-element.19), channel_id=1, source_target_pairs={{0,64},{32,96},{64,0},{96,32},{1,65},{33,97},{65,1},{97,33},{2,66}... | collective-permute-start | bytes 651272 | tf_op jit(solution)/shard_map/ppermute | solution.py:482
  37.9 10.0 %collective-permute-start.7 = (bf16[848,128]{1,0:T(8,128)(2,1)S(1)}, bf16[848,128]{1,0:T(8,128)(2,1)S(1)}, u32[]{:S(2)}, u32[]{:S(2)}) collective-permute-start(bf16[848,128]{1,0:T(8,128)(2,1)S(1)} %get-tuple-element.20), channel_id=1, source_target_pairs={{0,32},{32,64},{64,96},{96,0},{1,33},{33,65},{65,97},{97,1},{2,34}... | collective-permute-start | bytes 651272 | tf_op jit(solution)/shard_map/ppermute | solution.py:482
  38.9 9.4 %collective-permute-start.8 = (bf16[848,128]{1,0:T(8,128)(2,1)S(1)}, bf16[848,128]{1,0:T(8,128)(2,1)S(1)}, u32[]{:S(2)}, u32[]{:S(2)}) collective-permute-start(bf16[848,128]{1,0:T(8,128)(2,1)S(1)} %get-tuple-element.21), channel_id=1, source_target_pairs={{0,96},{32,0},{64,32},{96,64},{1,97},{33,1},{65,33},{97,65},{2,98}... | collective-permute-start | bytes 651272 | tf_op jit(solution)/shard_map/ppermute | solution.py:482
  50.0 12.2 %collective-permute-start.12 = (bf16[528,128]{1,0:T(8,128)(2,1)S(1)}, bf16[528,128]{1,0:T(8,128)(2,1)S(1)}, u32[]{:S(2)}, u32[]{:S(2)}) collective-permute-start(bf16[528,128]{1,0:T(8,128)(2,1)S(1)} %get-tuple-element.27), channel_id=1, source_target_pairs={{0,1},{1,2},{2,3},{3,4},{4,5},{5,6},{6,7},{7,8},{8,9},{9,10},{10,1... | collective-permute-start | bytes 405512 | tf_op jit(solution)/shard_map/ppermute | solution.py:506
  51.9 7.7 %collective-permute-start.9 = (bf16[272,128]{1,0:T(8,128)(2,1)S(1)}, bf16[272,128]{1,0:T(8,128)(2,1)S(1)}, u32[]{:S(2)}, u32[]{:S(2)}) collective-permute-start(bf16[272,128]{1,0:T(8,128)(2,1)S(1)} %get-tuple-element.24), channel_id=1, source_target_pairs={{0,64},{32,96},{64,0},{96,32},{1,65},{33,97},{65,1},{97,33},{2,66}... | collective-permute-start | bytes 208904 | tf_op jit(solution)/shard_map/ppermute | solution.py:482
  56.4 5.5 %collective-permute-start.10 = (bf16[272,128]{1,0:T(8,128)(2,1)S(1)}, bf16[272,128]{1,0:T(8,128)(2,1)S(1)}, u32[]{:S(2)}, u32[]{:S(2)}) collective-permute-start(bf16[272,128]{1,0:T(8,128)(2,1)S(1)} %get-tuple-element.25), channel_id=1, source_target_pairs={{0,32},{32,64},{64,96},{96,0},{1,33},{33,65},{65,97},{97,1},{2,34}... | collective-permute-start | bytes 208904 | tf_op jit(solution)/shard_map/ppermute | solution.py:482
  57.9 4.3 %collective-permute-start.11 = (bf16[272,128]{1,0:T(8,128)(2,1)S(1)}, bf16[272,128]{1,0:T(8,128)(2,1)S(1)}, u32[]{:S(2)}, u32[]{:S(2)}) collective-permute-start(bf16[272,128]{1,0:T(8,128)(2,1)S(1)} %get-tuple-element.26), channel_id=1, source_target_pairs={{0,96},{32,0},{64,32},{96,64},{1,97},{33,1},{65,33},{97,65},{2,98}... | collective-permute-start | bytes 208904 | tf_op jit(solution)/shard_map/ppermute | solution.py:482

commit v7 on v6

--- a/solution.py
+++ b/solution.py
@@ -29,7 +29,8 @@
 CHUNK = SLOTS * BODY + 16
 SEND2 = SHIFTED * BODY + 16
 SEND3 = 4 * BODY + 16
-PAIRS, MOVES, WRITES = 48, 32, 8
+CODES, PLACED, LISTED = 16, 64, 192
+PAIRS, MOVES, WRITES, PLAN = 48, 8, 40, 128
 TWO = CHUNK
 THREE = CHUNK + SEND2
 POOL = THREE + 3 * SEND3
@@ -180,9 +181,8 @@
     )(records)
 
 
-VISITS = [(p, d) for p in range(HALF) for d in range(1, REACH + 1) if p + d >= HALF] + [
-    (p, d) for p in range(HALF, 12) for d in range(1, REACH + 1) if p < GROUP or p + d < 12
-]
+OWN = [(p, d) for p in range(HALF, 12) for d in range(1, REACH + 1) if p < GROUP or p + d < 12]
+BEFORE = [(p, d) for p in range(HALF) for d in range(1, REACH + 1) if p + d >= HALF]
 UPWARD = (
     ((0, 0), (1, 0), (1, 1), (2, 0), (2, 1), (3, 0), (3, 1)),
     ((2, 2), (3, 2), (3, 3)),
@@ -194,40 +194,57 @@
 
 
 def behind(owner):
-    return 2 * jnp.bitwise_and(seg_index() - owner, 3)
-
-
-def list_pairs(own, before, codes, slots):
+    apart = jnp.bitwise_xor(seg_index(), owner)
+    return 2 * jnp.bitwise_xor(apart, jnp.right_shift(apart, 1))
+
+
+def list_pairs(visits, used, table, codes, at, slots, placed):
     s = seg_index()
-    used = [jnp.int32(0)] * PLANES
     n = jnp.int32(0)
-    for p, d in VISITS:
+    for p, d in visits:
         row = p + HALF if p < HALF else p - HALF
         owner = row // 2
-        live = (before if p < HALF else own)[behind(owner) + row % 2, d - 1]
-        code = p + d * 16 + jnp.bitwise_and(owner - s, 3) * 256 + used[owner] * 4096
-        slots[p * REACH + d - 1] = used[owner]
+        live = table[behind(owner) + row % 2, d - 1]
+        code = p + d * 16 + jnp.bitwise_xor(owner, s) * 256 + used[owner] * 4096
+        slots[placed + p * REACH + d - 1] = used[owner]
         used[owner] = used[owner] + live
         if p in (6, 7) and p + d in (12, 13):
-            slots[96 + (p - 6) * 2 + p + d - 12] = used[0]
+            slots[placed + 96 + (p - 6) * 2 + p + d - 12] = used[0]
             code = code + (used[0] + 1) * 65536
             used[0] = used[0] + live
-        codes[n] = code
+        codes[at + n] = code
         n = n + live
     return n
 
 
-def list_moves(own, before, slots, moves):
+def list_body(own, listed):
+    used = [jnp.int32(0)] * 2 + [jnp.int32(SHIFTED)] * 2
+    listed[0] = list_pairs(OWN, used, own, listed, CODES, listed, PLACED)
+
+
+def list_own(own):
+    return pl.pallas_call(
+        list_body,
+        in_specs=[SMEM],
+        out_specs=SMEM,
+        out_shape=jax.ShapeDtypeStruct((LISTED,), jnp.int32),
+        compiler_params=pltpu.CompilerParams(vmem_limit_bytes=4 * MIB),
+        cost_estimate=TINY,
+        name="plan",
+    )(own)
+
+
+def plan_body(own, before, listed, slots, plan):
     s = seg_index()
     n = jnp.int32(0)
     for owner in (0, 1):
         for k, (i, j) in enumerate(UPWARD[owner]):
             p, d = HALF + i, GROUP + j - i
             entry = p * REACH + d - 1 if i // 2 == owner else 96 + (i - 2) * 2 + j
-            moves[n] = slots[entry] + k * 4096
+            plan[MOVES + n] = listed[PLACED + entry] + k * 4096
             n = n + jnp.where(s == owner, own[behind(i // 2) + i % 2, d - 1], 0)
     for r in range(1, PLANES):
-        to = jnp.bitwise_and(s + r, 3)
+        to = jnp.bitwise_xor(s, r)
         ahead = s < to
         for i in range(2):
             for j in range(2):
@@ -235,16 +252,14 @@
                 p = jnp.where(ahead, row + HALF, jnp.maximum(row - HALF, 0))
                 d = 2 * to + j - row + jnp.where(ahead, 0, GROUP)
                 live = jnp.where(ahead, own[i, d - 1], jnp.where(s >= 2, before[i, d - 1], 0))
-                moves[n] = slots[p * REACH + d - 1] + r * 256 + (2 * i + j) * 4096
+                entry = p * REACH + d - 1
+                slot = jnp.where(ahead, listed[PLACED + entry], slots[entry])
+                plan[MOVES + n] = slot + r * 256 + (2 * i + j) * 4096
                 n = n + live
-    return n
-
-
-def list_writes(own, before, slots, writes):
-    s = seg_index()
+    plan[0] = n
 
     def write(n, i, d, base, size, slot):
-        writes[WRITES + n] = base + slot * BODY + (base + size * BODY + slot) * 4096 + (i * 8 + d - 1) * 16777216
+        plan[WRITES + n] = base + slot * BODY + (base + size * BODY + slot) * 4096 + (i * 8 + d - 1) * 16777216
 
     n = jnp.int32(0)
     above = jnp.int32(0)
@@ -253,11 +268,11 @@
             row = 2 * s + i
             live = own[i, d - 1]
             shift = (row + d >= GROUP) & (s >= 2)
-            slot = jnp.where(shift, above, slots[(HALF + row) * REACH + d - 1])
+            slot = jnp.where(shift, above, listed[PLACED + (HALF + row) * REACH + d - 1])
             write(n, i, d, jnp.where(shift, TWO, 0), jnp.where(shift, SHIFTED, SLOTS), slot)
             n = n + live
             above = above + jnp.where(shift, live, 0)
-    writes[0] = n
+    plan[1] = n
     for j in range(2):
         for d in range(1, REACH + 1):
             low = 2 * s + j - d
@@ -271,20 +286,35 @@
             k0 = jnp.where(row == 0, 0, 2 * row - 1) + j
             k1 = jnp.where(row == 2, 0, 1) + j
             entry = jnp.maximum((HALF + low) * REACH + d - 1, 0)
-            slot = jnp.where(mine, slots[entry], 2 * (row - 2 * owner) + j)
+            slot = jnp.where(crossing, slots[entry], listed[PLACED + entry])
+            slot = jnp.where(mine, slot, 2 * (row - 2 * owner) + j)
             slot = jnp.where(up, jnp.where(s == 0, k0, k1), slot)
-            base = jnp.where(mine, 0, THREE + (jnp.bitwise_and(s - owner, 3) - 1) * SEND3)
+            base = jnp.where(mine, 0, THREE + (jnp.bitwise_xor(s, owner) - 1) * SEND3)
             base = jnp.where(up, TWO, base)
             size = jnp.where(mine, SLOTS, jnp.where(up, SHIFTED, 4))
             write(n, j, d, base, size, slot)
             n = n + live
-    writes[1] = n
+    plan[2] = n
+
+
+def make_plan(*args):
+    return pl.pallas_call(
+        plan_body,
+        in_specs=[SMEM] * 4,
+        out_specs=SMEM,
+        out_shape=jax.ShapeDtypeStruct((PLAN,), jnp.int32),
+        compiler_params=pltpu.CompilerParams(vmem_limit_bytes=4 * MIB),
+        cost_estimate=TINY,
+        name="plan",
+    )(*args)
 
 
 def correlate_body(
-    own, before, own_ext, own_int, got_ext, got_int, lag, keep, out1, out2, out3, slots, low, high, stk, pq, codes, last
+    listed, before, own_ext, own_int, got_ext, got_int, lag, keep, out1, out2, out3, slots, low, high, stk, pq, codes, last
 ):
-    count = list_pairs(own, before, codes, slots)
+    others = list_pairs(BEFORE, [jnp.int32(0)] * PLANES, before, codes, 0, slots, 0)
+    first = listed[0]
+    count = first + others
     core = jnp.bitwise_and(lax.axis_index("blk"), 1)
     sources = (
         (own_ext, HALF * (1 + core)),
@@ -306,8 +336,12 @@
         stk[r, pl.ds(pl.multiple_of(n * BODY, BODY), BODY), :] = stack[:BODY]
         stk[r, pl.ds(SLOTS * BODY + n, 1), :] = stack[BODY:LAGS]
 
-    def pair(n, carry):
-        code = codes[n]
+    def code_of(n):
+        mine = n < first
+        return jnp.where(mine, listed[CODES + jnp.where(mine, n, 0)], codes[jnp.where(mine, 0, n - first)])
+
+    def products(n, half):
+        code = code_of(n)
         p = jnp.bitwise_and(code, 15)
         d = jnp.bitwise_and(jnp.right_shift(code, 4), 15)
 
@@ -319,6 +353,7 @@
         grab(high, p + d)
         for chunk in range(CHANS // 16):
             rows = pl.ds(chunk * 16, 16)
+            to = pl.ds(half * CHANS + chunk * 16, 16)
             real = jnp.zeros((16, BINS), F32)
             imag = jnp.zeros((16, BINS), F32)
             for k in range(segs):
@@ -330,29 +365,46 @@
                 imag += are * bim - aim * bre
             rhi, rlo = halves(real)
             ihi, ilo = halves(imag)
-            pq[0, rows, :BINS] = rhi
-            pq[0, rows, BINS:] = ihi
-            pq[1, rows, :BINS] = rlo
-            pq[1, rows, BINS:] = ilo
-        both = dot(pq[0], lag[...])
-        stack = (both[:, :CHANS] + both[:, CHANS:] + dot(pq[1], lag[:, :CHANS])).T
+            pq[0, to, :BINS] = rhi
+            pq[0, to, BINS:] = ihi
+            pq[1, to, :BINS] = rlo
+            pq[1, to, BINS:] = ilo
+
+    def place(n, stack):
+        code = code_of(n)
         put(jnp.bitwise_and(jnp.right_shift(code, 8), 3), jnp.bitwise_and(jnp.right_shift(code, 12), 15), stack)
         second = jnp.right_shift(code, 16)
 
         @pl.when(second > 0)
         def _():
-            put(jnp.bitwise_and(-seg_index(), 3), second - 1, stack)
+            put(seg_index(), second - 1, stack)
+
+    def couple(m, carry):
+        n = 2 * m
+        products(n, 0)
+
+        @pl.when(n + 1 < count)
+        def _():
+            products(n + 1, 1)
+
+        both = dot(pq[0], lag[...])
+        stacks = both[:, :CHANS] + both[:, CHANS:] + dot(pq[1], lag[:, :CHANS])
+        place(n, stacks[:CHANS].T)
+
+        @pl.when(n + 1 < count)
+        def _():
+            place(n + 1, stacks[CHANS:].T)
 
         return carry
 
-    lax.fori_loop(0, count, pair, 0)
+    lax.fori_loop(0, (count + 1) // 2, couple, 0)
     keep[...] = stk[0]
     out1[...] = stk[1].astype(BF)
     out2[...] = stk[2].astype(BF)
     out3[...] = stk[3].astype(BF)
 
 
-def correlate(own, before, whites, lag):
+def correlate(listed, before, whites, lag):
     segs = whites[0].shape[1]
     chunk = jax.ShapeDtypeStruct((CHUNK, CHANS), BF)
     return pl.pallas_call(
@@ -370,24 +422,21 @@
             pltpu.VMEM((segs, CHANS, LENGTH), BF),
             pltpu.VMEM((segs, CHANS, LENGTH), BF),
             pltpu.VMEM((PLANES, CHUNK, CHANS), F32),
-            pltpu.VMEM((2, CHANS, LENGTH), BF),
+            pltpu.VMEM((2, 2 * CHANS, LENGTH), BF),
             pltpu.SMEM((PAIRS,), jnp.int32),
             pltpu.SMEM((1,), jnp.int32),
         ],
         compiler_params=pltpu.CompilerParams(vmem_limit_bytes=16 * MIB),
         cost_estimate=TINY,
         name="correlate",
-    )(own, before, *whites, lag)
-
-
-def combine_body(
-    own, before, slots, keep, got2, got1, got3, full, send, out1, out2, out3, writes, stage, moves
-):
-    count = list_moves(own, before, slots, moves)
+    )(listed, before, *whites, lag)
+
+
+def combine_body(plan, keep, got2, got1, got3, full, send, out1, out2, out3, stage):
     full[...] = (keep[...] + got1[...].astype(F32)) + (got2[...].astype(F32) + got3[...].astype(F32))
 
     def move(n, carry):
-        code = moves[n]
+        code = plan[MOVES + n]
         slot = jnp.bitwise_and(code, 255)
         message = jnp.bitwise_and(jnp.right_shift(code, 8), 15)
         k = jnp.right_shift(code, 12)
@@ -397,7 +446,7 @@
         stage[message, pl.ds(size * BODY + k, 1), :] = full[pl.ds(SLOTS * BODY + slot, 1), :]
         return carry
 
-    lax.fori_loop(0, count, move, 0)
+    lax.fori_loop(0, plan[0], move, 0)
 
     @pl.when(seg_index() >= 2)
     def _():
@@ -410,31 +459,29 @@
 
     for r, out in ((1, out1), (2, out2), (3, out3)):
         out[...] = stage[r, :SEND3].astype(BF)
-    list_writes(own, before, slots, writes)
 
 
 def combine(*args):
     third = jax.ShapeDtypeStruct((SEND3, CHANS), BF)
     return pl.pallas_call(
         combine_body,
-        in_specs=[SMEM] * 3 + [VMEM] * 4,
-        out_specs=[VMEM] * 5 + [SMEM],
+        in_specs=[SMEM] + [VMEM] * 4,
+        out_specs=[VMEM] * 5,
         out_shape=[
             jax.ShapeDtypeStruct((CHUNK, CHANS), F32),
             jax.ShapeDtypeStruct((SEND2, CHANS), BF),
             third,
             third,
             third,
-            jax.ShapeDtypeStruct((WRITES + 40,), jnp.int32),
         ],
-        scratch_shapes=[pltpu.VMEM((PLANES, SEND2, CHANS), F32), pltpu.SMEM((MOVES,), jnp.int32)],
+        scratch_shapes=[pltpu.VMEM((PLANES, SEND2, CHANS), F32)],
         compiler_params=pltpu.CompilerParams(vmem_limit_bytes=8 * MIB),
         cost_estimate=TINY,
         name="combine",
     )(*args)
 
 
-def finish_body(writes, full, got2, got1, got3, shifted, fwd, bwd, pool):
+def finish_body(plan, full, got2, got1, got3, shifted, fwd, bwd, pool):
     pool[:TWO, :] = full[...]
     pool[TWO:THREE, :] = shifted[...].astype(F32)
     for r, got in ((1, got1), (2, got2), (3, got3)):
@@ -443,7 +490,7 @@
     bwd[...] = jnp.zeros(bwd.shape, F32)
 
     def write(out, place, n):
-        code = writes[WRITES + n]
+        code = plan[WRITES + n]
         body = jnp.bitwise_and(code, 4095)
         i = jnp.right_shift(code, 27)
         at = pl.ds(jnp.bitwise_and(jnp.right_shift(code, 24), 7), 1)
@@ -459,8 +506,8 @@
         write(bwd, lambda m: BODY - m, n)
         return carry
 
-    lax.fori_loop(0, writes[0], ahead, 0)
-    lax.fori_loop(writes[0], writes[1], behind, 0)
+    lax.fori_loop(0, plan[1], ahead, 0)
+    lax.fori_loop(plan[1], plan[2], behind, 0)
 
 
 def finish(blocks, *args):
@@ -478,8 +525,8 @@
 
 
 def shards(groups, planes, lag, records, pairs):
-    def ring(x, r):
-        return lax.ppermute(x, "seg", [(z, (z + r) % planes) for z in range(planes)])
+    def across(x, r):
+        return lax.ppermute(x, "seg", [(z, z ^ r) for z in range(planes)])
 
     outer = [(g, g + 1 if g % 2 else g - 1) for g in range(1, groups - 1)]
     inner = [(g, g ^ 1) for g in range(groups)]
@@ -496,15 +543,16 @@
     own_int = whiten(False, records)
     got_int = lax.ppermute(own_int, "blk", inner)
     rows, _ = lax.optimization_barrier((pairs, own_int))
-    own = jnp.concatenate([rows, ring(rows, 1), ring(rows, 2), ring(rows, 3)])
+    own = jnp.concatenate([rows, across(rows, 1)])
+    own = jnp.concatenate([own, across(own, 3)])
     before = lax.ppermute(own, "blk", upward)
 
-    keep, out1, out2, out3, slots = correlate(own, before, (own_ext, own_int, got_ext, got_int), lag)
-    full, send, out1, out2, out3, writes = combine(
-        own, before, slots, keep, ring(out2, 2), ring(out1, 1), ring(out3, 3)
-    )
+    listed = list_own(own)
+    keep, out1, out2, out3, slots = correlate(listed, before, (own_ext, own_int, got_ext, got_int), lag)
+    plan = make_plan(own, before, listed, slots)
+    full, send, out1, out2, out3 = combine(plan, keep, across(out2, 2), across(out1, 1), across(out3, 3))
     shifted = lax.ppermute(send, ("seg", "blk"), shift)
-    outs = finish(pairs.shape[0], writes, full, ring(out2, 2), ring(out1, 1), ring(out3, 3), shifted)
+    outs = finish(pairs.shape[0], plan, full, across(out2, 2), across(out1, 1), across(out3, 3), shifted)
     return tuple(jnp.transpose(out, (0, 2, 1, 3)) for out in outs)
 
 

time: 65.1 us -> 65.8 us (1.011)
  the two profiles are of different devices: /device:TPU:4 before, /device:TPU:6 now
where the time goes in v7:
time: 65.8 us; the launch traced here: 66 us
  starting transfers between devices  26.8 us (41%)
  Pallas kernels  20.6 us (31%)
  waiting for transfers between devices  17.9 us (27%)
  between operations  0.75 us (1%)
    ppermute x8, starting transfers between devices, across(): return lax.ppermute(x, 'seg', [(z, z ^ r) for z in range(planes)])  18.1 us
    ppermute x8, waiting for transfers between devices, across(): return lax.ppermute(x, 'seg', [(z, z ^ r) for z in range(planes)])  14.1 us
    pallas_call x2, Pallas kernels, whiten(): pl.pallas_call(functools.partial(whiten_body, outer), in_specs=[pl.BlockS...  10.2 us
    pallas_call x1, Pallas kernels, correlate(): pl.pallas_call(correlate_body, in_specs=[SMEM] * 2 + [VMEM] * 5, out_spec...  4.77 us
    ppermute x1, starting transfers between devices, shards(): got_ext = lax.ppermute(own_ext, 'blk', outer)  4.74 us
    ppermute x1, waiting for transfers between devices, shards(): before = lax.ppermute(own, 'blk', upward)  3.78 us
    ppermute x1, starting transfers between devices, shards(): before = lax.ppermute(own, 'blk', upward)  1.92 us
    ppermute x1, starting transfers between devices, shards(): shifted = lax.ppermute(send, ('seg', 'blk'), shift)  1.92 us
  transfers between devices with their start and end apart: 12, of which 9 were waited for; matrix products, arithmetic and copies ran while one was open for 0% of the time, Pallas kernels for 12%

profile of v7, /device:TPU:6, one launch (start us, length us, event | category | flops | bytes accessed | tf_op | source)
XLA Modules:
  0.0 66.0 jit_solution(9984843891476337578)
XLA Ops:
  0.6 5.1 %whiten.3.own_ext = bf16[4,3,128,512]{3,2,1,0:T(8,128)(2,1)S(1)} custom-call(f32[3,1024,512]{2,1,0:T(8,128)} %records.3), custom_call_target="tpu_custom_call" | custom-call | flops 1 | bytes 1 | tf_op jit(solution)/shard_map/whiten/pallas_call | solution.py:168
  5.7 0.0 copy-start.1
  5.7 0.0 copy-start
  5.8 4.7 %collective-permute-start.3 = (bf16[4,3,128,512]{3,2,1,0:T(8,128)(2,1)S(1)}, bf16[4,3,128,512]{3,2,1,0:T(8,128)(2,1)S(1)}, u32[]{:S(2)}, u32[]{:S(2)}) collective-permute-start(bf16[4,3,128,512]{3,2,1,0:T(8,128)(2,1)S(1)} %whiten.3.own_ext), channel_id=1, source_target_pairs={{1,2},{2,1},{3,4},{4,3},{5,6},{6,5},{7,8},{8,7},{9,10},{10,9},{11,... | collective-permute-start | bytes 4718600 | tf_op jit(solution)/shard_map/ppermute | solution.py:542
  10.5 5.1 %whiten.2.own_int = bf16[4,3,128,512]{3,2,1,0:T(8,128)(2,1)S(1)} custom-call(f32[3,1024,512]{2,1,0:T(8,128)} %records.3), custom_call_target="tpu_custom_call" | custom-call | flops 1 | bytes 1 | tf_op jit(solution)/shard_map/whiten/pallas_call | solution.py:168
  15.6 0.1 collective-permute-start.4
  15.7 0.0 copy-done.1
  15.7 2.0 %collective-permute-start = (s32[2,8]{1,0:T(2,128)S(1)}, s32[2,8]{1,0:T(2,128)S(1)}, u32[]{:S(2)}, u32[]{:S(2)}) collective-permute-start(s32[2,8]{1,0:T(2,128)S(1)} %copy-done.1), channel_id=1, source_target_pairs={{0,32},{32,0},{64,96},{96,64},{1,33},{33,1},{65,97},{97,65},{2,34}... | collective-permute-start | bytes 200 | tf_op jit(solution)/shard_map/ppermute | solution.py:529
  17.7 1.7 %collective-permute-done = s32[2,8]{1,0:T(2,128)S(1)} collective-permute-done((s32[2,8]{1,0:T(2,128)S(1)}, s32[2,8]{1,0:T(2,128)S(1)}, u32[]{:S(2)}, u32[]{:S(2)}) %collective-permute-start) | collective-permute-done | bytes 96 | tf_op jit(solution)/shard_map/ppermute | solution.py:529
  19.4 4.1 %collective-permute-start.1 = (s32[4,8]{1,0:T(4,128)S(1)}, s32[4,8]{1,0:T(4,128)S(1)}, u32[]{:S(2)}, u32[]{:S(2)}) collective-permute-start(s32[4,8]{1,0:T(4,128)S(1)} %pad_add_fusion.1), channel_id=1, source_target_pairs={{0,96},{32,64},{64,32},{96,0},{1,97},{33,65},{65,33},{97,1},{2,98}... | collective-permute-start | bytes 392 | tf_op jit(solution)/shard_map/ppermute | solution.py:529
  23.5 1.6 %collective-permute-done.1 = s32[4,8]{1,0:T(4,128)S(1)} collective-permute-done((s32[4,8]{1,0:T(4,128)S(1)}, s32[4,8]{1,0:T(4,128)S(1)}, u32[]{:S(2)}, u32[]{:S(2)}) %collective-permute-start.1) | collective-permute-done | bytes 160 | tf_op jit(solution)/shard_map/ppermute | solution.py:529
  25.1 1.9 %collective-permute-start.2 = (s32[8,8]{1,0:T(8,128)S(1)}, s32[8,8]{1,0:T(8,128)S(1)}, u32[]{:S(2)}, u32[]{:S(2)}) collective-permute-start(s32[8,8]{1,0:T(8,128)S(1)} %pad_add_fusion.own), channel_id=1, source_target_pairs={{0,1},{1,2},{2,3},{3,4},{4,5},{5,6},{6,7},{7,8},{8,9},{9,10},{10,1... | collective-permute-start | bytes 776 | tf_op jit(solution)/shard_map/ppermute | solution.py:548
  27.0 1.3 %plan.2.listed = s32[192]{0:T(256)S(1)} custom-call(s32[8,8]{1,0:T(8,128)S(1)} %pad_add_fusion.own), custom_call_target="tpu_custom_call" | custom-call | flops 1 | bytes 1 | tf_op jit(solution)/shard_map/plan/pallas_call | solution.py:226
  28.3 3.8 %collective-permute-done.2.before = s32[8,8]{1,0:T(8,128)S(1)} collective-permute-done((s32[8,8]{1,0:T(8,128)S(1)}, s32[8,8]{1,0:T(8,128)S(1)}, u32[]{:S(2)}, u32[]{:S(2)}) %collective-permute-start.2) | collective-permute-done | bytes 288 | tf_op jit(solution)/shard_map/ppermute | solution.py:548
  32.1 0.0 collective-permute-done.3.got_ext
  32.1 0.0 collective-permute-done.4.got_int
  32.1 0.0 copy-done
  32.1 4.8 %correlate.1 = (f32[848,128]{1,0:T(8,128)S(1)}, bf16[848,128]{1,0:T(8,128)(2,1)S(1)}, bf16[848,128]{1,0:T(8,128)(2,1)S(1)}, bf16[848,128]{1,0:T(8,128)(2,1)S(1)}, s32[128]{0:T(128)S(1)}) custom-call(s32[192]{0:T(256)S(1)} %plan.2.listed, s32[8,8]{1,0:T(8,128)S(1)} %collective-permute-done.2.before, bf16[4,3,128,512]{3,2,1,0:T(8,128)(2,1)S(1)} %whiten.3.own_ext, ...), custom_call_target="tpu_custom_call" | custom-call | flops 1 | bytes 1 | tf_op jit(solution)/shard_map/correlate/pallas_call | solution.py:410
  36.9 1.9 %collective-permute-start.5 = (bf16[848,128]{1,0:T(8,128)(2,1)S(1)}, bf16[848,128]{1,0:T(8,128)(2,1)S(1)}, u32[]{:S(2)}, u32[]{:S(2)}) collective-permute-start(bf16[848,128]{1,0:T(8,128)(2,1)S(1)} %get-tuple-element.18), channel_id=1, source_target_pairs={{0,64},{32,96},{64,0},{96,32},{1,65},{33,97},{65,1},{97,33},{2,66}... | collective-permute-start | bytes 651272 | tf_op jit(solution)/shard_map/ppermute | solution.py:529
  38.8 2.2 %collective-permute-start.6 = (bf16[848,128]{1,0:T(8,128)(2,1)S(1)}, bf16[848,128]{1,0:T(8,128)(2,1)S(1)}, u32[]{:S(2)}, u32[]{:S(2)}) collective-permute-start(bf16[848,128]{1,0:T(8,128)(2,1)S(1)} %get-tuple-element.19), channel_id=1, source_target_pairs={{0,32},{32,0},{64,96},{96,64},{1,33},{33,1},{65,97},{97,65},{2,34}... | collective-permute-start | bytes 651272 | tf_op jit(solution)/shard_map/ppermute | solution.py:529
  41.0 0.0 collective-permute-start.7
  41.1 1.7 %plan.3 = s32[128]{0:T(128)S(1)} custom-call(s32[8,8]{1,0:T(8,128)S(1)} %pad_add_fusion.own, s32[8,8]{1,0:T(8,128)S(1)} %collective-permute-done.2.before, s32[192]{0:T(256)S(1)} %plan.2.listed, s32[128]{0:T(128)S(1)} %get-tuple-element.16.slots), custom_call_target="tpu_custom_call" | custom-call | flops 1 | bytes 1 | tf_op jit(solution)/shard_map/plan/pallas_call | solution.py:301
  42.8 1.7 %collective-permute-done.5.got2 = bf16[848,128]{1,0:T(8,128)(2,1)S(1)} collective-permute-done((bf16[848,128]{1,0:T(8,128)(2,1)S(1)}, bf16[848,128]{1,0:T(8,128)(2,1)S(1)}, u32[]{:S(2)}, u32[]{:S(2)}) %collective-permute-start.5) | collective-permute-done | bytes 217120 | tf_op jit(solution)/shard_map/ppermute | solution.py:529
  44.5 2.8 %collective-permute-done.6.got1 = bf16[848,128]{1,0:T(8,128)(2,1)S(1)} collective-permute-done((bf16[848,128]{1,0:T(8,128)(2,1)S(1)}, bf16[848,128]{1,0:T(8,128)(2,1)S(1)}, u32[]{:S(2)}, u32[]{:S(2)}) %collective-permute-start.6) | collective-permute-done | bytes 217120 | tf_op jit(solution)/shard_map/ppermute | solution.py:529
  47.3 0.9 %collective-permute-done.7.got3 = bf16[848,128]{1,0:T(8,128)(2,1)S(1)} collective-permute-done((bf16[848,128]{1,0:T(8,128)(2,1)S(1)}, bf16[848,128]{1,0:T(8,128)(2,1)S(1)}, u32[]{:S(2)}, u32[]{:S(2)}) %collective-permute-start.7) | collective-permute-done | bytes 217120 | tf_op jit(solution)/shard_map/ppermute | solution.py:529
  48.1 0.7 %combine.1 = (f32[848,128]{1,0:T(8,128)S(1)}, bf16[528,128]{1,0:T(8,128)(2,1)S(1)}, bf16[272,128]{1,0:T(8,128)(2,1)S(1)}, bf16[272,128]{1,0:T(8,128)(2,1)S(1)}, bf16[272,128]{1,0:T(8,128)(2,1)S(1)}) custom-call(s32[128]{0:T(128)S(1)} %plan.3, f32[848,128]{1,0:T(8,128)S(1)} %get-tuple-element.17.keep, bf16[848,128]{1,0:T(8,128)(2,1)S(1)} %collective-permute-done.5.got2, ...), custom_call_target="tpu_custom_call" | custom-call | flops 1 | bytes 1 | tf_op jit(solution)/shard_map/combine/pallas_call | solution.py:466
  48.9 1.9 %collective-permute-start.11 = (bf16[528,128]{1,0:T(8,128)(2,1)S(1)}, bf16[528,128]{1,0:T(8,128)(2,1)S(1)}, u32[]{:S(2)}, u32[]{:S(2)}) collective-permute-start(bf16[528,128]{1,0:T(8,128)(2,1)S(1)} %get-tuple-element.25), channel_id=1, source_target_pairs={{0,1},{1,2},{2,3},{3,4},{4,5},{5,6},{6,7},{7,8},{8,9},{9,10},{10,1... | collective-permute-start | bytes 405512 | tf_op jit(solution)/shard_map/ppermute | solution.py:554
  50.8 6.8 %collective-permute-start.8 = (bf16[272,128]{1,0:T(8,128)(2,1)S(1)}, bf16[272,128]{1,0:T(8,128)(2,1)S(1)}, u32[]{:S(2)}, u32[]{:S(2)}) collective-permute-start(bf16[272,128]{1,0:T(8,128)(2,1)S(1)} %get-tuple-element.22), channel_id=1, source_target_pairs={{0,64},{32,96},{64,0},{96,32},{1,65},{33,97},{65,1},{97,33},{2,66}... | collective-permute-start | bytes 208904 | tf_op jit(solution)/shard_map/ppermute | solution.py:529
  57.6 1.0 %collective-permute-start.9 = (bf16[272,128]{1,0:T(8,128)(2,1)S(1)}, bf16[272,128]{1,0:T(8,128)(2,1)S(1)}, u32[]{:S(2)}, u32[]{:S(2)}) collective-permute-start(bf16[272,128]{1,0:T(8,128)(2,1)S(1)} %get-tuple-element.23), channel_id=1, source_target_pairs={{0,32},{32,0},{64,96},{96,64},{1,33},{33,1},{65,97},{97,65},{2,34}... | collective-permute-start | bytes 208904 | tf_op jit(solution)/shard_map/ppermute | solution.py:529
  58.7 0.0 collective-permute-start.10
  58.7 1.3 %collective-permute-done.8.got2 = bf16[272,128]{1,0:T(8,128)(2,1)S(1)} collective-permute-done((bf16[272,128]{1,0:T(8,128)(2,1)S(1)}, bf16[272,128]{1,0:T(8,128)(2,1)S(1)}, u32[]{:S(2)}, u32[]{:S(2)}) %collective-permute-start.8) | collective-permute-done | bytes 69664 | tf_op jit(solution)/shard_map/ppermute | solution.py:529
  59.9 2.0 %collective-permute-done.9.got1 = bf16[272,128]{1,0:T(8,128)(2,1)S(1)} collective-permute-done((bf16[272,128]{1,0:T(8,128)(2,1)S(1)}, bf16[272,128]{1,0:T(8,128)(2,1)S(1)}, u32[]{:S(2)}, u32[]{:S(2)}) %collective-permute-start.9) | collective-permute-done | bytes 69664 | tf_op jit(solution)/shard_map/ppermute | solution.py:529
  62.0 2.2 %collective-permute-done.10.got3 = bf16[272,128]{1,0:T(8,128)(2,1)S(1)} collective-permute-done((bf16[272,128]{1,0:T(8,128)(2,1)S(1)}, bf16[272,128]{1,0:T(8,128)(2,1)S(1)}, u32[]{:S(2)}, u32[]{:S(2)}) %collective-permute-start.10) | collective-permute-done | bytes 69664 | tf_op jit(solution)/shard_map/ppermute | solution.py:529
  64.2 0.0 collective-permute-done.11.shifted
  64.2 1.8 %finish.1 = (f32[2,65,8,128]{3,2,1,0:T(8,128)}, f32[2,65,8,128]{3,2,1,0:T(8,128)}) custom-call(s32[128]{0:T(128)S(1)} %plan.3, f32[848,128]{1,0:T(8,128)S(1)} %get-tuple-element.21.full, bf16[272,128]{1,0:T(8,128)(2,1)S(1)} %collective-permute-done.8.got2, bf16[272,128]{1,0:T(8,128)(2,1)S(1)} %collective-permute-done.9.got1, ...), custom_call_target="tpu_custom_call" | custom-call | flops 1 | bytes 1 | tf_op jit(solution)/shard_map/finish/pallas_call | solution.py:515
  (2 shorter events, 0.0 us)
Async XLA Ops:
  5.7 10.0 %copy-start.1 = (s32[2,8]{1,0:T(2,128)S(1)}, s32[2,8]{1,0:T(2,128)}, u32[]{:S(2)}) copy-start(s32[2,8]{1,0:T(2,128)} %param.4) | copy-start | bytes 196
  5.7 26.3 %copy-start = (bf16[512,256]{1,0:T(8,128)(2,1)S(1)}, bf16[512,256]{1,0:T(8,128)(2,1)}, u32[]{:S(2)}) copy-start(bf16[512,256]{1,0:T(8,128)(2,1)} %constant.2.clone.lag) | copy-start | bytes 786436
  5.8 26.3 %collective-permute-start.3 = (bf16[4,3,128,512]{3,2,1,0:T(8,128)(2,1)S(1)}, bf16[4,3,128,512]{3,2,1,0:T(8,128)(2,1)S(1)}, u32[]{:S(2)}, u32[]{:S(2)}) collective-permute-start(bf16[4,3,128,512]{3,2,1,0:T(8,128)(2,1)S(1)} %whiten.3.own_ext), channel_id=1, source_target_pairs={{1,2},{2,1},{3,4},{4,3},{5,6},{6,5},{7,8},{8,7},{9,10},{10,9},{11,... | collective-permute-start | bytes 4718600 | tf_op jit(solution)/shard_map/ppermute | solution.py:542
  15.6 16.5 %collective-permute-start.4 = (bf16[4,3,128,512]{3,2,1,0:T(8,128)(2,1)S(1)}, bf16[4,3,128,512]{3,2,1,0:T(8,128)(2,1)S(1)}, u32[]{:S(2)}, u32[]{:S(2)}) collective-permute-start(bf16[4,3,128,512]{3,2,1,0:T(8,128)(2,1)S(1)} %whiten.2.own_int), channel_id=1, source_target_pairs={{0,1},{1,0},{2,3},{3,2},{4,5},{5,4},{6,7},{7,6},{8,9},{9,8},{10,11... | collective-permute-start | bytes 4718600 | tf_op jit(solution)/shard_map/ppermute | solution.py:544
  15.7 3.6 %collective-permute-start = (s32[2,8]{1,0:T(2,128)S(1)}, s32[2,8]{1,0:T(2,128)S(1)}, u32[]{:S(2)}, u32[]{:S(2)}) collective-permute-start(s32[2,8]{1,0:T(2,128)S(1)} %copy-done.1), channel_id=1, source_target_pairs={{0,32},{32,0},{64,96},{96,64},{1,33},{33,1},{65,97},{97,65},{2,34}... | collective-permute-start | bytes 200 | tf_op jit(solution)/shard_map/ppermute | solution.py:529
  19.4 5.7 %collective-permute-start.1 = (s32[4,8]{1,0:T(4,128)S(1)}, s32[4,8]{1,0:T(4,128)S(1)}, u32[]{:S(2)}, u32[]{:S(2)}) collective-permute-start(s32[4,8]{1,0:T(4,128)S(1)} %pad_add_fusion.1), channel_id=1, source_target_pairs={{0,96},{32,64},{64,32},{96,0},{1,97},{33,65},{65,33},{97,1},{2,98}... | collective-permute-start | bytes 392 | tf_op jit(solution)/shard_map/ppermute | solution.py:529
  25.1 7.0 %collective-permute-start.2 = (s32[8,8]{1,0:T(8,128)S(1)}, s32[8,8]{1,0:T(8,128)S(1)}, u32[]{:S(2)}, u32[]{:S(2)}) collective-permute-start(s32[8,8]{1,0:T(8,128)S(1)} %pad_add_fusion.own), channel_id=1, source_target_pairs={{0,1},{1,2},{2,3},{3,4},{4,5},{5,6},{6,7},{7,8},{8,9},{9,10},{10,1... | collective-permute-start | bytes 776 | tf_op jit(solution)/shard_map/ppermute | solution.py:548
  36.9 7.6 %collective-permute-start.5 = (bf16[848,128]{1,0:T(8,128)(2,1)S(1)}, bf16[848,128]{1,0:T(8,128)(2,1)S(1)}, u32[]{:S(2)}, u32[]{:S(2)}) collective-permute-start(bf16[848,128]{1,0:T(8,128)(2,1)S(1)} %get-tuple-element.18), channel_id=1, source_target_pairs={{0,64},{32,96},{64,0},{96,32},{1,65},{33,97},{65,1},{97,33},{2,66}... | collective-permute-start | bytes 651272 | tf_op jit(solution)/shard_map/ppermute | solution.py:529
  38.8 8.5 %collective-permute-start.6 = (bf16[848,128]{1,0:T(8,128)(2,1)S(1)}, bf16[848,128]{1,0:T(8,128)(2,1)S(1)}, u32[]{:S(2)}, u32[]{:S(2)}) collective-permute-start(bf16[848,128]{1,0:T(8,128)(2,1)S(1)} %get-tuple-element.19), channel_id=1, source_target_pairs={{0,32},{32,0},{64,96},{96,64},{1,33},{33,1},{65,97},{97,65},{2,34}... | collective-permute-start | bytes 651272 | tf_op jit(solution)/shard_map/ppermute | solution.py:529
  41.0 7.1 %collective-permute-start.7 = (bf16[848,128]{1,0:T(8,128)(2,1)S(1)}, bf16[848,128]{1,0:T(8,128)(2,1)S(1)}, u32[]{:S(2)}, u32[]{:S(2)}) collective-permute-start(bf16[848,128]{1,0:T(8,128)(2,1)S(1)} %get-tuple-element.20), channel_id=1, source_target_pairs={{0,96},{32,64},{64,32},{96,0},{1,97},{33,65},{65,33},{97,1},{2,98}... | collective-permute-start | bytes 651272 | tf_op jit(solution)/shard_map/ppermute | solution.py:529
  48.9 15.3 %collective-permute-start.11 = (bf16[528,128]{1,0:T(8,128)(2,1)S(1)}, bf16[528,128]{1,0:T(8,128)(2,1)S(1)}, u32[]{:S(2)}, u32[]{:S(2)}) collective-permute-start(bf16[528,128]{1,0:T(8,128)(2,1)S(1)} %get-tuple-element.25), channel_id=1, source_target_pairs={{0,1},{1,2},{2,3},{3,4},{4,5},{5,6},{6,7},{7,8},{8,9},{9,10},{10,1... | collective-permute-start | bytes 405512 | tf_op jit(solution)/shard_map/ppermute | solution.py:554
  50.8 9.1 %collective-permute-start.8 = (bf16[272,128]{1,0:T(8,128)(2,1)S(1)}, bf16[272,128]{1,0:T(8,128)(2,1)S(1)}, u32[]{:S(2)}, u32[]{:S(2)}) collective-permute-start(bf16[272,128]{1,0:T(8,128)(2,1)S(1)} %get-tuple-element.22), channel_id=1, source_target_pairs={{0,64},{32,96},{64,0},{96,32},{1,65},{33,97},{65,1},{97,33},{2,66}... | collective-permute-start | bytes 208904 | tf_op jit(solution)/shard_map/ppermute | solution.py:529
  57.6 4.3 %collective-permute-start.9 = (bf16[272,128]{1,0:T(8,128)(2,1)S(1)}, bf16[272,128]{1,0:T(8,128)(2,1)S(1)}, u32[]{:S(2)}, u32[]{:S(2)}) collective-permute-start(bf16[272,128]{1,0:T(8,128)(2,1)S(1)} %get-tuple-element.23), channel_id=1, source_target_pairs={{0,32},{32,0},{64,96},{96,64},{1,33},{33,1},{65,97},{97,65},{2,34}... | collective-permute-start | bytes 208904 | tf_op jit(solution)/shard_map/ppermute | solution.py:529
  58.7 5.5 %collective-permute-start.10 = (bf16[272,128]{1,0:T(8,128)(2,1)S(1)}, bf16[272,128]{1,0:T(8,128)(2,1)S(1)}, u32[]{:S(2)}, u32[]{:S(2)}) collective-permute-start(bf16[272,128]{1,0:T(8,128)(2,1)S(1)} %get-tuple-element.24), channel_id=1, source_target_pairs={{0,96},{32,64},{64,32},{96,0},{1,97},{33,65},{65,33},{97,1},{2,98}... | collective-permute-start | bytes 208904 | tf_op jit(solution)/shard_map/ppermute | solution.py:529

commit v8 on v6

--- a/solution.py
+++ b/solution.py
@@ -29,7 +29,7 @@
 CHUNK = SLOTS * BODY + 16
 SEND2 = SHIFTED * BODY + 16
 SEND3 = 4 * BODY + 16
-PAIRS, MOVES, WRITES = 48, 32, 8
+PAIRS, MOVES, WRITES, PLAN = 48, 8, 40, 128
 TWO = CHUNK
 THREE = CHUNK + SEND2
 POOL = THREE + 3 * SEND3
@@ -194,7 +194,8 @@
 
 
 def behind(owner):
-    return 2 * jnp.bitwise_and(seg_index() - owner, 3)
+    apart = jnp.bitwise_xor(seg_index(), owner)
+    return 2 * jnp.bitwise_xor(apart, jnp.right_shift(apart, 1))
 
 
 def list_pairs(own, before, codes, slots):
@@ -205,7 +206,7 @@
         row = p + HALF if p < HALF else p - HALF
         owner = row // 2
         live = (before if p < HALF else own)[behind(owner) + row % 2, d - 1]
-        code = p + d * 16 + jnp.bitwise_and(owner - s, 3) * 256 + used[owner] * 4096
+        code = p + d * 16 + jnp.bitwise_xor(owner, s) * 256 + used[owner] * 4096
         slots[p * REACH + d - 1] = used[owner]
         used[owner] = used[owner] + live
         if p in (6, 7) and p + d in (12, 13):
@@ -217,17 +218,17 @@
     return n
 
 
-def list_moves(own, before, slots, moves):
+def plan_body(own, before, slots, plan):
     s = seg_index()
     n = jnp.int32(0)
     for owner in (0, 1):
         for k, (i, j) in enumerate(UPWARD[owner]):
             p, d = HALF + i, GROUP + j - i
             entry = p * REACH + d - 1 if i // 2 == owner else 96 + (i - 2) * 2 + j
-            moves[n] = slots[entry] + k * 4096
+            plan[MOVES + n] = slots[entry] + k * 4096
             n = n + jnp.where(s == owner, own[behind(i // 2) + i % 2, d - 1], 0)
     for r in range(1, PLANES):
-        to = jnp.bitwise_and(s + r, 3)
+        to = jnp.bitwise_xor(s, r)
         ahead = s < to
         for i in range(2):
             for j in range(2):
@@ -235,16 +236,12 @@
                 p = jnp.where(ahead, row + HALF, jnp.maximum(row - HALF, 0))
                 d = 2 * to + j - row + jnp.where(ahead, 0, GROUP)
                 live = jnp.where(ahead, own[i, d - 1], jnp.where(s >= 2, before[i, d - 1], 0))
-                moves[n] = slots[p * REACH + d - 1] + r * 256 + (2 * i + j) * 4096
+                plan[MOVES + n] = slots[p * REACH + d - 1] + r * 256 + (2 * i + j) * 4096
                 n = n + live
-    return n
-
-
-def list_writes(own, before, slots, writes):
-    s = seg_index()
+    plan[0] = n
 
     def write(n, i, d, base, size, slot):
-        writes[WRITES + n] = base + slot * BODY + (base + size * BODY + slot) * 4096 + (i * 8 + d - 1) * 16777216
+        plan[WRITES + n] = base + slot * BODY + (base + size * BODY + slot) * 4096 + (i * 8 + d - 1) * 16777216
 
     n = jnp.int32(0)
     above = jnp.int32(0)
@@ -257,7 +254,7 @@
             write(n, i, d, jnp.where(shift, TWO, 0), jnp.where(shift, SHIFTED, SLOTS), slot)
             n = n + live
             above = above + jnp.where(shift, live, 0)
-    writes[0] = n
+    plan[1] = n
     for j in range(2):
         for d in range(1, REACH + 1):
             low = 2 * s + j - d
@@ -273,16 +270,28 @@
             entry = jnp.maximum((HALF + low) * REACH + d - 1, 0)
             slot = jnp.where(mine, slots[entry], 2 * (row - 2 * owner) + j)
             slot = jnp.where(up, jnp.where(s == 0, k0, k1), slot)
-            base = jnp.where(mine, 0, THREE + (jnp.bitwise_and(s - owner, 3) - 1) * SEND3)
+            base = jnp.where(mine, 0, THREE + (jnp.bitwise_xor(s, owner) - 1) * SEND3)
             base = jnp.where(up, TWO, base)
             size = jnp.where(mine, SLOTS, jnp.where(up, SHIFTED, 4))
             write(n, j, d, base, size, slot)
             n = n + live
-    writes[1] = n
+    plan[2] = n
+
+
+def make_plan(*args):
+    return pl.pallas_call(
+        plan_body,
+        in_specs=[SMEM] * 3,
+        out_specs=SMEM,
+        out_shape=jax.ShapeDtypeStruct((PLAN,), jnp.int32),
+        compiler_params=pltpu.CompilerParams(vmem_limit_bytes=4 * MIB),
+        cost_estimate=TINY,
+        name="plan",
+    )(*args)
 
 
 def correlate_body(
-    own, before, own_ext, own_int, got_ext, got_int, lag, keep, out1, out2, out3, slots, low, high, stk, pq, codes, last
+    own, before, own_ext, own_int, got_ext, got_int, lag, keep, out1, out2, out3, slots, low, tails, pq, codes, last
 ):
     count = list_pairs(own, before, codes, slots)
     core = jnp.bitwise_and(lax.axis_index("blk"), 1)
@@ -303,20 +312,20 @@
                 dest[...] = ref[block - begin]
 
     def put(r, n, stack):
-        stk[r, pl.ds(pl.multiple_of(n * BODY, BODY), BODY), :] = stack[:BODY]
-        stk[r, pl.ds(SLOTS * BODY + n, 1), :] = stack[BODY:LAGS]
-
-    def pair(n, carry):
-        code = codes[n]
-        p = jnp.bitwise_and(code, 15)
-        d = jnp.bitwise_and(jnp.right_shift(code, 4), 15)
-
-        @pl.when(last[0] != p)
+        tails[r, pl.ds(n, 1), :] = stack[BODY:LAGS]
+        body = pl.ds(pl.multiple_of(n * BODY, BODY), BODY)
+
+        @pl.when(r == 0)
         def _():
-            grab(low, p)
-            last[0] = p
-
-        grab(high, p + d)
+            keep[body, :] = stack[:BODY]
+
+        for k, out in ((1, out1), (2, out2), (3, out3)):
+
+            @pl.when(r == k)
+            def _(out=out):
+                out[body, :] = stack[:BODY].astype(BF)
+
+    def products(high, block):
         for chunk in range(CHANS // 16):
             rows = pl.ds(chunk * 16, 16)
             real = jnp.zeros((16, BINS), F32)
@@ -324,8 +333,8 @@
             for k in range(segs):
                 are = low[k, rows, :BINS].astype(F32)
                 aim = low[k, rows, BINS:].astype(F32)
-                bre = high[k, rows, :BINS].astype(F32)
-                bim = high[k, rows, BINS:].astype(F32)
+                bre = high[block, k, rows, :BINS].astype(F32)
+                bim = high[block, k, rows, BINS:].astype(F32)
                 real += are * bre + aim * bim
                 imag += are * bim - aim * bre
             rhi, rlo = halves(real)
@@ -334,6 +343,23 @@
             pq[0, rows, BINS:] = ihi
             pq[1, rows, :BINS] = rlo
             pq[1, rows, BINS:] = ilo
+
+    def pair(n, carry):
+        code = codes[n]
+        p = jnp.bitwise_and(code, 15)
+        d = jnp.bitwise_and(jnp.right_shift(code, 4), 15)
+
+        @pl.when(last[0] != p)
+        def _():
+            grab(low, p)
+            last[0] = p
+
+        for ref, begin in sources:
+
+            @pl.when((p + d >= begin) & (p + d < begin + HALF))
+            def _(ref=ref, begin=begin):
+                products(ref, p + d - begin)
+
         both = dot(pq[0], lag[...])
         stack = (both[:, :CHANS] + both[:, CHANS:] + dot(pq[1], lag[:, :CHANS])).T
         put(jnp.bitwise_and(jnp.right_shift(code, 8), 3), jnp.bitwise_and(jnp.right_shift(code, 12), 15), stack)
@@ -341,15 +367,14 @@
 
         @pl.when(second > 0)
         def _():
-            put(jnp.bitwise_and(-seg_index(), 3), second - 1, stack)
+            put(seg_index(), second - 1, stack)
 
         return carry
 
     lax.fori_loop(0, count, pair, 0)
-    keep[...] = stk[0]
-    out1[...] = stk[1].astype(BF)
-    out2[...] = stk[2].astype(BF)
-    out3[...] = stk[3].astype(BF)
+    keep[SLOTS * BODY :, :] = tails[0]
+    for k, out in ((1, out1), (2, out2), (3, out3)):
+        out[SLOTS * BODY :, :] = tails[k].astype(BF)
 
 
 def correlate(own, before, whites, lag):
@@ -368,8 +393,7 @@
         ],
         scratch_shapes=[
             pltpu.VMEM((segs, CHANS, LENGTH), BF),
-            pltpu.VMEM((segs, CHANS, LENGTH), BF),
-            pltpu.VMEM((PLANES, CHUNK, CHANS), F32),
+            pltpu.VMEM((PLANES, 16, CHANS), F32),
             pltpu.VMEM((2, CHANS, LENGTH), BF),
             pltpu.SMEM((PAIRS,), jnp.int32),
             pltpu.SMEM((1,), jnp.int32),
@@ -380,14 +404,11 @@
     )(own, before, *whites, lag)
 
 
-def combine_body(
-    own, before, slots, keep, got2, got1, got3, full, send, out1, out2, out3, writes, stage, moves
-):
-    count = list_moves(own, before, slots, moves)
+def combine_body(plan, keep, got2, got1, got3, full, send, out1, out2, out3, stage):
     full[...] = (keep[...] + got1[...].astype(F32)) + (got2[...].astype(F32) + got3[...].astype(F32))
 
     def move(n, carry):
-        code = moves[n]
+        code = plan[MOVES + n]
         slot = jnp.bitwise_and(code, 255)
         message = jnp.bitwise_and(jnp.right_shift(code, 8), 15)
         k = jnp.right_shift(code, 12)
@@ -397,7 +418,7 @@
         stage[message, pl.ds(size * BODY + k, 1), :] = full[pl.ds(SLOTS * BODY + slot, 1), :]
         return carry
 
-    lax.fori_loop(0, count, move, 0)
+    lax.fori_loop(0, plan[0], move, 0)
 
     @pl.when(seg_index() >= 2)
     def _():
@@ -410,31 +431,29 @@
 
     for r, out in ((1, out1), (2, out2), (3, out3)):
         out[...] = stage[r, :SEND3].astype(BF)
-    list_writes(own, before, slots, writes)
 
 
 def combine(*args):
     third = jax.ShapeDtypeStruct((SEND3, CHANS), BF)
     return pl.pallas_call(
         combine_body,
-        in_specs=[SMEM] * 3 + [VMEM] * 4,
-        out_specs=[VMEM] * 5 + [SMEM],
+        in_specs=[SMEM] + [VMEM] * 4,
+        out_specs=[VMEM] * 5,
         out_shape=[
             jax.ShapeDtypeStruct((CHUNK, CHANS), F32),
             jax.ShapeDtypeStruct((SEND2, CHANS), BF),
             third,
             third,
             third,
-            jax.ShapeDtypeStruct((WRITES + 40,), jnp.int32),
         ],
-        scratch_shapes=[pltpu.VMEM((PLANES, SEND2, CHANS), F32), pltpu.SMEM((MOVES,), jnp.int32)],
+        scratch_shapes=[pltpu.VMEM((PLANES, SEND2, CHANS), F32)],
         compiler_params=pltpu.CompilerParams(vmem_limit_bytes=8 * MIB),
         cost_estimate=TINY,
         name="combine",
     )(*args)
 
 
-def finish_body(writes, full, got2, got1, got3, shifted, fwd, bwd, pool):
+def finish_body(plan, full, got2, got1, got3, shifted, fwd, bwd, pool):
     pool[:TWO, :] = full[...]
     pool[TWO:THREE, :] = shifted[...].astype(F32)
     for r, got in ((1, got1), (2, got2), (3, got3)):
@@ -443,7 +462,7 @@
     bwd[...] = jnp.zeros(bwd.shape, F32)
 
     def write(out, place, n):
-        code = writes[WRITES + n]
+        code = plan[WRITES + n]
         body = jnp.bitwise_and(code, 4095)
         i = jnp.right_shift(code, 27)
         at = pl.ds(jnp.bitwise_and(jnp.right_shift(code, 24), 7), 1)
@@ -459,8 +478,8 @@
         write(bwd, lambda m: BODY - m, n)
         return carry
 
-    lax.fori_loop(0, writes[0], ahead, 0)
-    lax.fori_loop(writes[0], writes[1], behind, 0)
+    lax.fori_loop(0, plan[1], ahead, 0)
+    lax.fori_loop(plan[1], plan[2], behind, 0)
 
 
 def finish(blocks, *args):
@@ -478,8 +497,8 @@
 
 
 def shards(groups, planes, lag, records, pairs):
-    def ring(x, r):
-        return lax.ppermute(x, "seg", [(z, (z + r) % planes) for z in range(planes)])
+    def across(x, r):
+        return lax.ppermute(x, "seg", [(z, z ^ r) for z in range(planes)])
 
     outer = [(g, g + 1 if g % 2 else g - 1) for g in range(1, groups - 1)]
     inner = [(g, g ^ 1) for g in range(groups)]
@@ -496,15 +515,15 @@
     own_int = whiten(False, records)
     got_int = lax.ppermute(own_int, "blk", inner)
     rows, _ = lax.optimization_barrier((pairs, own_int))
-    own = jnp.concatenate([rows, ring(rows, 1), ring(rows, 2), ring(rows, 3)])
+    own = jnp.concatenate([rows, across(rows, 1)])
+    own = jnp.concatenate([own, across(own, 3)])
     before = lax.ppermute(own, "blk", upward)
 
     keep, out1, out2, out3, slots = correlate(own, before, (own_ext, own_int, got_ext, got_int), lag)
-    full, send, out1, out2, out3, writes = combine(
-        own, before, slots, keep, ring(out2, 2), ring(out1, 1), ring(out3, 3)
-    )
+    plan = make_plan(own, before, slots)
+    full, send, out1, out2, out3 = combine(plan, keep, across(out2, 2), across(out1, 1), across(out3, 3))
     shifted = lax.ppermute(send, ("seg", "blk"), shift)
-    outs = finish(pairs.shape[0], writes, full, ring(out2, 2), ring(out1, 1), ring(out3, 3), shifted)
+    outs = finish(pairs.shape[0], plan, full, across(out2, 2), across(out1, 1), across(out3, 3), shifted)
     return tuple(jnp.transpose(out, (0, 2, 1, 3)) for out in outs)
 
 

time: 65.1 us -> 67 us (1.029)
  the two profiles are of different devices: /device:TPU:4 before, /device:TPU:6 now
where the time goes in v8:
time: 67 us; the launch traced here: 66 us
  starting transfers between devices  25.9 us (39%)
  Pallas kernels  20 us (30%)
  waiting for transfers between devices  19.2 us (29%)
  between operations  0.74 us (1%)
    ppermute x8, starting transfers between devices, across(): return lax.ppermute(x, 'seg', [(z, z ^ r) for z in range(planes)])  17.3 us
    ppermute x8, waiting for transfers between devices, across(): return lax.ppermute(x, 'seg', [(z, z ^ r) for z in range(planes)])  14.1 us
    pallas_call x2, Pallas kernels, whiten(): pl.pallas_call(functools.partial(whiten_body, outer), in_specs=[pl.BlockS...  10.2 us
    pallas_call x1, Pallas kernels, correlate(): pl.pallas_call(correlate_body, in_specs=[SMEM] * 2 + [VMEM] * 5, out_spec...  5.67 us
    ppermute x1, waiting for transfers between devices, shards(): before = lax.ppermute(own, 'blk', upward)  5.11 us
    ppermute x1, starting transfers between devices, shards(): got_ext = lax.ppermute(own_ext, 'blk', outer)  4.74 us
    ppermute x1, starting transfers between devices, shards(): shifted = lax.ppermute(send, ('seg', 'blk'), shift)  1.92 us
    ppermute x1, starting transfers between devices, shards(): before = lax.ppermute(own, 'blk', upward)  1.92 us
  transfers between devices with their start and end apart: 12, of which 9 were waited for; matrix products, arithmetic and copies ran while one was open for 0% of the time, Pallas kernels for 10%

profile of v8, /device:TPU:6, one launch (start us, length us, event | category | flops | bytes accessed | tf_op | source)
XLA Modules:
  0.0 66.0 jit_solution(6330790725142672282)
XLA Ops:
  0.6 5.1 %whiten.3.own_ext = bf16[4,3,128,512]{3,2,1,0:T(8,128)(2,1)S(1)} custom-call(f32[3,1024,512]{2,1,0:T(8,128)} %records.3), custom_call_target="tpu_custom_call" | custom-call | flops 1 | bytes 1 | tf_op jit(solution)/shard_map/whiten/pallas_call | solution.py:167
  5.7 0.0 copy-start.1
  5.7 0.0 copy-start
  5.8 4.7 %collective-permute-start.3 = (bf16[4,3,128,512]{3,2,1,0:T(8,128)(2,1)S(1)}, bf16[4,3,128,512]{3,2,1,0:T(8,128)(2,1)S(1)}, u32[]{:S(2)}, u32[]{:S(2)}) collective-permute-start(bf16[4,3,128,512]{3,2,1,0:T(8,128)(2,1)S(1)} %whiten.3.own_ext), channel_id=1, source_target_pairs={{1,2},{2,1},{3,4},{4,3},{5,6},{6,5},{7,8},{8,7},{9,10},{10,9},{11,... | collective-permute-start | bytes 4718600 | tf_op jit(solution)/shard_map/ppermute | solution.py:514
  10.5 5.1 %whiten.2.own_int = bf16[4,3,128,512]{3,2,1,0:T(8,128)(2,1)S(1)} custom-call(f32[3,1024,512]{2,1,0:T(8,128)} %records.3), custom_call_target="tpu_custom_call" | custom-call | flops 1 | bytes 1 | tf_op jit(solution)/shard_map/whiten/pallas_call | solution.py:167
  15.6 0.1 collective-permute-start.4
  15.7 0.0 copy-done.1
  15.7 2.0 %collective-permute-start = (s32[2,8]{1,0:T(2,128)S(1)}, s32[2,8]{1,0:T(2,128)S(1)}, u32[]{:S(2)}, u32[]{:S(2)}) collective-permute-start(s32[2,8]{1,0:T(2,128)S(1)} %copy-done.1), channel_id=1, source_target_pairs={{0,32},{32,0},{64,96},{96,64},{1,33},{33,1},{65,97},{97,65},{2,34}... | collective-permute-start | bytes 200 | tf_op jit(solution)/shard_map/ppermute | solution.py:501
  17.7 1.7 %collective-permute-done = s32[2,8]{1,0:T(2,128)S(1)} collective-permute-done((s32[2,8]{1,0:T(2,128)S(1)}, s32[2,8]{1,0:T(2,128)S(1)}, u32[]{:S(2)}, u32[]{:S(2)}) %collective-permute-start) | collective-permute-done | bytes 96 | tf_op jit(solution)/shard_map/ppermute | solution.py:501
  19.4 4.1 %collective-permute-start.1 = (s32[4,8]{1,0:T(4,128)S(1)}, s32[4,8]{1,0:T(4,128)S(1)}, u32[]{:S(2)}, u32[]{:S(2)}) collective-permute-start(s32[4,8]{1,0:T(4,128)S(1)} %pad_add_fusion.1), channel_id=1, source_target_pairs={{0,96},{32,64},{64,32},{96,0},{1,97},{33,65},{65,33},{97,1},{2,98}... | collective-permute-start | bytes 392 | tf_op jit(solution)/shard_map/ppermute | solution.py:501
  23.5 1.6 %collective-permute-done.1 = s32[4,8]{1,0:T(4,128)S(1)} collective-permute-done((s32[4,8]{1,0:T(4,128)S(1)}, s32[4,8]{1,0:T(4,128)S(1)}, u32[]{:S(2)}, u32[]{:S(2)}) %collective-permute-start.1) | collective-permute-done | bytes 160 | tf_op jit(solution)/shard_map/ppermute | solution.py:501
  25.1 1.9 %collective-permute-start.2 = (s32[8,8]{1,0:T(8,128)S(1)}, s32[8,8]{1,0:T(8,128)S(1)}, u32[]{:S(2)}, u32[]{:S(2)}) collective-permute-start(s32[8,8]{1,0:T(8,128)S(1)} %pad_add_fusion.own), channel_id=1, source_target_pairs={{0,1},{1,2},{2,3},{3,4},{4,5},{5,6},{6,7},{7,8},{8,9},{9,10},{10,1... | collective-permute-start | bytes 776 | tf_op jit(solution)/shard_map/ppermute | solution.py:520
  27.0 5.1 %collective-permute-done.2.before = s32[8,8]{1,0:T(8,128)S(1)} collective-permute-done((s32[8,8]{1,0:T(8,128)S(1)}, s32[8,8]{1,0:T(8,128)S(1)}, u32[]{:S(2)}, u32[]{:S(2)}) %collective-permute-start.2) | collective-permute-done | bytes 288 | tf_op jit(solution)/shard_map/ppermute | solution.py:520
  32.1 0.0 collective-permute-done.3.got_ext
  32.1 0.0 collective-permute-done.4.got_int
  32.1 0.0 copy-done
  32.1 5.7 %correlate.1 = (f32[848,128]{1,0:T(8,128)S(1)}, bf16[848,128]{1,0:T(8,128)(2,1)S(1)}, bf16[848,128]{1,0:T(8,128)(2,1)S(1)}, bf16[848,128]{1,0:T(8,128)(2,1)S(1)}, s32[128]{0:T(128)S(1)}) custom-call(s32[8,8]{1,0:T(8,128)S(1)} %pad_add_fusion.own, s32[8,8]{1,0:T(8,128)S(1)} %collective-permute-done.2.before, bf16[4,3,128,512]{3,2,1,0:T(8,128)(2,1)S(1)} %whiten.3.own_ext, ...), custom_call_target="tpu_custom_call" | custom-call | flops 1 | bytes 1 | tf_op jit(solution)/shard_map/correlate/pallas_call | solution.py:383
  37.8 1.9 %collective-permute-start.5 = (bf16[848,128]{1,0:T(8,128)(2,1)S(1)}, bf16[848,128]{1,0:T(8,128)(2,1)S(1)}, u32[]{:S(2)}, u32[]{:S(2)}) collective-permute-start(bf16[848,128]{1,0:T(8,128)(2,1)S(1)} %get-tuple-element.18), channel_id=1, source_target_pairs={{0,64},{32,96},{64,0},{96,32},{1,65},{33,97},{65,1},{97,33},{2,66}... | collective-permute-start | bytes 651272 | tf_op jit(solution)/shard_map/ppermute | solution.py:501
  39.7 2.2 %collective-permute-start.6 = (bf16[848,128]{1,0:T(8,128)(2,1)S(1)}, bf16[848,128]{1,0:T(8,128)(2,1)S(1)}, u32[]{:S(2)}, u32[]{:S(2)}) collective-permute-start(bf16[848,128]{1,0:T(8,128)(2,1)S(1)} %get-tuple-element.19), channel_id=1, source_target_pairs={{0,32},{32,0},{64,96},{96,64},{1,33},{33,1},{65,97},{97,65},{2,34}... | collective-permute-start | bytes 651272 | tf_op jit(solution)/shard_map/ppermute | solution.py:501
  41.9 0.0 collective-permute-start.7
  42.0 1.7 %plan.1 = s32[128]{0:T(128)S(1)} custom-call(s32[8,8]{1,0:T(8,128)S(1)} %pad_add_fusion.own, s32[8,8]{1,0:T(8,128)S(1)} %collective-permute-done.2.before, s32[128]{0:T(128)S(1)} %get-tuple-element.16.slots), custom_call_target="tpu_custom_call" | custom-call | flops 1 | bytes 1 | tf_op jit(solution)/shard_map/plan/pallas_call | solution.py:282
  43.6 1.7 %collective-permute-done.5.got2 = bf16[848,128]{1,0:T(8,128)(2,1)S(1)} collective-permute-done((bf16[848,128]{1,0:T(8,128)(2,1)S(1)}, bf16[848,128]{1,0:T(8,128)(2,1)S(1)}, u32[]{:S(2)}, u32[]{:S(2)}) %collective-permute-start.5) | collective-permute-done | bytes 217120 | tf_op jit(solution)/shard_map/ppermute | solution.py:501
  45.4 2.8 %collective-permute-done.6.got1 = bf16[848,128]{1,0:T(8,128)(2,1)S(1)} collective-permute-done((bf16[848,128]{1,0:T(8,128)(2,1)S(1)}, bf16[848,128]{1,0:T(8,128)(2,1)S(1)}, u32[]{:S(2)}, u32[]{:S(2)}) %collective-permute-start.6) | collective-permute-done | bytes 217120 | tf_op jit(solution)/shard_map/ppermute | solution.py:501
  48.2 0.9 %collective-permute-done.7.got3 = bf16[848,128]{1,0:T(8,128)(2,1)S(1)} collective-permute-done((bf16[848,128]{1,0:T(8,128)(2,1)S(1)}, bf16[848,128]{1,0:T(8,128)(2,1)S(1)}, u32[]{:S(2)}, u32[]{:S(2)}) %collective-permute-start.7) | collective-permute-done | bytes 217120 | tf_op jit(solution)/shard_map/ppermute | solution.py:501
  49.0 0.7 %combine.1 = (f32[848,128]{1,0:T(8,128)S(1)}, bf16[528,128]{1,0:T(8,128)(2,1)S(1)}, bf16[272,128]{1,0:T(8,128)(2,1)S(1)}, bf16[272,128]{1,0:T(8,128)(2,1)S(1)}, bf16[272,128]{1,0:T(8,128)(2,1)S(1)}) custom-call(s32[128]{0:T(128)S(1)} %plan.1, f32[848,128]{1,0:T(8,128)S(1)} %get-tuple-element.17.keep, bf16[848,128]{1,0:T(8,128)(2,1)S(1)} %collective-permute-done.5.got2, ...), custom_call_target="tpu_custom_call" | custom-call | flops 1 | bytes 1 | tf_op jit(solution)/shard_map/combine/pallas_call | solution.py:438
  49.8 1.9 %collective-permute-start.11 = (bf16[528,128]{1,0:T(8,128)(2,1)S(1)}, bf16[528,128]{1,0:T(8,128)(2,1)S(1)}, u32[]{:S(2)}, u32[]{:S(2)}) collective-permute-start(bf16[528,128]{1,0:T(8,128)(2,1)S(1)} %get-tuple-element.25), channel_id=1, source_target_pairs={{0,1},{1,2},{2,3},{3,4},{4,5},{5,6},{6,7},{7,8},{8,9},{9,10},{10,1... | collective-permute-start | bytes 405512 | tf_op jit(solution)/shard_map/ppermute | solution.py:525
  51.7 5.9 %collective-permute-start.8 = (bf16[272,128]{1,0:T(8,128)(2,1)S(1)}, bf16[272,128]{1,0:T(8,128)(2,1)S(1)}, u32[]{:S(2)}, u32[]{:S(2)}) collective-permute-start(bf16[272,128]{1,0:T(8,128)(2,1)S(1)} %get-tuple-element.22), channel_id=1, source_target_pairs={{0,64},{32,96},{64,0},{96,32},{1,65},{33,97},{65,1},{97,33},{2,66}... | collective-permute-start | bytes 208904 | tf_op jit(solution)/shard_map/ppermute | solution.py:501
  57.6 1.1 %collective-permute-start.9 = (bf16[272,128]{1,0:T(8,128)(2,1)S(1)}, bf16[272,128]{1,0:T(8,128)(2,1)S(1)}, u32[]{:S(2)}, u32[]{:S(2)}) collective-permute-start(bf16[272,128]{1,0:T(8,128)(2,1)S(1)} %get-tuple-element.23), channel_id=1, source_target_pairs={{0,32},{32,0},{64,96},{96,64},{1,33},{33,1},{65,97},{97,65},{2,34}... | collective-permute-start | bytes 208904 | tf_op jit(solution)/shard_map/ppermute | solution.py:501
  58.7 0.0 collective-permute-start.10
  58.7 1.2 %collective-permute-done.8.got2 = bf16[272,128]{1,0:T(8,128)(2,1)S(1)} collective-permute-done((bf16[272,128]{1,0:T(8,128)(2,1)S(1)}, bf16[272,128]{1,0:T(8,128)(2,1)S(1)}, u32[]{:S(2)}, u32[]{:S(2)}) %collective-permute-start.8) | collective-permute-done | bytes 69664 | tf_op jit(solution)/shard_map/ppermute | solution.py:501
  59.9 2.0 %collective-permute-done.9.got1 = bf16[272,128]{1,0:T(8,128)(2,1)S(1)} collective-permute-done((bf16[272,128]{1,0:T(8,128)(2,1)S(1)}, bf16[272,128]{1,0:T(8,128)(2,1)S(1)}, u32[]{:S(2)}, u32[]{:S(2)}) %collective-permute-start.9) | collective-permute-done | bytes 69664 | tf_op jit(solution)/shard_map/ppermute | solution.py:501
  61.9 2.3 %collective-permute-done.10.got3 = bf16[272,128]{1,0:T(8,128)(2,1)S(1)} collective-permute-done((bf16[272,128]{1,0:T(8,128)(2,1)S(1)}, bf16[272,128]{1,0:T(8,128)(2,1)S(1)}, u32[]{:S(2)}, u32[]{:S(2)}) %collective-permute-start.10) | collective-permute-done | bytes 69664 | tf_op jit(solution)/shard_map/ppermute | solution.py:501
  64.2 0.0 collective-permute-done.11.shifted
  64.2 1.8 %finish.1 = (f32[2,65,8,128]{3,2,1,0:T(8,128)}, f32[2,65,8,128]{3,2,1,0:T(8,128)}) custom-call(s32[128]{0:T(128)S(1)} %plan.1, f32[848,128]{1,0:T(8,128)S(1)} %get-tuple-element.21.full, bf16[272,128]{1,0:T(8,128)(2,1)S(1)} %collective-permute-done.8.got2, bf16[272,128]{1,0:T(8,128)(2,1)S(1)} %collective-permute-done.9.got1, ...), custom_call_target="tpu_custom_call" | custom-call | flops 1 | bytes 1 | tf_op jit(solution)/shard_map/finish/pallas_call | solution.py:487
  (2 shorter events, 0.0 us)
Async XLA Ops:
  5.7 10.0 %copy-start.1 = (s32[2,8]{1,0:T(2,128)S(1)}, s32[2,8]{1,0:T(2,128)}, u32[]{:S(2)}) copy-start(s32[2,8]{1,0:T(2,128)} %param.4) | copy-start | bytes 196
  5.7 26.3 %copy-start = (bf16[512,256]{1,0:T(8,128)(2,1)S(1)}, bf16[512,256]{1,0:T(8,128)(2,1)}, u32[]{:S(2)}) copy-start(bf16[512,256]{1,0:T(8,128)(2,1)} %constant.2.clone.lag) | copy-start | bytes 786436
  5.8 26.3 %collective-permute-start.3 = (bf16[4,3,128,512]{3,2,1,0:T(8,128)(2,1)S(1)}, bf16[4,3,128,512]{3,2,1,0:T(8,128)(2,1)S(1)}, u32[]{:S(2)}, u32[]{:S(2)}) collective-permute-start(bf16[4,3,128,512]{3,2,1,0:T(8,128)(2,1)S(1)} %whiten.3.own_ext), channel_id=1, source_target_pairs={{1,2},{2,1},{3,4},{4,3},{5,6},{6,5},{7,8},{8,7},{9,10},{10,9},{11,... | collective-permute-start | bytes 4718600 | tf_op jit(solution)/shard_map/ppermute | solution.py:514
  15.6 16.5 %collective-permute-start.4 = (bf16[4,3,128,512]{3,2,1,0:T(8,128)(2,1)S(1)}, bf16[4,3,128,512]{3,2,1,0:T(8,128)(2,1)S(1)}, u32[]{:S(2)}, u32[]{:S(2)}) collective-permute-start(bf16[4,3,128,512]{3,2,1,0:T(8,128)(2,1)S(1)} %whiten.2.own_int), channel_id=1, source_target_pairs={{0,1},{1,0},{2,3},{3,2},{4,5},{5,4},{6,7},{7,6},{8,9},{9,8},{10,11... | collective-permute-start | bytes 4718600 | tf_op jit(solution)/shard_map/ppermute | solution.py:516
  15.7 3.6 %collective-permute-start = (s32[2,8]{1,0:T(2,128)S(1)}, s32[2,8]{1,0:T(2,128)S(1)}, u32[]{:S(2)}, u32[]{:S(2)}) collective-permute-start(s32[2,8]{1,0:T(2,128)S(1)} %copy-done.1), channel_id=1, source_target_pairs={{0,32},{32,0},{64,96},{96,64},{1,33},{33,1},{65,97},{97,65},{2,34}... | collective-permute-start | bytes 200 | tf_op jit(solution)/shard_map/ppermute | solution.py:501
  19.4 5.7 %collective-permute-start.1 = (s32[4,8]{1,0:T(4,128)S(1)}, s32[4,8]{1,0:T(4,128)S(1)}, u32[]{:S(2)}, u32[]{:S(2)}) collective-permute-start(s32[4,8]{1,0:T(4,128)S(1)} %pad_add_fusion.1), channel_id=1, source_target_pairs={{0,96},{32,64},{64,32},{96,0},{1,97},{33,65},{65,33},{97,1},{2,98}... | collective-permute-start | bytes 392 | tf_op jit(solution)/shard_map/ppermute | solution.py:501
  25.1 7.0 %collective-permute-start.2 = (s32[8,8]{1,0:T(8,128)S(1)}, s32[8,8]{1,0:T(8,128)S(1)}, u32[]{:S(2)}, u32[]{:S(2)}) collective-permute-start(s32[8,8]{1,0:T(8,128)S(1)} %pad_add_fusion.own), channel_id=1, source_target_pairs={{0,1},{1,2},{2,3},{3,4},{4,5},{5,6},{6,7},{7,8},{8,9},{9,10},{10,1... | collective-permute-start | bytes 776 | tf_op jit(solution)/shard_map/ppermute | solution.py:520
  37.8 7.6 %collective-permute-start.5 = (bf16[848,128]{1,0:T(8,128)(2,1)S(1)}, bf16[848,128]{1,0:T(8,128)(2,1)S(1)}, u32[]{:S(2)}, u32[]{:S(2)}) collective-permute-start(bf16[848,128]{1,0:T(8,128)(2,1)S(1)} %get-tuple-element.18), channel_id=1, source_target_pairs={{0,64},{32,96},{64,0},{96,32},{1,65},{33,97},{65,1},{97,33},{2,66}... | collective-permute-start | bytes 651272 | tf_op jit(solution)/shard_map/ppermute | solution.py:501
  39.7 8.4 %collective-permute-start.6 = (bf16[848,128]{1,0:T(8,128)(2,1)S(1)}, bf16[848,128]{1,0:T(8,128)(2,1)S(1)}, u32[]{:S(2)}, u32[]{:S(2)}) collective-permute-start(bf16[848,128]{1,0:T(8,128)(2,1)S(1)} %get-tuple-element.19), channel_id=1, source_target_pairs={{0,32},{32,0},{64,96},{96,64},{1,33},{33,1},{65,97},{97,65},{2,34}... | collective-permute-start | bytes 651272 | tf_op jit(solution)/shard_map/ppermute | solution.py:501
  41.9 7.1 %collective-permute-start.7 = (bf16[848,128]{1,0:T(8,128)(2,1)S(1)}, bf16[848,128]{1,0:T(8,128)(2,1)S(1)}, u32[]{:S(2)}, u32[]{:S(2)}) collective-permute-start(bf16[848,128]{1,0:T(8,128)(2,1)S(1)} %get-tuple-element.20), channel_id=1, source_target_pairs={{0,96},{32,64},{64,32},{96,0},{1,97},{33,65},{65,33},{97,1},{2,98}... | collective-permute-start | bytes 651272 | tf_op jit(solution)/shard_map/ppermute | solution.py:501
  49.8 14.4 %collective-permute-start.11 = (bf16[528,128]{1,0:T(8,128)(2,1)S(1)}, bf16[528,128]{1,0:T(8,128)(2,1)S(1)}, u32[]{:S(2)}, u32[]{:S(2)}) collective-permute-start(bf16[528,128]{1,0:T(8,128)(2,1)S(1)} %get-tuple-element.25), channel_id=1, source_target_pairs={{0,1},{1,2},{2,3},{3,4},{4,5},{5,6},{6,7},{7,8},{8,9},{9,10},{10,1... | collective-permute-start | bytes 405512 | tf_op jit(solution)/shard_map/ppermute | solution.py:525
  51.7 8.2 %collective-permute-start.8 = (bf16[272,128]{1,0:T(8,128)(2,1)S(1)}, bf16[272,128]{1,0:T(8,128)(2,1)S(1)}, u32[]{:S(2)}, u32[]{:S(2)}) collective-permute-start(bf16[272,128]{1,0:T(8,128)(2,1)S(1)} %get-tuple-element.22), channel_id=1, source_target_pairs={{0,64},{32,96},{64,0},{96,32},{1,65},{33,97},{65,1},{97,33},{2,66}... | collective-permute-start | bytes 208904 | tf_op jit(solution)/shard_map/ppermute | solution.py:501
  57.6 4.3 %collective-permute-start.9 = (bf16[272,128]{1,0:T(8,128)(2,1)S(1)}, bf16[272,128]{1,0:T(8,128)(2,1)S(1)}, u32[]{:S(2)}, u32[]{:S(2)}) collective-permute-start(bf16[272,128]{1,0:T(8,128)(2,1)S(1)} %get-tuple-element.23), channel_id=1, source_target_pairs={{0,32},{32,0},{64,96},{96,64},{1,33},{33,1},{65,97},{97,65},{2,34}... | collective-permute-start | bytes 208904 | tf_op jit(solution)/shard_map/ppermute | solution.py:501
  58.7 5.5 %collective-permute-start.10 = (bf16[272,128]{1,0:T(8,128)(2,1)S(1)}, bf16[272,128]{1,0:T(8,128)(2,1)S(1)}, u32[]{:S(2)}, u32[]{:S(2)}) collective-permute-start(bf16[272,128]{1,0:T(8,128)(2,1)S(1)} %get-tuple-element.24), channel_id=1, source_target_pairs={{0,96},{32,64},{64,32},{96,0},{1,97},{33,65},{65,33},{97,1},{2,98}... | collective-permute-start | bytes 208904 | tf_op jit(solution)/shard_map/ppermute | solution.py:501
